TPU v7x, 256 devices: a whole 4x4x8 slice. The times are simulated.
256 devices in a mesh: cp: 8 (over z), tp: 8 (over x_lo, y), ep: 4 (over x_hi, core).
Axes of the slice: x: 4 (x_hi: 2, x_lo: 2; x = x_hi * 2 + x_lo), y: 4, z: 8, core: 2. Of those that a mesh axis runs over, the one named last changes fastest.
Arguments:
- layer_input: bfloat16 [8192, 4096], P('cp', ('tp', 'ep')), may hold values from -6 to 6
- output_cot: bfloat16 [8192, 4096], P(('cp', 'tp'), 'ep'), may hold values from -6 to 6
- routes: int32 [8192, 2], P(('cp', 'tp')), may hold values from 0 to 63, all different within a row; in each aligned block of 128 rows (0 to 127, 128 to 255, ...) at most 5 rows name the same one
- gate_values: float32 [8192, 2], P(('cp', 'tp')), may hold values from 0.05 to 1
- gate_weight: bfloat16 [64, 4096, 1536], P(('cp', 'tp'), None, 'ep'), may hold values from -0.09375 to 0.09375
- up_weight: bfloat16 [64, 4096, 1536], P(('cp', 'tp'), None, 'ep'), may hold values from -0.09375 to 0.09375
- down_weight: bfloat16 [64, 1536, 4096], P(('cp', 'tp'), 'ep'), may hold values from -0.15625 to 0.15625
Outputs:
- moe_output: bfloat16 [8192, 4096], P(('cp', 'tp'), 'ep')
- input_grad: bfloat16 [8192, 4096], P(('cp', 'tp'), 'ep')
- gate_grad: float32 [8192, 2], P(('cp', 'tp'))
Inputs may be any that keep to these rules, and one draw needn't show every extreme that they name: `routes`: each row names 2 different experts. Within the 128 rows of one device no expert is named by more than 5 rows, a bound that some block reaches.
All inputs are finite; a program needn't handle non-finite values.
Results may differ from a plain program's by a relative error of at most 0.015.
Values may be sent and summed in bfloat16 or wider, within the bound.
No kernel may reach another device: no remote copies, remote signals or barrier semaphores. Data moves between devices by JAX's collectives and lax.ppermute only.
A program may use at most 128 MiB of HBM per device.

v0:
```python
import jax
import jax.numpy as jnp
from jax import lax
from jax.sharding import PartitionSpec as P


def transposed(left, right):
    return lax.dot_general(
        left, right, (((1,), (1,)), ((), ())), preferred_element_type=jnp.float32
    )


def local(layer_input, output_cot, routes, gate_values, gate_weight, up_weight, down_weight):
    row_count, pick_count = routes.shape
    expert_count = lax.axis_size(("cp", "tp"))
    capacity = max(2, row_count * pick_count * 5 // (4 * expert_count))
    entries = row_count * pick_count
    slot_total = expert_count * capacity
    flat_routes = routes.reshape(-1)
    onehot = (flat_routes[:, None] == jnp.arange(expert_count, dtype=jnp.int32)[None, :]).astype(
        jnp.int32
    )
    before = jnp.cumsum(onehot, axis=0) - onehot
    position = flat_routes * capacity + jnp.sum(before * onehot, axis=1)
    owner_entry = (
        jnp.full((slot_total,), entries, jnp.int32)
        .at[position]
        .set(jnp.arange(entries, dtype=jnp.int32))
    )
    filled = (owner_entry < entries)[:, None]
    source = jnp.minimum(owner_entry, entries - 1)
    gate_w = gate_weight[0]
    up_w = up_weight[0]
    down_w = down_weight[0]
    feature = lax.all_gather(layer_input, "ep", axis=1, tiled=True)
    token_feats = lax.all_to_all(feature, "tp", split_axis=0, concat_axis=1, tiled=True)
    outgoing = jnp.where(filled, token_feats[source // pick_count], 0)
    arrived = lax.all_to_all(
        outgoing.reshape(expert_count, capacity, -1),
        ("cp", "tp"),
        split_axis=0,
        concat_axis=0,
        tiled=True,
    ).reshape(slot_total, -1)
    pre_gate = jnp.dot(arrived, gate_w, preferred_element_type=jnp.float32)
    pre_up = jnp.dot(arrived, up_w, preferred_element_type=jnp.float32)
    sigmoid_gate = jax.nn.sigmoid(pre_gate)
    silu_gate = pre_gate * sigmoid_gate
    act = (silu_gate * pre_up).astype(jnp.bfloat16)
    partial_value = jnp.dot(act, down_w, preferred_element_type=jnp.float32).astype(jnp.bfloat16)
    gate_column = gate_values[:, :, None]
    summed = lax.psum_scatter(
        partial_value.astype(jnp.float32).astype(jnp.bfloat16),
        "ep",
        scatter_dimension=1,
        tiled=True,
    ).astype(jnp.float32)
    returned = (
        lax.all_to_all(
            summed.reshape(expert_count, capacity, -1).astype(jnp.bfloat16),
            ("cp", "tp"),
            split_axis=0,
            concat_axis=0,
            tiled=True,
        )
        .astype(jnp.float32)
        .reshape(slot_total, -1)
    )
    picked = returned[position].reshape(row_count, pick_count, -1)
    cot_quarter = output_cot.astype(jnp.float32)
    moe_output = jnp.sum(gate_column * picked, axis=1).astype(jnp.bfloat16)
    gate_grad = lax.psum(jnp.sum(cot_quarter[:, None, :] * picked, axis=-1), "ep")
    scaled = (gate_column * cot_quarter[:, None, :]).astype(jnp.bfloat16).reshape(entries, -1)
    slot_rows = jnp.where(filled, scaled[source], 0)
    cot_slots = lax.all_to_all(
        slot_rows.reshape(expert_count, capacity, -1),
        ("cp", "tp"),
        split_axis=0,
        concat_axis=0,
        tiled=True,
    ).reshape(slot_total, -1)
    d_act = transposed(lax.all_gather(cot_slots, "ep", axis=1, tiled=True), down_w)
    d_gate = (d_act * pre_up * sigmoid_gate * (1.0 + pre_gate * (1.0 - sigmoid_gate))).astype(
        jnp.bfloat16
    )
    d_up = (d_act * silu_gate).astype(jnp.bfloat16)
    grad_part = (transposed(d_gate, gate_w) + transposed(d_up, up_w)).astype(jnp.bfloat16)
    grad_total = lax.psum_scatter(
        grad_part.astype(jnp.float32).astype(jnp.bfloat16), "ep", scatter_dimension=1, tiled=True
    ).astype(jnp.float32)
    grad_back = (
        lax.all_to_all(
            grad_total.reshape(expert_count, capacity, -1).astype(jnp.bfloat16),
            ("cp", "tp"),
            split_axis=0,
            concat_axis=0,
            tiled=True,
        )
        .astype(jnp.float32)
        .reshape(slot_total, -1)
    )
    input_grad = jnp.sum(grad_back[position].reshape(row_count, pick_count, -1), axis=1).astype(
        jnp.bfloat16
    )
    return (moe_output, input_grad, gate_grad)


def solution(mesh):
    placed = (
        P("cp", ("tp", "ep")),
        P(("cp", "tp"), "ep"),
        P(("cp", "tp"), None),
        P(("cp", "tp"), None),
        P(("cp", "tp"), None, "ep"),
        P(("cp", "tp"), None, "ep"),
        P(("cp", "tp"), "ep", None),
    )
    return jax.shard_map(
        local,
        mesh=mesh,
        in_specs=placed,
        out_specs=(P(("cp", "tp"), "ep"), P(("cp", "tp"), "ep"), P(("cp", "tp"), None)),
        check_vma=False,
    )
```

profile of v0, /device:TPU:4, one launch (start us, length us, event | category | flops | bytes accessed | tf_op | source)
XLA Modules:
  0.0 383.8 jit_solution(16070313147977601322)
XLA Ops:
  7.2 0.0 all-gather.3.cloned.1.call-start
  7.2 0.7 all-gather.3.cloned.1.call-update
  7.9 0.9 copy.21
  8.8 0.1 eq.25
  9.0 0.1 eq.29
  9.1 0.7 broadcast_multiply_fusion
  9.8 0.1 copy.20
  9.9 0.1 mul.79
  10.1 0.6 reduce-window.6
  10.7 0.2 slice_reduce_fusion
  10.9 0.1 fusion.17
  11.0 1.4 scatter_custom_fusion
  12.4 21.1 %all-gather.3.cloned.1.call-done = bf16[1024,512]{1,0:T(8,128)(2,1)} async-done(((bf16[1024,128]{1,0:T(8,128)(2,1)}), bf16[1024,512]{1,0:T(8,128)(2,1)}) %all-gather.3.cloned.1.call-update) | async-done | bytes 1048592 | tf_op jit(solution)/shard_map/all_gather | solution.py:35
  33.6 6.0 %all-to-all-start = ((bf16[8,128,512]{2,1,0:T(8,128)(2,1)}), bf16[8,128,512]{2,1,0:T(8,128)(2,1)}, u32[]{:S(2)}, u32[]{:S(2)}) async-start(bf16[8,128,512]{2,1,0:T(8,128)(2,1)} %bitcast.44), calls=%async_computation | async-start | bytes 2097152 | tf_op jit(solution)/shard_map/all_to_all | solution.py:36
  39.6 0.1 broadcast_in_dim.40
  39.7 0.8 copy.19
  40.5 1.3 mul.86
  41.8 2.9 mul.87
  44.7 0.1 mul.84
  44.9 2.1 multiply_convert_fusion
  47.1 4.4 %gather_fusion.2 = bf16[320,1024]{1,0:T(8,128)(2,1)} fusion(bf16[256,1024]{1,0:T(8,128)(2,1)} %multiply_convert_fusion, s32[1024]{0:T(1024)S(1)} %get-tuple-element.10), kind=kCustom, calls=%fused_computation.2 | custom fusion | bytes 1312000 | tf_op jit(solution)/shard_map/gather | solution.py:74
  51.5 2.1 gather.20
  53.6 2.3 broadcast_select_fusion.1
  56.0 12.2 %all-to-all-start.3 = ((bf16[64,5,1024]{2,1,0:T(8,128)(2,1)}), bf16[64,5,1024]{2,1,0:T(8,128)(2,1)}, u32[]{:S(2)}, u32[]{:S(2)}) async-start(bf16[64,5,1024]{2,1,0:T(8,128)(2,1)} %broadcast_select_fusion.1), calls=%async_computation.4 | async-start | bytes 2097152 | tf_op jit(solution)/shard_map/all_to_all | solution.py:75
  68.1 2.3 copy.28
  70.4 9.4 %gather_fusion = bf16[320,4096]{1,0:T(8,128)(2,1)} fusion(bf16[128,4096]{1,0:T(8,128)(2,1)} %bitcast.43, s32[1024]{0:T(1024)S(1)} %get-tuple-element.11), kind=kCustom, calls=%fused_computation | custom fusion | bytes 5244160 | tf_op jit(solution)/shard_map/gather | solution.py:37
  79.9 4.7 %gather.17 = bf16[64,5,4096]{2,1,0:T(8,128)(2,1)} reshape(bf16[320,4096]{1,0:T(8,128)(2,1)} %gather_fusion) | data formatting | bytes 5242880 | tf_op jit(solution)/shard_map/gather | solution.py:37
  84.6 4.6 %broadcast_select_fusion = bf16[64,5,4096]{2,1,0:T(8,128)(2,1)} fusion(bf16[64,5,4096]{2,1,0:T(8,128)(2,1)} %gather.17, pred[64,5]{1,0:T(8,128)(4,1)S(1)} %broadcast_in_dim.40), kind=kLoop, calls=%fused_computation.8 | loop fusion | flops 1310720 | bytes 5243200 | tf_op jit(solution)/shard_map/jit(_where)/select_n | solution.py:37
  89.2 6.8 %all-to-all-done.3 = bf16[64,5,1024]{2,1,0:T(8,128)(2,1)} async-done(((bf16[64,5,1024]{2,1,0:T(8,128)(2,1)}), bf16[64,5,1024]{2,1,0:T(8,128)(2,1)}, u32[]{:S(2)}, u32[]{:S(2)}) %all-to-all-start.3) | async-done | bytes 655392 | tf_op jit(solution)/shard_map/all_to_all | solution.py:75
  96.0 6.8 %all-to-all-start.1 = ((bf16[64,5,4096]{2,1,0:T(8,128)(2,1)}), bf16[64,5,4096]{2,1,0:T(8,128)(2,1)}, u32[]{:S(2)}, u32[]{:S(2)}) async-start(bf16[64,5,4096]{2,1,0:T(8,128)(2,1)} %broadcast_select_fusion), calls=%async_computation.1 | async-start | bytes 8388608 | tf_op jit(solution)/shard_map/all_to_all | solution.py:38
  102.9 0.2 all-gather.5.cloned.1.call-start
  103.1 2.1 reshape.117
  105.2 0.0 reduce-scatter.3.cloned.1.call-start
  105.3 91.7 %all-to-all-done.1 = bf16[64,5,4096]{2,1,0:T(8,128)(2,1)} async-done(((bf16[64,5,4096]{2,1,0:T(8,128)(2,1)}), bf16[64,5,4096]{2,1,0:T(8,128)(2,1)}, u32[]{:S(2)}, u32[]{:S(2)}) %all-to-all-start.1) | async-done | bytes 2621472 | tf_op jit(solution)/shard_map/all_to_all | solution.py:38
  196.9 4.8 %reshape.113 = bf16[320,4096]{1,0:T(8,128)(2,1)} reshape(bf16[64,5,4096]{2,1,0:T(8,128)(2,1)} %all-to-all-done.1) | data formatting | bytes 5242880 | tf_op jit(solution)/shard_map/reshape | solution.py:44
  201.7 4.3 %fusion.5 = f32[320,384]{1,0:T(8,128)S(1)} fusion(bf16[320,4096]{1,0:T(8,128)(2,1)} %reshape.113, bf16[1,4096,384]{2,1,0:T(8,128)(2,1)} %param.12), kind=kOutput, calls=%fused_computation.13 | convolution fusion | flops 1006632960 | bytes 6258688 | tf_op jit(solution)/shard_map/dot_general | solution.py:46
  206.1 0.0 copy-done.6
  206.1 1.5 fusion.9
  207.6 0.8 copy-done.1
  208.4 3.1 convolution_convert_fusion
  211.5 0.0 reduce-scatter.5.cloned.1.call-start
  211.6 0.0 all-gather.5.cloned.1.call-done
  211.6 3.4 fusion.1
  215.1 1.6 fusion.7
  216.7 0.2 copy-done.5
  217.0 3.1 fusion
  220.1 33.2 %reduce-scatter.3.cloned.1.call-done = bf16[320,1024]{1,0:T(8,128)(2,1)} async-done(((bf16[320,4096]{1,0:T(8,128)(2,1)}), bf16[320,1024]{1,0:T(8,128)(2,1)}) %reduce-scatter.3.cloned.1.call-update) | async-done | bytes 655376 | tf_op jit(solution)/shard_map/reduce_scatter | solution.py:52
  253.3 2.1 convert_element_type.59
  255.5 12.5 %all-to-all-start.2 = ((bf16[64,5,1024]{2,1,0:T(8,128)(2,1)}), bf16[64,5,1024]{2,1,0:T(8,128)(2,1)}, u32[]{:S(2)}, u32[]{:S(2)}) async-start(bf16[64,5,1024]{2,1,0:T(8,128)(2,1)} %convert_element_type.59), calls=%async_computation.3 | async-start | bytes 2097152 | tf_op jit(solution)/shard_map/all_to_all | solution.py:59
  267.9 36.6 %reduce-scatter.5.cloned.1.call-done = bf16[320,1024]{1,0:T(8,128)(2,1)} async-done(((bf16[320,4096]{1,0:T(8,128)(2,1)}), bf16[320,1024]{1,0:T(8,128)(2,1)}) %reduce-scatter.5.cloned.1.call-update) | async-done | bytes 655376 | tf_op jit(solution)/shard_map/reduce_scatter | solution.py:88
  304.5 2.2 convert_element_type.66
  306.7 12.2 %all-to-all-start.4 = ((bf16[64,5,1024]{2,1,0:T(8,128)(2,1)}), bf16[64,5,1024]{2,1,0:T(8,128)(2,1)}, u32[]{:S(2)}, u32[]{:S(2)}) async-start(bf16[64,5,1024]{2,1,0:T(8,128)(2,1)} %convert_element_type.66), calls=%async_computation.6 | async-start | bytes 2097152 | tf_op jit(solution)/shard_map/all_to_all | solution.py:92
  318.9 0.8 convert_element_type.61
  319.8 2.3 reshape.122
  322.1 3.8 gather_fusion.1
  325.9 2.8 reshape.116
  328.7 18.2 %all-to-all-done.4 = bf16[64,5,1024]{2,1,0:T(8,128)(2,1)} async-done(((bf16[64,5,1024]{2,1,0:T(8,128)(2,1)}), bf16[64,5,1024]{2,1,0:T(8,128)(2,1)}, u32[]{:S(2)}, u32[]{:S(2)}) %all-to-all-start.4) | async-done | bytes 655392 | tf_op jit(solution)/shard_map/all_to_all | solution.py:92
  346.9 2.3 reshape.124
  349.2 3.8 gather_fusion.3
  353.1 2.8 reshape.120
  355.9 3.9 %multiply_reduce_fusion = (f32[128,2]{1,0:T(8,128)S(1)}, bf16[128,1024]{1,0:T(8,128)(2,1)}) fusion(f32[128,2,1024]{2,1,0:T(2,128)} %reshape.116, f32[128,1024]{1,0:T(8,128)} %convert_element_type.61, f32[128,2]{1,0:T(8,128)S(1)} %copy.19), kind=kLoop, calls=%fused_computation.19 | loop fusion | flops 917248 | bytes 1837056 | tf_op jit(solution)/shard_map/reduce_sum | solution.py:72
  359.8 13.7 %psum.7 = f32[128,2]{1,0:T(8,128)S(1)} all-reduce(f32[128,2]{1,0:T(8,128)S(1)} %get-tuple-element.6), channel_id=1, replica_groups=mesh['cp'=8,'tp'=8,'ep'=4] {'ep'}, use_global_device_ids=true, to_apply=%region_9.10 | all-reduce | flops 256 | bytes 2048 | tf_op jit(solution)/shard_map/psum | solution.py:72
  373.5 0.6 copy.26
  374.1 3.2 reduce_sum.41
  (31 shorter events, 0.2 us)
Async XLA Ops:
  7.2 201.3 %copy-start = (bf16[1,384,4096]{2,1,0:T(8,128)(2,1)S(1)}, bf16[1,384,4096]{2,1,0:T(8,128)(2,1)}, u32[]{:S(2)}) copy-start(bf16[1,384,4096]{2,1,0:T(8,128)(2,1)} %param.13) | copy-start | bytes 9437188
  7.2 33.4 %copy-start.7 = (bf16[128,1024]{1,0:T(8,128)(2,1)S(1)}, bf16[128,1024]{1,0:T(8,128)(2,1)}, u32[]{:S(2)}) copy-start(bf16[128,1024]{1,0:T(8,128)(2,1)} %param.8) | copy-start | bytes 786436
  7.2 26.4 %all-gather.3.cloned.1.call-start = ((), (), s32[]{:S(2)}) async-start(), calls=%async_computation.7 | async-start | bytes 1310720 | tf_op jit(solution)/shard_map/all_gather | solution.py:35
  33.6 22.4 %all-to-all-start = ((bf16[8,128,512]{2,1,0:T(8,128)(2,1)}), bf16[8,128,512]{2,1,0:T(8,128)(2,1)}, u32[]{:S(2)}, u32[]{:S(2)}) async-start(bf16[8,128,512]{2,1,0:T(8,128)(2,1)} %bitcast.44), calls=%async_computation | async-start | bytes 2097152 | tf_op jit(solution)/shard_map/all_to_all | solution.py:36
  56.0 40.0 %all-to-all-start.3 = ((bf16[64,5,1024]{2,1,0:T(8,128)(2,1)}), bf16[64,5,1024]{2,1,0:T(8,128)(2,1)}, u32[]{:S(2)}, u32[]{:S(2)}) async-start(bf16[64,5,1024]{2,1,0:T(8,128)(2,1)} %broadcast_select_fusion.1), calls=%async_computation.4 | async-start | bytes 2097152 | tf_op jit(solution)/shard_map/all_to_all | solution.py:75
  96.0 100.9 %all-to-all-start.1 = ((bf16[64,5,4096]{2,1,0:T(8,128)(2,1)}), bf16[64,5,4096]{2,1,0:T(8,128)(2,1)}, u32[]{:S(2)}, u32[]{:S(2)}) async-start(bf16[64,5,4096]{2,1,0:T(8,128)(2,1)} %broadcast_select_fusion), calls=%async_computation.1 | async-start | bytes 8388608 | tf_op jit(solution)/shard_map/all_to_all | solution.py:38
  102.9 108.7 %all-gather.5.cloned.1.call-start = ((), (), s32[]{:S(2)}) async-start(), calls=%async_computation.9 | async-start | bytes 3276800 | tf_op jit(solution)/shard_map/all_gather | solution.py:82
  105.2 148.1 %reduce-scatter.3.cloned.1.call-start = ((), (), s32[]{:S(2)}) async-start(), calls=%async_computation.8 | async-start | bytes 3276800 | tf_op jit(solution)/shard_map/reduce_scatter | solution.py:52
  201.7 4.3 %copy-start.3 = (bf16[1,4096,384]{2,1,0:T(8,128)(2,1)S(1)}, bf16[1,4096,384]{2,1,0:T(8,128)(2,1)}, u32[]{:S(2)}) copy-start(bf16[1,4096,384]{2,1,0:T(8,128)(2,1)} %param.11) | copy-start | bytes 9437188
  201.7 4.4 %copy-start.6 = (bf16[320,4096]{1,0:T(8,128)(2,1)S(1)}, bf16[320,4096]{1,0:T(8,128)(2,1)}, u32[]{:S(2)}) copy-start(bf16[320,4096]{1,0:T(8,128)(2,1)} %reshape.113) | copy-start | bytes 7864324
  206.1 1.5 copy-start.8
  207.6 0.8 copy-start.1
  211.5 93.0 %reduce-scatter.5.cloned.1.call-start = ((), (), s32[]{:S(2)}) async-start(), calls=%async_computation.10 | async-start | bytes 3276800 | tf_op jit(solution)/shard_map/reduce_scatter | solution.py:88
  211.6 3.5 copy-start.2
  211.6 3.5 copy-start.4
  211.6 3.5 copy-start.9
  215.1 1.9 copy-start.5
  255.5 51.2 %all-to-all-start.2 = ((bf16[64,5,1024]{2,1,0:T(8,128)(2,1)}), bf16[64,5,1024]{2,1,0:T(8,128)(2,1)}, u32[]{:S(2)}, u32[]{:S(2)}) async-start(bf16[64,5,1024]{2,1,0:T(8,128)(2,1)} %convert_element_type.59), calls=%async_computation.3 | async-start | bytes 2097152 | tf_op jit(solution)/shard_map/all_to_all | solution.py:59
  306.7 40.2 %all-to-all-start.4 = ((bf16[64,5,1024]{2,1,0:T(8,128)(2,1)}), bf16[64,5,1024]{2,1,0:T(8,128)(2,1)}, u32[]{:S(2)}, u32[]{:S(2)}) async-start(bf16[64,5,1024]{2,1,0:T(8,128)(2,1)} %convert_element_type.66), calls=%async_computation.6 | async-start | bytes 2097152 | tf_op jit(solution)/shard_map/all_to_all | solution.py:92
Sparse Core Ops, SparseCore 0:
  9.8 23.6 all-gather.2
  105.5 43.8 all-gather.4
  211.6 41.6 reduce-scatter.2
  256.2 48.2 reduce-scatter.4
where the time goes:
time: 386 us; the launch traced here: 384 us
  waiting for transfers between devices  208 us (54%)
  local copies, waits for them, and re-layouts  62.1 us (16%)
  starting transfers between devices  50 us (13%)
  other arithmetic  18.5 us (5%)
  matrix products  17.1 us (4%)
  between operations  14 us (4%)
  blocking collectives  13.7 us (4%)
    all_to_all x1, waiting for transfers between devices, local(): lax.all_to_all(outgoing.reshape(expert_count, capacity, -1), ('cp', 'tp')...  91.7 us
    reduce_scatter x1, waiting for transfers between devices, local(): lax.psum_scatter(grad_part.astype(jnp.float32).astype(jnp.bfloat16), 'ep'...  36.6 us
    reduce_scatter x1, waiting for transfers between devices, local(): lax.psum_scatter(partial_value.astype(jnp.float32).astype(jnp.bfloat16),...  33.2 us
    all_gather x1, waiting for transfers between devices, local(): feature = lax.all_gather(layer_input, 'ep', axis=1, tiled=True)  21.1 us
    all_to_all x1, waiting for transfers between devices, local(): lax.all_to_all(grad_total.reshape(expert_count, capacity, -1).astype(jnp....  18.2 us
    gather x2, local copies, waits for them, and re-layouts, local(): outgoing = jnp.where(filled, token_feats[source // pick_count], 0)  14.1 us
    psum x1, blocking collectives, local(): lax.psum(jnp.sum(cot_quarter[:, None, :] * picked, axis=-1), 'ep')  13.7 us
    all_to_all x1, starting transfers between devices, local(): lax.all_to_all(summed.reshape(expert_count, capacity, -1).astype(jnp.bflo...  12.5 us
  transfers between devices with their start and end apart: 9, of which 6 were waited for; matrix products, arithmetic and copies ran while one was open for 21% of the time, Pallas kernels for 0%

commit v1 on v0

v1 whole, which is shorter than its diff:
```python
import functools

import jax
import jax.numpy as jnp
from jax import lax
from jax.experimental import pallas as pl
from jax.experimental.pallas import tpu as pltpu
from jax.sharding import PartitionSpec as P

BF = jnp.bfloat16
F32 = jnp.float32
LANES = 128


def nt(left, right):
    return lax.dot_general(
        left, right, (((1,), (1,)), ((), ())), preferred_element_type=F32
    )


def tn(left, right):
    return lax.dot_general(
        left, right, (((0,), (0,)), ((), ())), preferred_element_type=F32
    )


def slot_masks(routes, experts, capacity):
    picks, tokens = routes.shape
    expert = lax.broadcasted_iota(jnp.int32, (experts, tokens), 0)
    earlier = (
        lax.broadcasted_iota(jnp.int32, (tokens, tokens), 0)
        < lax.broadcasted_iota(jnp.int32, (tokens, tokens), 1)
    ).astype(F32).astype(BF)
    slot = lax.broadcasted_iota(jnp.int32, (experts * capacity, tokens), 0)
    taken = jnp.zeros((experts, 1), F32)
    masks = []
    for k in range(picks):
        named = routes[k : k + 1, :]
        chosen = (expert == named).astype(F32)
        before = jnp.dot(chosen.astype(BF), earlier, preferred_element_type=F32) + taken
        rank = jnp.sum(before * chosen, axis=0, keepdims=True)
        place = named * capacity + rank.astype(jnp.int32)
        masks.append((slot == place).astype(F32))
        taken = taken + jnp.sum(chosen, axis=1, keepdims=True)
    return masks


def tile_rows(values, blocks, wide_ref, out_ref):
    rows = wide_ref.shape[0] // blocks
    for f in range(blocks):
        wide_ref[pl.ds(f, rows, stride=blocks), :] = values(f)
    out_ref[...] = wide_ref[...].astype(BF)


def untile_rows(in_ref, blocks, wide_ref, out_ref):
    rows = wide_ref.shape[0] // blocks
    wide_ref[...] = in_ref[...].astype(F32)
    for f in range(blocks):
        out_ref[:, f * LANES : (f + 1) * LANES] = wide_ref[
            pl.ds(f, rows, stride=blocks), :
        ].astype(BF)


def pack_cot_kernel(experts, capacity, routes_ref, gates_ref, cot_ref, out_ref, wide_ref):
    masks = slot_masks(routes_ref[...], experts, capacity)
    both = functools.reduce(lambda a, b: a + b, masks)
    gate = functools.reduce(
        lambda a, b: a + b,
        [
            jnp.sum(m * gates_ref[k : k + 1, :], axis=1, keepdims=True)
            for k, m in enumerate(masks)
        ],
    )
    both = both.astype(BF)
    blocks = cot_ref.shape[1] // LANES

    def block(f):
        rows = jnp.dot(
            both, cot_ref[:, f * LANES : (f + 1) * LANES], preferred_element_type=F32
        )
        return rows * gate

    tile_rows(block, blocks, wide_ref, out_ref)


def pack_input_kernel(experts, capacity, routes_ref, x_ref, out_ref, wide_ref):
    masks = slot_masks(routes_ref[...], experts, capacity)
    both = functools.reduce(lambda a, b: a + b, masks).astype(BF)
    blocks = x_ref.shape[0]
    tile_rows(
        lambda f: jnp.dot(both, x_ref[f], preferred_element_type=F32),
        blocks,
        wide_ref,
        out_ref,
    )


def dact_kernel(ep_ref, c0, c1, c2, c3, down_hbm, out_ref, wide, lhs, weights, sems):
    ep = ep_ref[0]
    quarter = lhs.shape[1]
    copies = []
    for j in range(4):
        start = pl.multiple_of((ep ^ j) * quarter, LANES)
        copy = pltpu.make_async_copy(
            down_hbm.at[:, pl.ds(start, quarter)], weights.at[j], sems.at[j]
        )
        copy.start()
        copies.append(copy)
    for j, part in enumerate((c0, c1, c2, c3)):
        untile_rows(part, quarter // LANES, wide, lhs)
        copies[j].wait()
        product = nt(lhs[...], weights[j])
        if j == 0:
            out_ref[...] = product
        else:
            out_ref[...] += product


def pre_kernel(ep_ref, x0, x1, gate_hbm, up_hbm, g_ref, u_ref, wide, lhs, weights, sems):
    ep = ep_ref[0]
    width = lhs.shape[1]
    copies = []
    for j in range(2):
        for i, w in enumerate((gate_hbm, up_hbm)):
            copy = pltpu.make_async_copy(
                w.at[:, ep ^ j], weights.at[2 * j + i], sems.at[2 * j + i]
            )
            copy.start()
            copies.append(copy)
    for j, part in enumerate((x0, x1)):
        untile_rows(part, width // LANES, wide, lhs)
        for i, ref in enumerate((g_ref, u_ref)):
            copies[2 * j + i].wait()
            w = weights[2 * j + i].reshape(width, -1)
            product = jnp.dot(lhs[...], w, preferred_element_type=F32)
            if j == 0:
                ref[...] = product
            else:
                ref[...] += product


def forward_kernel(
    ep_ref, x2, x3, g_in, u_in, gate_hbm, up_hbm, down_hbm,
    act_ref, silu_ref, dsilu_ref, send_ref, keep_ref,
    wide, lhs, g_acc, u_acc, weights, down, sems,
):
    ep = ep_ref[0]
    width = lhs.shape[1]
    copies = []
    for j in range(2):
        for i, w in enumerate((gate_hbm, up_hbm)):
            copy = pltpu.make_async_copy(
                w.at[:, ep ^ (j + 2)], weights.at[2 * j + i], sems.at[2 * j + i]
            )
            copy.start()
            copies.append(copy)
    for j, q in enumerate((ep ^ 3, ep ^ 2)):
        start = pl.multiple_of(q * width, LANES)
        copy = pltpu.make_async_copy(
            down_hbm.at[:, pl.ds(start, width)], down.at[j], sems.at[4 + j]
        )
        copy.start()
        copies.append(copy)
    for j, part in enumerate((x2, x3)):
        untile_rows(part, width // LANES, wide, lhs)
        for i, (acc, old) in enumerate(((g_acc, g_in), (u_acc, u_in))):
            copies[2 * j + i].wait()
            w = weights[2 * j + i].reshape(width, -1)
            product = jnp.dot(lhs[...], w, preferred_element_type=F32)
            if j == 0:
                acc[...] = old[...] + product
            else:
                acc[...] += product
    pre_gate = g_acc[...]
    pre_up = u_acc[...]
    sigmoid = jax.nn.sigmoid(pre_gate)
    silu = pre_gate * sigmoid
    silu_ref[...] = silu
    dsilu_ref[...] = pre_up * sigmoid * (1.0 + pre_gate * (1.0 - sigmoid))
    act_ref[...] = (silu * pre_up).astype(BF)
    copies[4].wait()
    send_ref[...] = jnp.dot(act_ref[...], down[0], preferred_element_type=F32).astype(BF)
    copies[5].wait()
    keep_ref[...] = jnp.dot(act_ref[...], down[1], preferred_element_type=F32)


def own_out_kernel(ep_ref, act_ref, down_hbm, send_ref, keep_ref, down, sems):
    ep = ep_ref[0]
    width = send_ref.shape[1]
    copies = []
    for j, q in enumerate((ep ^ 1, ep)):
        start = pl.multiple_of(q * width, LANES)
        copy = pltpu.make_async_copy(
            down_hbm.at[:, pl.ds(start, width)], down.at[j], sems.at[j]
        )
        copy.start()
        copies.append(copy)
    copies[0].wait()
    send_ref[...] = jnp.dot(act_ref[...], down[0], preferred_element_type=F32).astype(BF)
    copies[1].wait()
    keep_ref[...] = jnp.dot(act_ref[...], down[1], preferred_element_type=F32)


def grad_kernel(
    ep_ref, dact_ref, silu_ref, dsilu_ref, gate_hbm, up_hbm,
    dgate_ref, dup_ref, send_ref, keep_ref, weights, sems,
):
    ep = ep_ref[0]
    width = send_ref.shape[1]
    copies = []
    for j, q in enumerate((ep ^ 3, ep ^ 2)):
        for i, w in enumerate((gate_hbm, up_hbm)):
            copy = pltpu.make_async_copy(w.at[q], weights.at[2 * j + i], sems.at[2 * j + i])
            copy.start()
            copies.append(copy)
    d_act = dact_ref[...]
    dgate_ref[...] = (d_act * dsilu_ref[...]).astype(BF)
    dup_ref[...] = (d_act * silu_ref[...]).astype(BF)
    copies[0].wait()
    copies[1].wait()
    send_ref[...] = (nt(dgate_ref[...], weights[0]) + nt(dup_ref[...], weights[1])).astype(BF)
    copies[2].wait()
    copies[3].wait()
    keep_ref[...] = nt(dgate_ref[...], weights[2]) + nt(dup_ref[...], weights[3])


def own_grad_kernel(
    ep_ref, dgate_ref, dup_ref, gate_hbm, up_hbm, send_ref, keep_ref, weights, sems
):
    ep = ep_ref[0]
    copies = []
    for j, q in enumerate((ep ^ 1, ep)):
        for i, w in enumerate((gate_hbm, up_hbm)):
            copy = pltpu.make_async_copy(w.at[q], weights.at[2 * j + i], sems.at[2 * j + i])
            copy.start()
            copies.append(copy)
    copies[0].wait()
    copies[1].wait()
    send_ref[...] = (nt(dgate_ref[...], weights[0]) + nt(dup_ref[...], weights[1])).astype(BF)
    copies[2].wait()
    copies[3].wait()
    keep_ref[...] = nt(dgate_ref[...], weights[2]) + nt(dup_ref[...], weights[3])


def chip_sum_kernel(keep_ref, came_ref, out_ref):
    out_ref[...] = (keep_ref[...] + came_ref[...].astype(F32)).astype(BF)


def finish_kernel(keep_ref, near_ref, far_ref, out_ref, wide_ref):
    def block(f):
        cols = slice(f * LANES, (f + 1) * LANES)
        return keep_ref[:, cols] + near_ref[:, cols].astype(F32) + far_ref[:, cols].astype(F32)

    tile_rows(block, keep_ref.shape[1] // LANES, wide_ref, out_ref)


def combine_out_kernel(
    experts, capacity, routes_ref, gates_ref, cot_ref, rows_ref, out_ref, grad_ref, wide, lhs
):
    masks = slot_masks(routes_ref[...], experts, capacity)
    untile_rows(rows_ref, lhs.shape[1] // LANES, wide, lhs)
    cot = cot_ref[...].astype(F32)
    total = None
    grads = []
    for k, m in enumerate(masks):
        picked = tn(m.astype(BF), lhs[...])
        term = gates_ref[:, k : k + 1] * picked
        total = term if total is None else total + term
        grads.append(jnp.sum(cot * picked, axis=1, keepdims=True))
    out_ref[...] = total.astype(BF)
    grad_ref[...] = jnp.concatenate(grads, axis=1)


def combine_grad_kernel(experts, capacity, routes_ref, rows_ref, out_ref, wide, lhs):
    masks = slot_masks(routes_ref[...], experts, capacity)
    both = functools.reduce(lambda a, b: a + b, masks).astype(BF)
    untile_rows(rows_ref, lhs.shape[1] // LANES, wide, lhs)
    out_ref[...] = tn(both, lhs[...]).astype(BF)


SMEM = pl.BlockSpec(memory_space=pltpu.SMEM)
VMEM = pl.BlockSpec(memory_space=pltpu.VMEM)
ANY = pl.BlockSpec(memory_space=pl.ANY)


def call(kernel, specs, outs, scratch, flops, moved, *operands):
    single = not isinstance(outs, (list, tuple))
    return pl.pallas_call(
        kernel,
        out_shape=outs,
        in_specs=specs,
        out_specs=VMEM if single else [VMEM] * len(outs),
        scratch_shapes=scratch,
        compiler_params=pltpu.CompilerParams(vmem_limit_bytes=40 * 1024 * 1024),
        cost_estimate=pl.CostEstimate(flops=flops, bytes_accessed=moved, transcendentals=0),
    )(*operands)


def local(layer_input, output_cot, routes, gate_values, gate_weight, up_weight, down_weight):
    tokens, picks = routes.shape
    experts = lax.axis_size(("cp", "tp"))
    tp = lax.axis_size("tp")
    ep_size = lax.axis_size("ep")
    capacity = max(2, tokens * picks * 5 // (4 * experts))
    slots = experts * capacity
    width = output_cot.shape[1]
    blocks = width // LANES
    hidden = gate_weight.shape[2]
    tiled = slots * blocks
    ep = lax.axis_index("ep").astype(jnp.int32).reshape(1)
    routes_t = routes.T
    gates_t = gate_values.T
    down_w = down_weight[0]
    gate_x = gate_weight.reshape(tp, ep_size, LANES, hidden)
    up_x = up_weight.reshape(tp, ep_size, LANES, hidden)
    gate_q = gate_weight.reshape(ep_size, width, hidden)
    up_q = up_weight.reshape(ep_size, width, hidden)
    shape = jax.ShapeDtypeStruct
    wide = pltpu.VMEM((tiled, LANES), F32)
    lhs = pltpu.VMEM((slots, width), BF)
    near = [(i, i ^ 1) for i in range(ep_size)]
    far = [(i, i ^ 2) for i in range(ep_size)]

    def exchange(rows):
        return lax.all_to_all(
            rows.reshape(experts, capacity * blocks, LANES),
            ("cp", "tp"),
            split_axis=0,
            concat_axis=0,
            tiled=True,
        ).reshape(tiled, LANES)

    def gather(own):
        across = lax.ppermute(own, "ep", far)
        beside = lax.ppermute(own, "ep", near)
        return own, beside, across, lax.ppermute(across, "ep", near)

    x_cols = lax.all_to_all(
        layer_input.reshape(tp, tokens, LANES), "tp", split_axis=0, concat_axis=0, tiled=True
    )
    moved = slots * width * 6
    cot_rows = call(
        functools.partial(pack_cot_kernel, experts, capacity),
        [VMEM] * 3, shape((tiled, LANES), BF), [wide], 10**8, moved,
        routes_t, gates_t, output_cot,
    )
    c0, c1, c2, c3 = gather(exchange(cot_rows))
    x_rows = call(
        functools.partial(pack_input_kernel, experts, capacity),
        [VMEM] * 2, shape((tiled, LANES), BF), [wide], 10**8, moved,
        routes_t, x_cols,
    )
    x0, x1, x2, x3 = gather(exchange(x_rows))

    sems = lambda n: pltpu.SemaphoreType.DMA((n,))
    acc = shape((slots, hidden), F32)
    dot_flops = 2 * slots * width * hidden
    d_act = call(
        dact_kernel, [SMEM] + [VMEM] * 4 + [ANY], acc,
        [wide, lhs, pltpu.VMEM((4, hidden, width), BF), sems(4)],
        4 * dot_flops, 2 * moved, ep, c0, c1, c2, c3, down_w,
    )
    weights_x = pltpu.VMEM((4, tp, LANES, hidden), BF)
    weights_q = pltpu.VMEM((4, width, hidden), BF)
    down_half = pltpu.VMEM((2, hidden, width), BF)
    g_part, u_part = call(
        pre_kernel, [SMEM] + [VMEM] * 2 + [ANY] * 2, [acc, acc],
        [wide, lhs, weights_x, sems(4)],
        4 * dot_flops, 2 * moved, ep, x0, x1, gate_x, up_x,
    )
    send_t = shape((slots, width), BF)
    keep_t = shape((slots, width), F32)
    hid = shape((slots, hidden), BF)
    act, silu, dsilu, out_send, out_keep = call(
        forward_kernel, [SMEM] + [VMEM] * 4 + [ANY] * 3, [hid, acc, acc, send_t, keep_t],
        [wide, lhs, pltpu.VMEM((slots, hidden), F32), pltpu.VMEM((slots, hidden), F32),
         weights_x, down_half, sems(6)],
        6 * dot_flops, 3 * moved, ep, x2, x3, g_part, u_part, gate_x, up_x, down_w,
    )
    out_far = call(
        chip_sum_kernel, [VMEM] * 2, send_t, [], 10**6, moved,
        out_keep, lax.ppermute(out_send, "ep", near),
    )
    out_far = lax.ppermute(out_far, "ep", far)
    out_send2, out_keep2 = call(
        own_out_kernel, [SMEM, VMEM, ANY], [send_t, keep_t], [down_half, sems(2)],
        2 * dot_flops, 2 * moved, ep, act, down_w,
    )
    out_near = lax.ppermute(out_send2, "ep", near)
    d_gate, d_up, grad_send, grad_keep = call(
        grad_kernel, [SMEM] + [VMEM] * 3 + [ANY] * 2, [hid, hid, send_t, keep_t],
        [weights_q, sems(4)],
        4 * dot_flops, 3 * moved, ep, d_act, silu, dsilu, gate_q, up_q,
    )
    grad_far = call(
        chip_sum_kernel, [VMEM] * 2, send_t, [], 10**6, moved,
        grad_keep, lax.ppermute(grad_send, "ep", near),
    )
    grad_far = lax.ppermute(grad_far, "ep", far)
    grad_send2, grad_keep2 = call(
        own_grad_kernel, [SMEM] + [VMEM] * 2 + [ANY] * 2, [send_t, keep_t],
        [weights_q, sems(4)],
        4 * dot_flops, 3 * moved, ep, d_gate, d_up, gate_q, up_q,
    )
    grad_near = lax.ppermute(grad_send2, "ep", near)
    out_rows = call(
        finish_kernel, [VMEM] * 3, shape((tiled, LANES), BF), [wide], 10**6, moved,
        out_keep2, out_near, out_far,
    )
    out_back = exchange(out_rows)
    grad_rows = call(
        finish_kernel, [VMEM] * 3, shape((tiled, LANES), BF), [wide], 10**6, moved,
        grad_keep2, grad_near, grad_far,
    )
    grad_back = exchange(grad_rows)
    moe_output, gate_grad = call(
        functools.partial(combine_out_kernel, experts, capacity), [VMEM] * 4,
        [shape((tokens, width), BF), shape((tokens, picks), F32)], [wide, lhs], 10**8, moved,
        routes_t, gate_values, output_cot, out_back,
    )
    gate_grad = gate_grad + lax.ppermute(gate_grad, "ep", near)
    gate_grad = gate_grad + lax.ppermute(gate_grad, "ep", far)
    input_grad = call(
        functools.partial(combine_grad_kernel, experts, capacity), [VMEM] * 2,
        shape((tokens, width), BF), [wide, lhs], 10**8, moved,
        routes_t, grad_back,
    )
    return (moe_output, input_grad, gate_grad)


def solution(mesh):
    placed = (
        P("cp", ("tp", "ep")),
        P(("cp", "tp"), "ep"),
        P(("cp", "tp"), None),
        P(("cp", "tp"), None),
        P(("cp", "tp"), None, "ep"),
        P(("cp", "tp"), None, "ep"),
        P(("cp", "tp"), "ep", None),
    )
    return jax.shard_map(
        local,
        mesh=mesh,
        in_specs=placed,
        out_specs=(P(("cp", "tp"), "ep"), P(("cp", "tp"), "ep"), P(("cp", "tp"), None)),
        check_vma=False,
    )
```

time: 386 us -> 189 us (0.49)
  waiting for transfers between devices: 208 us -> 91.3 us
  local copies, waits for them, and re-layouts: 62.1 us -> 9.64 us
  Pallas kernels: 0 us -> 27.2 us
  other arithmetic: 18.5 us -> 0.02 us
  matrix products: 17.1 us -> 0 us
  between operations: 14 us -> 0.97 us
  starting transfers between devices: 50 us -> 46 us
    all_to_all x5 -> x4, waiting for transfers between devices: 117 us -> 32.8 us  [exchange(): lax.all_to_all(rows.reshape(experts, capacity * blocks, LANES), ('cp', 't...]
    reduce_scatter x2 -> x0, waiting for transfers between devices: 69.8 us -> none  [the longest x1 36.6 us: local(): lax.psum_scatter(grad_part.astype(jnp.float32).astype(jnp.bfloat16), 'ep'...]
    ppermute x0 -> x14, waiting for transfers between devices: none -> 58.4 us  [the longest x2 27.5 us: gather(): across = lax.ppermute(own, 'ep', far)]
    gather x6 -> x0, local copies, waits for them, and re-layouts: 28.3 us -> none  [the longest x2 14.1 us: local(): outgoing = jnp.where(filled, token_feats[source // pick_count], 0)]
    pallas_call x0 -> x14, Pallas kernels: none -> 27.2 us  [call(): pl.pallas_call(kernel, out_shape=outs, in_specs=specs, out_specs=VMEM if...]
    all_gather x2 -> x0, waiting for transfers between devices: 21.1 us -> none  [the longest x1 21.1 us: local(): feature = lax.all_gather(layer_input, 'ep', axis=1, tiled=True)]
    reshape x6 -> x0, local copies, waits for them, and re-layouts: 17.1 us -> none  [the longest x1 4.75 us: local(): arrived = lax.all_to_all(outgoing.reshape(expert_count, capacity, -1), ('...]
    dot_general x6 -> x0, matrix products: 17.1 us -> none  [the longest x3 8.15 us: transposed(): lax.dot_general(left, right, (((1,), (1,)), ((), ())), preferred_element_...]
  transfers between devices with their start and end apart: 9 -> 18, of which waited for: 6 -> 7; matrix products, arithmetic and copies ran while one was open for 21% -> 0% of each run, Pallas kernels for 0% -> 14%
where the time goes in v1:
time: 189 us; the launch traced here: 188 us
  waiting for transfers between devices  91.3 us (48%)
  starting transfers between devices  46 us (24%)
  Pallas kernels  27.2 us (14%)
  blocking collectives  12.5 us (7%)
  local copies, waits for them, and re-layouts  9.64 us (5%)
    all_to_all x4, starting transfers between devices, exchange(): lax.all_to_all(rows.reshape(experts, capacity * blocks, LANES), ('cp', 't...  37.8 us
    all_to_all x4, waiting for transfers between devices, exchange(): lax.all_to_all(rows.reshape(experts, capacity * blocks, LANES), ('cp', 't...  32.8 us
    ppermute x2, waiting for transfers between devices, gather(): across = lax.ppermute(own, 'ep', far)  27.5 us
    pallas_call x14, Pallas kernels, call(): pl.pallas_call(kernel, out_shape=outs, in_specs=specs, out_specs=VMEM if...  27.2 us
    ppermute x1, waiting for transfers between devices, local(): grad_far = lax.ppermute(grad_far, 'ep', far)  19.1 us
    all_to_all x1, blocking collectives, local(): lax.all_to_all(layer_input.reshape(tp, tokens, LANES), 'tp', split_axis=0...  12.5 us
    ppermute x1, waiting for transfers between devices, local(): out_far = lax.ppermute(out_far, 'ep', far)  10.6 us
    unnamed x38, local copies, waits for them, and re-layouts  9.64 us
  transfers between devices with their start and end apart: 18, of which 7 were waited for; matrix products, arithmetic and copies ran while one was open for 0% of the time, Pallas kernels for 14%

profile of v1, /device:TPU:4, one launch (start us, length us, event | category | flops | bytes accessed | tf_op | source)
XLA Modules:
  0.0 187.5 jit_solution(10151750741910663322)
XLA Ops:
  0.6 0.0 copy-start.16
  0.7 12.5 %all_to_all.25.x_ref = bf16[8,128,128]{2,1,0:T(8,128)(2,1)S(1)} all-to-all(bf16[8,128,128]{2,1,0:T(8,128)(2,1)} %bitcast.37), channel_id=1, replica_groups=mesh['cp'=8,'tp'=8,'ep'=4] {'tp'}, dimensions={0} | all-to-all | bytes 524288 | tf_op jit(solution)/shard_map/all_to_all | solution.py:338
  13.1 0.7 copy-done.15
  13.8 0.6 shard_map.94
  14.4 0.8 copy-done.6
  15.2 10.9 %all-to-all-start.1 = ((bf16[64,40,128]{2,1,0:T(8,128)(2,1)}), bf16[64,40,128]{2,1,0:T(8,128)(2,1)}, u32[]{:S(2)}, u32[]{:S(2)}) async-start(bf16[64,40,128]{2,1,0:T(8,128)(2,1)} %bitcast.30), calls=%async_computation.1 | async-start | bytes 1310720 | tf_op jit(solution)/shard_map/all_to_all | solution.py:325
  26.2 0.6 shard_map.101
  26.8 0.8 copy-done.5
  27.6 17.7 %all-to-all-done.1 = bf16[64,40,128]{2,1,0:T(8,128)(2,1)} async-done(((bf16[64,40,128]{2,1,0:T(8,128)(2,1)}), bf16[64,40,128]{2,1,0:T(8,128)(2,1)}, u32[]{:S(2)}, u32[]{:S(2)}) %all-to-all-start.1) | async-done | bytes 655392 | tf_op jit(solution)/shard_map/all_to_all | solution.py:325
  45.3 5.9 %all-to-all-start.3 = ((bf16[64,40,128]{2,1,0:T(8,128)(2,1)}), bf16[64,40,128]{2,1,0:T(8,128)(2,1)}, u32[]{:S(2)}, u32[]{:S(2)}) async-start(bf16[64,40,128]{2,1,0:T(8,128)(2,1)} %bitcast.28), calls=%async_computation.3 | async-start | bytes 1310720 | tf_op jit(solution)/shard_map/all_to_all | solution.py:325
  51.2 0.9 collective-permute-start
  52.1 0.0 collective-permute-start.2
  52.1 21.5 %collective-permute-done.x2 = bf16[2560,128]{1,0:T(8,128)(2,1)} collective-permute-done((bf16[2560,128]{1,0:T(8,128)(2,1)}, bf16[2560,128]{1,0:T(8,128)(2,1)}, u32[]{:S(2)}, u32[]{:S(2)}) %collective-permute-start) | collective-permute-done | bytes 655392 | tf_op jit(solution)/shard_map/ppermute | solution.py:334
  73.7 0.0 collective-permute-start.1
  73.7 0.0 all-to-all-done.3
  73.7 1.4 collective-permute-start.7
  75.1 0.0 collective-permute-done.2.x1
  75.1 1.9 %copy-done.1 = bf16[1,4096,384]{2,1,0:T(8,128)(2,1)S(1)} copy-done((bf16[1,4096,384]{2,1,0:T(8,128)(2,1)S(1)}, bf16[1,4096,384]{2,1,0:T(8,128)(2,1)}, u32[]{:S(2)}) %copy-start.1) | copy-done | bytes 3145752
  77.0 3.8 %shard_map.95 = (f32[320,384]{1,0:T(8,128)S(1)}, f32[320,384]{1,0:T(8,128)S(1)}) custom-call(s32[1]{0:T(128)} %bitcast.1.ep_ref, bf16[2560,128]{1,0:T(8,128)(2,1)} %bitcast.4.x0, bf16[2560,128]{1,0:T(8,128)(2,1)} %collective-permute-done.2.x1, bf16[8,4,128,384]{3,2,1,0:T(8,128)(2,1)S(1)} %bitcast.17, bf16[8,4,128,384]{3,2,1,0:T(8,128)(2,1)S(1)} %bitcast.21), custom_call_target="tpu_custom_call" | custom-call | flops 1006632960 | bytes 3932160 | tf_op jit(solution)/shard_map/pallas_call | solution.py:288
  80.8 0.0 collective-permute-done.1.x3
  80.8 0.0 copy-start.4
  80.8 5.1 %shard_map.96 = (bf16[320,384]{1,0:T(8,128)(2,1)S(1)}, f32[320,384]{1,0:T(8,128)S(1)}, f32[320,384]{1,0:T(8,128)S(1)}, bf16[320,1024]{1,0:T(8,128)(2,1)S(1)}, f32[320,1024]{1,0:T(8,128)S(1)}) custom-call(s32[1]{0:T(128)} %bitcast.1.ep_ref, bf16[2560,128]{1,0:T(8,128)(2,1)} %collective-permute-done.x2, bf16[2560,128]{1,0:T(8,128)(2,1)} %collective-permute-done.1.x3, ...), custom_call_target="tpu_custom_call" | custom-call | flops 1509949440 | bytes 5898240 | tf_op jit(solution)/shard_map/pallas_call | solution.py:288
  85.9 0.3 collective-permute-start.4
  86.2 0.3 collective-permute-start.6
  86.5 6.0 %collective-permute-done.7.c2 = bf16[2560,128]{1,0:T(8,128)(2,1)S(1)} collective-permute-done((bf16[2560,128]{1,0:T(8,128)(2,1)}, bf16[2560,128]{1,0:T(8,128)(2,1)S(1)}, u32[]{:S(2)}, u32[]{:S(2)}) %collective-permute-start.7) | collective-permute-done | bytes 655392 | tf_op jit(solution)/shard_map/ppermute | solution.py:334
  92.5 0.0 collective-permute-start.8
  92.5 1.2 shard_map.97
  93.7 0.8 collective-permute-start.3
  94.5 0.0 collective-permute-done.4.came_ref
  94.5 0.2 shard_map.98
  94.7 1.5 collective-permute-start.5
  96.2 0.0 collective-permute-done.6.c1
  96.2 0.0 collective-permute-done.8.c3
  96.2 3.9 %shard_map.102.dact_ref = f32[320,384]{1,0:T(8,128)S(1)} custom-call(s32[1]{0:T(128)} %bitcast.1.ep_ref, bf16[2560,128]{1,0:T(8,128)(2,1)} %bitcast.12.c0, bf16[2560,128]{1,0:T(8,128)(2,1)S(1)} %collective-permute-done.6.c1, bf16[2560,128]{1,0:T(8,128)(2,1)S(1)} %collective-permute-done.7.c2, bf16[2560,128]{1,0:T(8,128)(2,1)S(1)} %collective-permute-done.8.c3, ...), custom_call_target="tpu_custom_call" | custom-call | flops 1006632960 | bytes 3932160 | tf_op jit(solution)/shard_map/pallas_call | solution.py:288
  100.1 2.1 %shard_map.103 = (bf16[320,384]{1,0:T(8,128)(2,1)S(1)}, bf16[320,384]{1,0:T(8,128)(2,1)S(1)}, bf16[320,1024]{1,0:T(8,128)(2,1)}, f32[320,1024]{1,0:T(8,128)S(1)}) custom-call(s32[1]{0:T(128)} %bitcast.1.ep_ref, f32[320,384]{1,0:T(8,128)S(1)} %shard_map.102.dact_ref, f32[320,384]{1,0:T(8,128)S(1)} %get-tuple-element.28.silu_ref, ...), custom_call_target="tpu_custom_call" | custom-call | flops 1006632960 | bytes 5898240 | tf_op jit(solution)/shard_map/pallas_call | solution.py:288
  102.2 0.0 copy-start.11
  102.3 0.0 copy-start.13
  102.3 0.1 collective-permute-start.10
  102.4 0.0 collective-permute-done.3.near_ref
  102.4 10.6 %collective-permute-done.5.far_ref = bf16[320,1024]{1,0:T(8,128)(2,1)S(1)} collective-permute-done((bf16[320,1024]{1,0:T(8,128)(2,1)S(1)}, bf16[320,1024]{1,0:T(8,128)(2,1)S(1)}, u32[]{:S(2)}, u32[]{:S(2)}) %collective-permute-start.5) | collective-permute-done | bytes 655392 | tf_op jit(solution)/shard_map/ppermute | solution.py:384
  112.9 0.8 shard_map.99
  113.7 0.8 copy-done.7
  114.6 10.4 %all-to-all-start.2 = ((bf16[64,40,128]{2,1,0:T(8,128)(2,1)}), bf16[64,40,128]{2,1,0:T(8,128)(2,1)}, u32[]{:S(2)}, u32[]{:S(2)}) async-start(bf16[64,40,128]{2,1,0:T(8,128)(2,1)} %bitcast.31), calls=%async_computation.2 | async-start | bytes 1310720 | tf_op jit(solution)/shard_map/all_to_all | solution.py:325
  125.0 0.0 copy-start.3
  125.0 1.9 %copy-done.3 = bf16[1,4096,384]{2,1,0:T(8,128)(2,1)S(1)} copy-done((bf16[1,4096,384]{2,1,0:T(8,128)(2,1)S(1)}, bf16[1,4096,384]{2,1,0:T(8,128)(2,1)}, u32[]{:S(2)}) %copy-start.3) | copy-done | bytes 3145752
  126.9 0.9 copy-done.12
  127.8 0.9 copy-done.14
  128.8 2.0 %shard_map.104 = (bf16[320,1024]{1,0:T(8,128)(2,1)S(1)}, f32[320,1024]{1,0:T(8,128)S(1)}) custom-call(s32[1]{0:T(128)} %bitcast.1.ep_ref, bf16[320,384]{1,0:T(8,128)(2,1)S(1)} %copy-done.12, bf16[320,384]{1,0:T(8,128)(2,1)S(1)} %copy-done.14, bf16[4,1024,384]{2,1,0:T(8,128)(2,1)S(1)} %bitcast.20, bf16[4,1024,384]{2,1,0:T(8,128)(2,1)S(1)} %bitcast.24), custom_call_target="tpu_custom_call" | custom-call | flops 1006632960 | bytes 5898240 | tf_op jit(solution)/shard_map/pallas_call | solution.py:288
  130.8 0.1 collective-permute-start.9
  130.9 0.0 collective-permute-done.10.came_ref
  130.9 1.2 shard_map.105
  132.1 1.6 collective-permute-start.11
  133.7 19.1 %collective-permute-done.11.far_ref = bf16[320,1024]{1,0:T(8,128)(2,1)S(1)} collective-permute-done((bf16[320,1024]{1,0:T(8,128)(2,1)S(1)}, bf16[320,1024]{1,0:T(8,128)(2,1)S(1)}, u32[]{:S(2)}, u32[]{:S(2)}) %collective-permute-start.11) | collective-permute-done | bytes 655392 | tf_op jit(solution)/shard_map/ppermute | solution.py:399
  152.8 1.6 shard_map.106
  154.4 10.6 %all-to-all-start.4 = ((bf16[64,40,128]{2,1,0:T(8,128)(2,1)}), bf16[64,40,128]{2,1,0:T(8,128)(2,1)S(1)}, u32[]{:S(2)}, u32[]{:S(2)}) async-start(bf16[64,40,128]{2,1,0:T(8,128)(2,1)} %bitcast.15), calls=%async_computation.4 | async-start | bytes 1310720 | tf_op jit(solution)/shard_map/all_to_all | solution.py:325
  165.0 0.1 copy.10.gates_ref
  165.1 2.7 %shard_map.100 = (bf16[128,1024]{1,0:T(8,128)(2,1)}, f32[128,2]{1,0:T(8,128)S(1)}) custom-call(s32[2,128]{1,0:T(2,128)S(1)} %bitcast.34, f32[128,2]{1,0:T(8,128)S(1)} %copy.10.gates_ref, bf16[128,1024]{1,0:T(8,128)(2,1)S(1)} %copy-done.10, bf16[2560,128]{1,0:T(8,128)(2,1)} %bitcast.9.rows_ref), custom_call_target="tpu_custom_call" | custom-call | flops 100000000 | bytes 1966080 | tf_op jit(solution)/shard_map/pallas_call | solution.py:288
  167.8 0.0 collective-permute-start.12
  167.8 1.3 collective-permute-done.12
  169.1 1.2 collective-permute-start.13
  170.3 15.1 %all-to-all-done.4 = bf16[64,40,128]{2,1,0:T(8,128)(2,1)S(1)} async-done(((bf16[64,40,128]{2,1,0:T(8,128)(2,1)}), bf16[64,40,128]{2,1,0:T(8,128)(2,1)S(1)}, u32[]{:S(2)}, u32[]{:S(2)}) %all-to-all-start.4) | async-done | bytes 655392 | tf_op jit(solution)/shard_map/all_to_all | solution.py:325
  185.4 1.4 shard_map.107
  186.9 0.0 collective-permute-done.13
  186.9 0.6 copy.11
  (27 shorter events, 0.1 us)
Async XLA Ops:
  0.6 25.5 %copy-start.10 = (bf16[128,1024]{1,0:T(8,128)(2,1)S(1)}, bf16[128,1024]{1,0:T(8,128)(2,1)}, u32[]{:S(2)}) copy-start(bf16[128,1024]{1,0:T(8,128)(2,1)} %cot_ref.3) | copy-start | bytes 786436
  0.6 25.5 %copy-start.16 = (s32[128,2]{0,1:T(2,128)S(1)}, s32[128,2]{0,1:T(2,128)}, u32[]{:S(2)}) copy-start(s32[128,2]{0,1:T(2,128)} %param.9) | copy-start | bytes 3076
  0.7 25.5 %copy-start.17 = (f32[128,2]{0,1:T(2,128)S(1)}, f32[128,2]{0,1:T(2,128)}, u32[]{:S(2)}) copy-start(f32[128,2]{0,1:T(2,128)} %param.10) | copy-start | bytes 3076
  13.1 0.7 copy-start.15
  14.4 0.8 copy-start.6
  15.2 59.8 %copy-start = (bf16[1,4096,384]{2,1,0:T(8,128)(2,1)S(1)}, bf16[1,4096,384]{2,1,0:T(8,128)(2,1)}, u32[]{:S(2)}) copy-start(bf16[1,4096,384]{2,1,0:T(8,128)(2,1)} %param.11) | copy-start | bytes 9437188
  15.2 30.1 %all-to-all-start.1 = ((bf16[64,40,128]{2,1,0:T(8,128)(2,1)}), bf16[64,40,128]{2,1,0:T(8,128)(2,1)}, u32[]{:S(2)}, u32[]{:S(2)}) async-start(bf16[64,40,128]{2,1,0:T(8,128)(2,1)} %bitcast.30), calls=%async_computation.1 | async-start | bytes 1310720 | tf_op jit(solution)/shard_map/all_to_all | solution.py:325
  26.8 0.8 copy-start.5
  45.3 28.3 %all-to-all-start.3 = ((bf16[64,40,128]{2,1,0:T(8,128)(2,1)}), bf16[64,40,128]{2,1,0:T(8,128)(2,1)}, u32[]{:S(2)}, u32[]{:S(2)}) async-start(bf16[64,40,128]{2,1,0:T(8,128)(2,1)} %bitcast.28), calls=%async_computation.3 | async-start | bytes 1310720 | tf_op jit(solution)/shard_map/all_to_all | solution.py:325
  51.2 22.4 %collective-permute-start = (bf16[2560,128]{1,0:T(8,128)(2,1)}, bf16[2560,128]{1,0:T(8,128)(2,1)}, u32[]{:S(2)}, u32[]{:S(2)}) collective-permute-start(bf16[2560,128]{1,0:T(8,128)(2,1)} %bitcast.4.x0), channel_id=1, source_target_pairs={{0,2},{1,3},{2,0},{3,1},{4,6},{5,7},{6,4},{7,5},{8,10},{9,11},{10,... | collective-permute-start | bytes 1966088 | tf_op jit(solution)/shard_map/ppermute | solution.py:334
  52.1 22.9 %collective-permute-start.2 = (bf16[2560,128]{1,0:T(8,128)(2,1)}, bf16[2560,128]{1,0:T(8,128)(2,1)}, u32[]{:S(2)}, u32[]{:S(2)}) collective-permute-start(bf16[2560,128]{1,0:T(8,128)(2,1)} %bitcast.4.x0), channel_id=1, source_target_pairs={{0,1},{1,0},{2,3},{3,2},{4,5},{5,4},{6,7},{7,6},{8,9},{9,8},{10,11... | collective-permute-start | bytes 1966088 | tf_op jit(solution)/shard_map/ppermute | solution.py:335
  73.7 7.1 %collective-permute-start.1 = (bf16[2560,128]{1,0:T(8,128)(2,1)}, bf16[2560,128]{1,0:T(8,128)(2,1)}, u32[]{:S(2)}, u32[]{:S(2)}) collective-permute-start(bf16[2560,128]{1,0:T(8,128)(2,1)} %collective-permute-done.x2), channel_id=1, source_target_pairs={{0,1},{1,0},{2,3},{3,2},{4,5},{5,4},{6,7},{7,6},{8,9},{9,8},{10,11... | collective-permute-start | bytes 1966088 | tf_op jit(solution)/shard_map/ppermute | solution.py:336
  73.7 18.9 %collective-permute-start.7 = (bf16[2560,128]{1,0:T(8,128)(2,1)}, bf16[2560,128]{1,0:T(8,128)(2,1)S(1)}, u32[]{:S(2)}, u32[]{:S(2)}) collective-permute-start(bf16[2560,128]{1,0:T(8,128)(2,1)} %bitcast.12.c0), channel_id=1, source_target_pairs={{0,2},{1,3},{2,0},{3,1},{4,6},{5,7},{6,4},{7,5},{8,10},{9,11},{10,... | collective-permute-start | bytes 1966088 | tf_op jit(solution)/shard_map/ppermute | solution.py:334
  75.1 1.9 %copy-start.1 = (bf16[1,4096,384]{2,1,0:T(8,128)(2,1)S(1)}, bf16[1,4096,384]{2,1,0:T(8,128)(2,1)}, u32[]{:S(2)}) copy-start(bf16[1,4096,384]{2,1,0:T(8,128)(2,1)} %param.12) | copy-start | bytes 9437188
  80.8 11.8 %copy-start.4 = (bf16[1,384,4096]{2,1,0:T(8,128)(2,1)S(1)}, bf16[1,384,4096]{2,1,0:T(8,128)(2,1)}, u32[]{:S(2)}) copy-start(bf16[1,384,4096]{2,1,0:T(8,128)(2,1)} %param.13) | copy-start | bytes 9437188
  85.9 8.6 %collective-permute-start.4 = (bf16[320,1024]{1,0:T(8,128)(2,1)S(1)}, bf16[320,1024]{1,0:T(8,128)(2,1)S(1)}, u32[]{:S(2)}, u32[]{:S(2)}) collective-permute-start(bf16[320,1024]{1,0:T(8,128)(2,1)S(1)} %get-tuple-element.26), channel_id=1, source_target_pairs={{0,1},{1,0},{2,3},{3,2},{4,5},{5,4},{6,7},{7,6},{8,9},{9,8},{10,11... | collective-permute-start | bytes 1966088 | tf_op jit(solution)/shard_map/ppermute | solution.py:382
  86.2 9.9 %collective-permute-start.6 = (bf16[2560,128]{1,0:T(8,128)(2,1)}, bf16[2560,128]{1,0:T(8,128)(2,1)S(1)}, u32[]{:S(2)}, u32[]{:S(2)}) collective-permute-start(bf16[2560,128]{1,0:T(8,128)(2,1)} %bitcast.12.c0), channel_id=1, source_target_pairs={{0,1},{1,0},{2,3},{3,2},{4,5},{5,4},{6,7},{7,6},{8,9},{9,8},{10,11... | collective-permute-start | bytes 1966088 | tf_op jit(solution)/shard_map/ppermute | solution.py:335
  92.5 3.6 %collective-permute-start.8 = (bf16[2560,128]{1,0:T(8,128)(2,1)S(1)}, bf16[2560,128]{1,0:T(8,128)(2,1)S(1)}, u32[]{:S(2)}, u32[]{:S(2)}) collective-permute-start(bf16[2560,128]{1,0:T(8,128)(2,1)S(1)} %collective-permute-done.7.c2), channel_id=1, source_target_pairs={{0,1},{1,0},{2,3},{3,2},{4,5},{5,4},{6,7},{7,6},{8,9},{9,8},{10,11... | collective-permute-start | bytes 1966088 | tf_op jit(solution)/shard_map/ppermute | solution.py:336
  93.7 8.6 %collective-permute-start.3 = (bf16[320,1024]{1,0:T(8,128)(2,1)S(1)}, bf16[320,1024]{1,0:T(8,128)(2,1)S(1)}, u32[]{:S(2)}, u32[]{:S(2)}) collective-permute-start(bf16[320,1024]{1,0:T(8,128)(2,1)S(1)} %get-tuple-element.24), channel_id=1, source_target_pairs={{0,1},{1,0},{2,3},{3,2},{4,5},{5,4},{6,7},{7,6},{8,9},{9,8},{10,11... | collective-permute-start | bytes 1966088 | tf_op jit(solution)/shard_map/ppermute | solution.py:389
  94.7 18.3 %collective-permute-start.5 = (bf16[320,1024]{1,0:T(8,128)(2,1)S(1)}, bf16[320,1024]{1,0:T(8,128)(2,1)S(1)}, u32[]{:S(2)}, u32[]{:S(2)}) collective-permute-start(bf16[320,1024]{1,0:T(8,128)(2,1)S(1)} %shard_map.98), channel_id=1, source_target_pairs={{0,2},{1,3},{2,0},{3,1},{4,6},{5,7},{6,4},{7,5},{8,10},{9,11},{10,... | collective-permute-start | bytes 1966088 | tf_op jit(solution)/shard_map/ppermute | solution.py:384
  96.2 3.9 %copy-start.2 = (bf16[1,4096,384]{2,1,0:T(8,128)(2,1)S(1)}, bf16[1,4096,384]{2,1,0:T(8,128)(2,1)}, u32[]{:S(2)}) copy-start(bf16[1,4096,384]{2,1,0:T(8,128)(2,1)} %param.12) | copy-start | bytes 9437188
  102.2 11.5 %copy-start.8 = (f32[320,1024]{1,0:T(8,128)}, f32[320,1024]{1,0:T(8,128)S(1)}, u32[]{:S(2)}) copy-start(f32[320,1024]{1,0:T(8,128)S(1)} %get-tuple-element.34.keep_ref) | copy-start | bytes 3932164
  102.2 11.5 %copy-start.11 = (bf16[320,384]{1,0:T(8,128)(2,1)}, bf16[320,384]{1,0:T(8,128)(2,1)S(1)}, u32[]{:S(2)}) copy-start(bf16[320,384]{1,0:T(8,128)(2,1)S(1)} %get-tuple-element.30.dgate_ref) | copy-start | bytes 737284
  102.3 11.5 %copy-start.13 = (bf16[320,384]{1,0:T(8,128)(2,1)}, bf16[320,384]{1,0:T(8,128)(2,1)S(1)}, u32[]{:S(2)}) copy-start(bf16[320,384]{1,0:T(8,128)(2,1)S(1)} %get-tuple-element.31.dup_ref) | copy-start | bytes 737284
  102.3 28.6 %collective-permute-start.10 = (bf16[320,1024]{1,0:T(8,128)(2,1)}, bf16[320,1024]{1,0:T(8,128)(2,1)}, u32[]{:S(2)}, u32[]{:S(2)}) collective-permute-start(bf16[320,1024]{1,0:T(8,128)(2,1)} %get-tuple-element.35), channel_id=1, source_target_pairs={{0,1},{1,0},{2,3},{3,2},{4,5},{5,4},{6,7},{7,6},{8,9},{9,8},{10,11... | collective-permute-start | bytes 1966088 | tf_op jit(solution)/shard_map/ppermute | solution.py:397
  113.7 0.8 copy-start.7
  114.6 39.8 %all-to-all-start.2 = ((bf16[64,40,128]{2,1,0:T(8,128)(2,1)}), bf16[64,40,128]{2,1,0:T(8,128)(2,1)}, u32[]{:S(2)}, u32[]{:S(2)}) async-start(bf16[64,40,128]{2,1,0:T(8,128)(2,1)} %bitcast.31), calls=%async_computation.2 | async-start | bytes 1310720 | tf_op jit(solution)/shard_map/all_to_all | solution.py:325
  125.0 1.9 %copy-start.3 = (bf16[1,4096,384]{2,1,0:T(8,128)(2,1)S(1)}, bf16[1,4096,384]{2,1,0:T(8,128)(2,1)}, u32[]{:S(2)}) copy-start(bf16[1,4096,384]{2,1,0:T(8,128)(2,1)} %param.12) | copy-start | bytes 9437188
  126.9 0.9 copy-start.12
  127.8 0.9 copy-start.14
  128.8 2.1 %copy-start.9 = (f32[320,1024]{1,0:T(8,128)S(1)}, f32[320,1024]{1,0:T(8,128)}, u32[]{:S(2)}) copy-start(f32[320,1024]{1,0:T(8,128)} %copy-done.8) | copy-start | bytes 3932164
  130.8 2.9 %collective-permute-start.9 = (bf16[320,1024]{1,0:T(8,128)(2,1)S(1)}, bf16[320,1024]{1,0:T(8,128)(2,1)S(1)}, u32[]{:S(2)}, u32[]{:S(2)}) collective-permute-start(bf16[320,1024]{1,0:T(8,128)(2,1)S(1)} %get-tuple-element.33), channel_id=1, source_target_pairs={{0,1},{1,0},{2,3},{3,2},{4,5},{5,4},{6,7},{7,6},{8,9},{9,8},{10,11... | collective-permute-start | bytes 1966088 | tf_op jit(solution)/shard_map/ppermute | solution.py:405
  132.1 20.7 %collective-permute-start.11 = (bf16[320,1024]{1,0:T(8,128)(2,1)S(1)}, bf16[320,1024]{1,0:T(8,128)(2,1)S(1)}, u32[]{:S(2)}, u32[]{:S(2)}) collective-permute-start(bf16[320,1024]{1,0:T(8,128)(2,1)S(1)} %shard_map.105), channel_id=1, source_target_pairs={{0,2},{1,3},{2,0},{3,1},{4,6},{5,7},{6,4},{7,5},{8,10},{9,11},{10,... | collective-permute-start | bytes 1966088 | tf_op jit(solution)/shard_map/ppermute | solution.py:399
  154.4 31.0 %all-to-all-start.4 = ((bf16[64,40,128]{2,1,0:T(8,128)(2,1)}), bf16[64,40,128]{2,1,0:T(8,128)(2,1)S(1)}, u32[]{:S(2)}, u32[]{:S(2)}) async-start(bf16[64,40,128]{2,1,0:T(8,128)(2,1)} %bitcast.15), calls=%async_computation.4 | async-start | bytes 1310720 | tf_op jit(solution)/shard_map/all_to_all | solution.py:325
  167.8 1.3 collective-permute-start.12
  169.1 17.8 %collective-permute-start.13 = (f32[128,2]{1,0:T(8,128)S(1)}, f32[128,2]{1,0:T(8,128)S(1)}, u32[]{:S(2)}, u32[]{:S(2)}) collective-permute-start(f32[128,2]{1,0:T(8,128)S(1)} %add.6), channel_id=1, source_target_pairs={{0,2},{1,3},{2,0},{3,1},{4,6},{5,7},{6,4},{7,5},{8,10},{9,11},{10,... | collective-permute-start | bytes 3080 | tf_op jit(solution)/shard_map/ppermute | solution.py:422

commit v2 on v1

v2 whole, which is shorter than its diff:
```python
import functools

import jax
import jax.numpy as jnp
from jax import lax
from jax.experimental import pallas as pl
from jax.experimental.pallas import tpu as pltpu
from jax.sharding import PartitionSpec as P

BF = jnp.bfloat16
F32 = jnp.float32
LANES = 128
VMEM_BYTES = 24 * 1024 * 1024
LONG = 2 * 10**11


def nt(left, right):
    return lax.dot_general(
        left, right, (((1,), (1,)), ((), ())), preferred_element_type=F32
    )


def tn(left, right):
    return lax.dot_general(
        left, right, (((0,), (0,)), ((), ())), preferred_element_type=F32
    )


def slot_masks(routes, experts, capacity):
    picks, tokens = routes.shape
    expert = lax.broadcasted_iota(jnp.int32, (experts, tokens), 0)
    earlier = (
        lax.broadcasted_iota(jnp.int32, (tokens, tokens), 0)
        < lax.broadcasted_iota(jnp.int32, (tokens, tokens), 1)
    ).astype(F32).astype(BF)
    slot = lax.broadcasted_iota(jnp.int32, (experts * capacity, tokens), 0)
    taken = jnp.zeros((experts, 1), F32)
    masks = []
    for k in range(picks):
        named = routes[k : k + 1, :]
        chosen = (expert == named).astype(F32)
        before = jnp.dot(chosen.astype(BF), earlier, preferred_element_type=F32) + taken
        rank = jnp.sum(before * chosen, axis=0, keepdims=True)
        place = named * capacity + rank.astype(jnp.int32)
        masks.append((slot == place).astype(F32))
        taken = taken + jnp.sum(chosen, axis=1, keepdims=True)
    return masks


def tile_rows(values, blocks, wide_ref, out_ref):
    rows = wide_ref.shape[0] // blocks
    for f in range(blocks):
        wide_ref[pl.ds(f, rows, stride=blocks), :] = values(f)
    out_ref[...] = wide_ref[...].astype(BF)


def untile_rows(in_ref, blocks, wide_ref, out_ref):
    rows = wide_ref.shape[0] // blocks
    wide_ref[...] = in_ref[...].astype(F32)
    for f in range(blocks):
        out_ref[:, f * LANES : (f + 1) * LANES] = wide_ref[
            pl.ds(f, rows, stride=blocks), :
        ].astype(BF)


def pack_cot_kernel(
    experts, capacity, routes_ref, gates_ref, cot_ref, out_ref, wide_ref
):
    masks = slot_masks(routes_ref[...], experts, capacity)
    both = functools.reduce(lambda a, b: a + b, masks)
    gate = functools.reduce(
        lambda a, b: a + b,
        [
            jnp.sum(m * gates_ref[k : k + 1, :], axis=1, keepdims=True)
            for k, m in enumerate(masks)
        ],
    )
    both = both.astype(BF)
    blocks = cot_ref.shape[1] // LANES

    def block(f):
        rows = jnp.dot(
            both, cot_ref[:, f * LANES : (f + 1) * LANES], preferred_element_type=F32
        )
        return rows * gate

    tile_rows(block, blocks, wide_ref, out_ref.at[0])
    out_ref[1] = out_ref[0]


def pack_input_kernel(experts, capacity, routes_ref, x_ref, after, out_ref, wide_ref):
    masks = slot_masks(routes_ref[...], experts, capacity)
    both = functools.reduce(lambda a, b: a + b, masks).astype(BF)
    blocks = x_ref.shape[0]
    tile_rows(
        lambda f: jnp.dot(both, x_ref[f], preferred_element_type=F32),
        blocks,
        wide_ref,
        out_ref,
    )


def tie_kernel(x_ref, *rest):
    pass


class Loads:
    def __init__(self, refs, buffer, sems):
        self.buffer = buffer
        self.copies = [
            pltpu.make_async_copy(ref, buffer.at[i], sems.at[i]) for i, ref in enumerate(refs)
        ]
        for copy in self.copies:
            copy.start()

    def __getitem__(self, i):
        self.copies[i].wait()
        block = self.buffer[i]
        return block.reshape(-1, block.shape[-1])


def columns(ref, index, width):
    return ref.at[:, pl.ds(pl.multiple_of(index * width, LANES), width)]


def dact_first_kernel(place_ref, c, down, out_ref, wide, lhs, buffer, sems):
    core = place_ref[0] & 1
    width = lhs.shape[1]
    w = Loads([columns(down, core + 2 * j, width) for j in range(2)], buffer, sems)
    untile_rows(c.at[0], width // LANES, wide, lhs)
    out_ref[...] = nt(lhs[...], w[0])
    untile_rows(c.at[1], width // LANES, wide, lhs)
    out_ref[...] += nt(lhs[...], w[1])


def dact_last_kernel(place_ref, c, part, down, out_ref, wide, lhs, buffer, sems):
    core = 1 - (place_ref[0] & 1)
    width = lhs.shape[1]
    w = Loads([columns(down, core + 2 * j, width) for j in range(2)], buffer, sems)
    untile_rows(c.at[0], width // LANES, wide, lhs)
    out_ref[...] = part[...] + nt(lhs[...], w[0])
    untile_rows(c.at[1], width // LANES, wide, lhs)
    out_ref[...] += nt(lhs[...], w[1])


def pre_first_kernel(place_ref, x0, x1, gate, up, g_ref, u_ref, wide, lhs, buffer, sems):
    ep = place_ref[0]
    w = Loads([gate.at[:, ep], up.at[:, ep], gate.at[:, ep ^ 1], up.at[:, ep ^ 1]], buffer, sems)
    blocks = lhs.shape[1] // LANES
    untile_rows(x0, blocks, wide, lhs)
    g_ref[...] = jnp.dot(lhs[...], w[0], preferred_element_type=F32)
    u_ref[...] = jnp.dot(lhs[...], w[1], preferred_element_type=F32)
    untile_rows(x1, blocks, wide, lhs)
    g_ref[...] += jnp.dot(lhs[...], w[2], preferred_element_type=F32)
    u_ref[...] += jnp.dot(lhs[...], w[3], preferred_element_type=F32)


def pre_next_kernel(place_ref, x2, g_in, u_in, gate, up, g_ref, u_ref, wide, lhs, buffer, sems):
    ep = place_ref[0]
    w = Loads([gate.at[:, ep ^ 2], up.at[:, ep ^ 2]], buffer, sems)
    untile_rows(x2, lhs.shape[1] // LANES, wide, lhs)
    g_ref[...] = g_in[...] + jnp.dot(lhs[...], w[0], preferred_element_type=F32)
    u_ref[...] = u_in[...] + jnp.dot(lhs[...], w[1], preferred_element_type=F32)


def forward_kernel(
    place_ref, x3, g_in, u_in, gate, up, down,
    act_ref, silu_ref, dsilu_ref, send_ref, wide, lhs, buffer, down_buffer, sems, down_sems,
):
    ep = place_ref[0]
    width = lhs.shape[1]
    w = Loads([gate.at[:, ep ^ 3], up.at[:, ep ^ 3]], buffer, sems)
    w_down = Loads([columns(down, ep ^ 3, width)], down_buffer, down_sems)
    untile_rows(x3, width // LANES, wide, lhs)
    pre_gate = g_in[...] + jnp.dot(lhs[...], w[0], preferred_element_type=F32)
    pre_up = u_in[...] + jnp.dot(lhs[...], w[1], preferred_element_type=F32)
    sigmoid = jax.nn.sigmoid(pre_gate)
    silu = pre_gate * sigmoid
    silu_ref[...] = silu
    dsilu_ref[...] = pre_up * sigmoid * (1.0 + pre_gate * (1.0 - sigmoid))
    act_ref[...] = (silu * pre_up).astype(BF)
    send_ref[...] = jnp.dot(act_ref[...], w_down[0], preferred_element_type=F32).astype(BF)


def keep_kernel(place_ref, act_ref, down, keep_ref, buffer, sems):
    w = Loads([columns(down, place_ref[0] ^ 2, keep_ref.shape[1])], buffer, sems)
    keep_ref[...] = jnp.dot(act_ref[...], w[0], preferred_element_type=F32)


def grad_kernel(
    place_ref, dact_ref, silu_ref, dsilu_ref, gate, up,
    dgate_ref, dup_ref, send_ref, keep_ref, buffer, sems,
):
    ep = place_ref[0]
    w = Loads([gate.at[ep ^ 3], up.at[ep ^ 3], gate.at[ep ^ 2], up.at[ep ^ 2]], buffer, sems)
    d_act = dact_ref[...]
    dgate_ref[...] = (d_act * dsilu_ref[...]).astype(BF)
    dup_ref[...] = (d_act * silu_ref[...]).astype(BF)
    send_ref[...] = (nt(dgate_ref[...], w[0]) + nt(dup_ref[...], w[1])).astype(BF)
    keep_ref[...] = nt(dgate_ref[...], w[2]) + nt(dup_ref[...], w[3])


def own_out_kernel(place_ref, act_ref, down, send_ref, keep_ref, buffer, sems):
    ep = place_ref[0]
    width = send_ref.shape[1]
    w = Loads([columns(down, ep ^ 1, width), columns(down, ep, width)], buffer, sems)
    send_ref[...] = jnp.dot(act_ref[...], w[0], preferred_element_type=F32).astype(BF)
    keep_ref[...] = jnp.dot(act_ref[...], w[1], preferred_element_type=F32)


def own_grad_kernel(place_ref, dgate_ref, dup_ref, gate, up, send_ref, keep_ref, buffer, sems):
    ep = place_ref[0]
    w = Loads([gate.at[ep ^ 1], up.at[ep ^ 1], gate.at[ep], up.at[ep]], buffer, sems)
    send_ref[...] = (nt(dgate_ref[...], w[0]) + nt(dup_ref[...], w[1])).astype(BF)
    keep_ref[...] = nt(dgate_ref[...], w[2]) + nt(dup_ref[...], w[3])


def chip_sum_kernel(keep_ref, came_ref, after, out_ref):
    out_ref[...] = (keep_ref[...] + came_ref[...].astype(F32)).astype(BF)


def finish_kernel(keep_ref, near_ref, far_ref, after, out_ref, wide_ref):
    def block(f):
        cols = slice(f * LANES, (f + 1) * LANES)
        return keep_ref[:, cols] + near_ref[:, cols].astype(F32) + far_ref[:, cols].astype(F32)

    tile_rows(block, keep_ref.shape[1] // LANES, wide_ref, out_ref)


def combine_out_kernel(
    experts, capacity, routes_ref, gates_ref, cot_ref, rows_ref, out_ref, grad_ref, wide, lhs
):
    masks = slot_masks(routes_ref[...], experts, capacity)
    untile_rows(rows_ref, lhs.shape[1] // LANES, wide, lhs)
    cot = cot_ref[...].astype(F32)
    total = None
    grads = []
    for k, m in enumerate(masks):
        picked = tn(m.astype(BF), lhs[...])
        term = gates_ref[:, k : k + 1] * picked
        total = term if total is None else total + term
        grads.append(jnp.sum(cot * picked, axis=1, keepdims=True))
    out_ref[...] = total.astype(BF)
    grad_ref[...] = jnp.concatenate(grads, axis=1)


def combine_grad_kernel(experts, capacity, routes_ref, rows_ref, out_ref, wide, lhs):
    masks = slot_masks(routes_ref[...], experts, capacity)
    both = functools.reduce(lambda a, b: a + b, masks).astype(BF)
    untile_rows(rows_ref, lhs.shape[1] // LANES, wide, lhs)
    out_ref[...] = tn(both, lhs[...]).astype(BF)


SMEM = pl.BlockSpec(memory_space=pltpu.SMEM)
VMEM = pl.BlockSpec(memory_space=pltpu.VMEM)
ANY = pl.BlockSpec(memory_space=pl.ANY)
HBM = pl.BlockSpec(memory_space=pltpu.HBM)


def call(kernel, specs, outs, scratch, flops, moved, *operands):
    single = not isinstance(outs, (list, tuple))
    return pl.pallas_call(
        kernel,
        out_shape=outs,
        in_specs=specs,
        out_specs=VMEM if single else [VMEM] * len(outs),
        scratch_shapes=scratch,
        compiler_params=pltpu.CompilerParams(vmem_limit_bytes=VMEM_BYTES),
        cost_estimate=pl.CostEstimate(flops=flops, bytes_accessed=moved, transcendentals=0),
    )(*operands)


def tie(x, *after):
    return pl.pallas_call(
        tie_kernel,
        out_shape=jax.ShapeDtypeStruct(x.shape, x.dtype),
        in_specs=[ANY] * (1 + len(after)),
        out_specs=ANY,
        input_output_aliases={0: 0},
    )(x, *after)


def local(layer_input, output_cot, routes, gate_values, gate_weight, up_weight, down_weight):
    tokens, picks = routes.shape
    experts = lax.axis_size(("cp", "tp"))
    tp = lax.axis_size("tp")
    ep_size = lax.axis_size("ep")
    capacity = max(2, tokens * picks * 5 // (4 * experts))
    slots = experts * capacity
    width = output_cot.shape[1]
    blocks = width // LANES
    hidden = gate_weight.shape[2]
    tiled = slots * blocks
    place = lax.axis_index("ep").astype(jnp.int32).reshape(1)
    routes_t = routes.T
    gates_t = gate_values.T
    down_w = down_weight[0]
    gate_x = gate_weight.reshape(tp, ep_size, LANES, hidden)
    up_x = up_weight.reshape(tp, ep_size, LANES, hidden)
    gate_q = gate_weight.reshape(ep_size, width, hidden)
    up_q = up_weight.reshape(ep_size, width, hidden)
    shape = jax.ShapeDtypeStruct
    wide = pltpu.VMEM((tiled, LANES), F32)
    lhs = pltpu.VMEM((slots, width), BF)
    near = [(i, i ^ 1) for i in range(ep_size)]
    far = [(i, i ^ 2) for i in range(ep_size)]

    def exchange(rows):
        return lax.all_to_all(
            rows.reshape(experts, capacity * blocks, LANES),
            ("cp", "tp"),
            split_axis=0,
            concat_axis=0,
            tiled=True,
        ).reshape(tiled, LANES)

    moved = slots * width * 6
    dot_flops = 2 * slots * width * hidden
    acc = shape((slots, hidden), F32)
    send_t = shape((slots, width), BF)
    keep_t = shape((slots, width), F32)
    hid = shape((slots, hidden), BF)
    rows_t = shape((tiled, LANES), BF)

    quarter_x = lambda n: [
        pltpu.VMEM((n, tp, LANES, hidden), BF), pltpu.SemaphoreType.DMA((n,))
    ]
    quarter_q = lambda n: [pltpu.VMEM((n, width, hidden), BF), pltpu.SemaphoreType.DMA((n,))]
    quarter_d = lambda n: [pltpu.VMEM((n, hidden, width), BF), pltpu.SemaphoreType.DMA((n,))]

    x_cols = lax.all_to_all(
        layer_input.reshape(tp, tokens, LANES), "tp", split_axis=0, concat_axis=0, tiled=True
    )
    cot_rows = call(
        functools.partial(pack_cot_kernel, experts, capacity),
        [VMEM] * 3, shape((2, tiled, LANES), BF), [wide], 10**8, moved,
        routes_t, gates_t, output_cot,
    )
    x_rows = call(
        functools.partial(pack_input_kernel, experts, capacity),
        [VMEM] * 2 + [ANY], rows_t, [wide], 10**8, moved, routes_t, x_cols, cot_rows,
    )
    x0 = exchange(x_rows)
    x1 = lax.ppermute(x0, "ep", near)
    x2 = lax.ppermute(x0, "ep", far)
    chips = experts // tp
    groups = [
        [(z * tp + t) * ep_size + half * 2 + core
         for half in range(2) for z in range(chips) for t in range(tp)]
        for core in range(2)
    ]
    cot_here = lax.all_to_all(
        cot_rows.reshape(2 * experts, capacity * blocks, LANES),
        ("cp", "tp", "ep"), split_axis=0, concat_axis=0, tiled=True, axis_index_groups=groups,
    ).reshape(2, tiled, LANES)
    pre = call(
        pre_first_kernel, [SMEM] + [VMEM] * 2 + [HBM] * 2, [acc, acc],
        [wide, lhs, *quarter_x(4)], 4 * dot_flops, moved, place, x0, x1, gate_x, up_x,
    )
    x2 = tie(x2, *pre)
    x3 = lax.ppermute(x2, "ep", near)
    pre = call(
        pre_next_kernel, [SMEM] + [VMEM] * 3 + [HBM] * 2, [acc, acc],
        [wide, lhs, *quarter_x(2)], LONG, moved, place, x2, *pre, gate_x, up_x,
    )
    x_buf, x_sem = quarter_x(2)
    d_buf, d_sem = quarter_d(1)
    act, silu, dsilu, out_send = call(
        forward_kernel, [SMEM] + [VMEM] * 3 + [HBM] * 3, [hid, acc, acc, send_t],
        [wide, lhs, x_buf, d_buf, x_sem, d_sem],
        LONG, moved, place, x3, *pre, gate_x, up_x, down_w,
    )
    out_came = lax.ppermute(out_send, "ep", near)
    out_keep = call(
        keep_kernel, [SMEM, VMEM, HBM], keep_t, quarter_d(1), dot_flops, moved,
        place, act, down_w,
    )
    out_sum = call(
        chip_sum_kernel, [VMEM] * 2 + [ANY], send_t, [], 10**6, moved, out_keep, out_came, act
    )
    out_far = lax.ppermute(out_sum, "ep", far)
    out_send2, out_keep2 = call(
        own_out_kernel, [SMEM, VMEM, HBM], [send_t, keep_t], quarter_d(2),
        2 * dot_flops, moved, place, act, down_w,
    )
    cot_here = tie(cot_here, out_sum, out_keep2)
    cot_there = lax.ppermute(cot_here, "ep", near)
    d_part = call(
        dact_first_kernel, [SMEM, VMEM, HBM], acc, [wide, lhs, *quarter_d(2)],
        2 * dot_flops, moved, place, cot_here, down_w,
    )
    d_act = call(
        dact_last_kernel, [SMEM, VMEM, VMEM, HBM], acc, [wide, lhs, *quarter_d(2)],
        2 * dot_flops, moved, place, cot_there, d_part, down_w,
    )
    d_gate, d_up, grad_send, grad_keep = call(
        grad_kernel, [SMEM] + [VMEM] * 3 + [HBM] * 2, [hid, hid, send_t, keep_t], quarter_q(4),
        4 * dot_flops, moved, place, d_act, silu, dsilu, gate_q, up_q,
    )
    grad_came = lax.ppermute(grad_send, "ep", near)
    out_near = lax.ppermute(out_send2, "ep", near)
    grad_send2, grad_keep2 = call(
        own_grad_kernel, [SMEM] + [VMEM] * 2 + [HBM] * 2, [send_t, keep_t], quarter_q(4),
        4 * dot_flops, moved, place, d_gate, d_up, gate_q, up_q,
    )
    grad_near = lax.ppermute(grad_send2, "ep", near)
    grad_sum = call(
        chip_sum_kernel, [VMEM] * 2 + [ANY], send_t, [], 10**6, moved,
        grad_keep, grad_came, out_far,
    )
    grad_far = lax.ppermute(grad_sum, "ep", far)
    out_rows = call(
        finish_kernel, [VMEM] * 3 + [ANY], rows_t, [wide], 10**6, moved,
        out_keep2, out_near, out_far, grad_sum,
    )
    out_back = exchange(out_rows)
    grad_rows = call(
        finish_kernel, [VMEM] * 3 + [ANY], rows_t, [wide], LONG, moved,
        grad_keep2, grad_near, grad_far, out_rows,
    )
    grad_back = exchange(grad_rows)
    moe_output, gate_grad = call(
        functools.partial(combine_out_kernel, experts, capacity), [VMEM] * 4,
        [shape((tokens, width), BF), shape((tokens, picks), F32)], [wide, lhs], 10**8, moved,
        routes_t, gate_values, output_cot, out_back,
    )
    gate_grad = gate_grad + lax.ppermute(gate_grad, "ep", near)
    gate_grad = gate_grad + lax.ppermute(gate_grad, "ep", far)
    input_grad = call(
        functools.partial(combine_grad_kernel, experts, capacity), [VMEM] * 2,
        shape((tokens, width), BF), [wide, lhs], 10**8, moved,
        routes_t, grad_back,
    )
    return (moe_output, input_grad, gate_grad)


def solution(mesh):
    placed = (
        P("cp", ("tp", "ep")),
        P(("cp", "tp"), "ep"),
        P(("cp", "tp"), None),
        P(("cp", "tp"), None),
        P(("cp", "tp"), None, "ep"),
        P(("cp", "tp"), None, "ep"),
        P(("cp", "tp"), "ep", None),
    )
    return jax.shard_map(
        local,
        mesh=mesh,
        in_specs=placed,
        out_specs=(P(("cp", "tp"), "ep"), P(("cp", "tp"), "ep"), P(("cp", "tp"), None)),
        check_vma=False,
    )
```

time: 189 us -> 167 us (0.88)
  waiting for transfers between devices: 91.3 us -> 50.5 us
  blocking collectives: 12.5 us -> 29.9 us
  starting transfers between devices: 46 us -> 37 us
  local copies, waits for them, and re-layouts: 9.64 us -> 15.4 us
  Pallas kernels: 27.2 us -> 32.1 us
    ppermute x10 -> x8, waiting for transfers between devices: 57.2 us -> 24.5 us  [the longest x1 12.3 us: local(): grad_far = lax.ppermute(grad_sum, 'ep', far)]
    all_to_all x4 -> x2, starting transfers between devices: 37.8 us -> 11.5 us  [exchange(): lax.all_to_all(rows.reshape(experts, capacity * blocks, LANES), ('cp', 't...]
    all_to_all x4 -> x2, waiting for transfers between devices: 32.8 us -> 13.4 us  [exchange(): lax.all_to_all(rows.reshape(experts, capacity * blocks, LANES), ('cp', 't...]
    all_to_all x1, blocking collectives: 12.5 us -> 29.9 us  [exchange(): lax.all_to_all(rows.reshape(experts, capacity * blocks, LANES), ('cp', 't...]
    all_to_all x0 -> x2, starting transfers between devices: none -> 14.8 us  [the longest x1 9.68 us: local(): lax.all_to_all(cot_rows.reshape(2 * experts, capacity * blocks, LANES), (...]
    all_to_all x0 -> x2, waiting for transfers between devices: none -> 5.81 us  [the longest x1 4.24 us: local(): lax.all_to_all(layer_input.reshape(tp, tokens, LANES), 'tp', split_axis=0...]
    unnamed x38 -> x58, local copies, waits for them, and re-layouts: 9.64 us -> 15.4 us
    ppermute x1, waiting for transfers between devices: 0.01 us -> 5.47 us  [local(): gate_grad = gate_grad + lax.ppermute(gate_grad, 'ep', far)]
  transfers between devices with their start and end apart: 18 -> 16, of which waited for: 7 -> 9; matrix products, arithmetic and copies ran while one was open for 0% -> 0% of each run, Pallas kernels for 14% -> 18%
where the time goes in v2:
time: 167 us; the launch traced here: 166 us
  waiting for transfers between devices  50.5 us (30%)
  starting transfers between devices  37 us (22%)
  Pallas kernels  32.1 us (19%)
  blocking collectives  29.9 us (18%)
  local copies, waits for them, and re-layouts  15.4 us (9%)
    pallas_call x17, Pallas kernels, call(): pl.pallas_call(kernel, out_shape=outs, in_specs=specs, out_specs=VMEM if...  32.1 us
    all_to_all x1, blocking collectives, exchange(): lax.all_to_all(rows.reshape(experts, capacity * blocks, LANES), ('cp', 't...  29.9 us
    unnamed x58, local copies, waits for them, and re-layouts  15.4 us
    all_to_all x2, waiting for transfers between devices, exchange(): lax.all_to_all(rows.reshape(experts, capacity * blocks, LANES), ('cp', 't...  13.4 us
    ppermute x1, waiting for transfers between devices, local(): grad_far = lax.ppermute(grad_sum, 'ep', far)  12.3 us
    all_to_all x2, starting transfers between devices, exchange(): lax.all_to_all(rows.reshape(experts, capacity * blocks, LANES), ('cp', 't...  11.5 us
    all_to_all x1, starting transfers between devices, local(): lax.all_to_all(cot_rows.reshape(2 * experts, capacity * blocks, LANES), (...  9.68 us
    ppermute x1, waiting for transfers between devices, local(): x2 = lax.ppermute(x0, 'ep', far)  7.65 us
  transfers between devices with their start and end apart: 16, of which 9 were waited for; matrix products, arithmetic and copies ran while one was open for 0% of the time, Pallas kernels for 18%

profile of v2, /device:TPU:4, one launch (start us, length us, event | category | flops | bytes accessed | tf_op | source)
XLA Modules:
  0.0 165.8 jit_solution(18021635720682239602)
XLA Ops:
  0.6 0.0 copy-start.22
  0.6 5.1 %all-to-all-start = ((bf16[8,128,128]{2,1,0:T(8,128)(2,1)}), bf16[8,128,128]{2,1,0:T(8,128)(2,1)S(1)}, u32[]{:S(2)}, u32[]{:S(2)}) async-start(bf16[8,128,128]{2,1,0:T(8,128)(2,1)} %bitcast.40), calls=%async_computation | async-start | bytes 524288 | tf_op jit(solution)/shard_map/all_to_all | solution.py:331
  5.8 0.9 copy-done.11
  6.7 0.7 copy-done.21
  7.4 0.7 copy-done.24
  8.1 0.7 shard_map.94.after
  8.7 4.2 %all-to-all-done.x_ref = bf16[8,128,128]{2,1,0:T(8,128)(2,1)S(1)} async-done(((bf16[8,128,128]{2,1,0:T(8,128)(2,1)}), bf16[8,128,128]{2,1,0:T(8,128)(2,1)S(1)}, u32[]{:S(2)}, u32[]{:S(2)}) %all-to-all-start) | async-done | bytes 262176 | tf_op jit(solution)/shard_map/all_to_all | solution.py:331
  13.0 0.6 shard_map.95
  13.6 0.0 copy-start.1
  13.6 29.9 %all_to_all.25 = bf16[64,40,128]{2,1,0:T(8,128)(2,1)} all-to-all(bf16[64,40,128]{2,1,0:T(8,128)(2,1)S(1)} %bitcast.34), channel_id=1, replica_groups=mesh['cp'=8,'tp'=8,'ep'=4] {'cp','tp'}, dimensions={0} | all-to-all | bytes 1310720 | tf_op jit(solution)/shard_map/all_to_all | solution.py:309
  43.5 0.0 collective-permute-start.1
  43.5 0.8 collective-permute-start
  44.3 9.7 %all-to-all-start.2 = ((bf16[128,40,128]{2,1,0:T(8,128)(2,1)}), bf16[128,40,128]{2,1,0:T(8,128)(2,1)}, u32[]{:S(2)}, u32[]{:S(2)}) async-start(bf16[128,40,128]{2,1,0:T(8,128)(2,1)} %bitcast.32), calls=%async_computation.2 | async-start | bytes 2621440 | tf_op jit(solution)/shard_map/all_to_all | solution.py:352
  54.0 0.0 copy-start.4
  54.0 1.9 %copy-done.4 = bf16[1,4096,384]{2,1,0:T(8,128)(2,1)S(1)} copy-done((bf16[1,4096,384]{2,1,0:T(8,128)(2,1)S(1)}, bf16[1,4096,384]{2,1,0:T(8,128)(2,1)}, u32[]{:S(2)}) %copy-start.4) | copy-done | bytes 3145752
  55.9 4.2 %shard_map.96 = (f32[320,384]{1,0:T(8,128)S(1)}, f32[320,384]{1,0:T(8,128)S(1)}) custom-call(s32[1]{0:T(128)} %bitcast.1.place_ref, bf16[2560,128]{1,0:T(8,128)(2,1)} %bitcast.5.x0, bf16[2560,128]{1,0:T(8,128)(2,1)} %collective-permute-done.1.x1, bf16[8,4,128,384]{3,2,1,0:T(8,128)(2,1)S(1)} %bitcast.22, bf16[8,4,128,384]{3,2,1,0:T(8,128)(2,1)S(1)} %bitcast.27), custom_call_target="tpu_custom_call" | custom-call | flops 1006632960 | bytes 1966080 | tf_op jit(solution)/shard_map/pallas_call | solution.py:262
  60.2 0.8 copy-done.13
  61.0 0.8 copy-done.15
  61.8 7.6 %collective-permute-done.x_ref = bf16[2560,128]{1,0:T(8,128)(2,1)} collective-permute-done((bf16[2560,128]{1,0:T(8,128)(2,1)}, bf16[2560,128]{1,0:T(8,128)(2,1)}, u32[]{:S(2)}, u32[]{:S(2)}) %collective-permute-start) | collective-permute-done | bytes 655392 | tf_op jit(solution)/shard_map/ppermute | solution.py:345
  69.4 1.9 %copy-done.2 = bf16[1,4096,384]{2,1,0:T(8,128)(2,1)S(1)} copy-done((bf16[1,4096,384]{2,1,0:T(8,128)(2,1)S(1)}, bf16[1,4096,384]{2,1,0:T(8,128)(2,1)}, u32[]{:S(2)}) %copy-start.2) | copy-done | bytes 3145752
  71.3 1.9 %copy-done.5 = bf16[1,4096,384]{2,1,0:T(8,128)(2,1)S(1)} copy-done((bf16[1,4096,384]{2,1,0:T(8,128)(2,1)S(1)}, bf16[1,4096,384]{2,1,0:T(8,128)(2,1)}, u32[]{:S(2)}) %copy-start.5) | copy-done | bytes 3145752
  73.2 1.0 copy-done.14
  74.2 1.0 copy-done.16
  75.3 2.9 %shard_map.98 = (f32[320,384]{1,0:T(8,128)S(1)}, f32[320,384]{1,0:T(8,128)S(1)}) custom-call(s32[1]{0:T(128)} %bitcast.1.place_ref, bf16[2560,128]{1,0:T(8,128)(2,1)} %shard_map.97.x2, f32[320,384]{1,0:T(8,128)S(1)} %copy-done.14, f32[320,384]{1,0:T(8,128)S(1)} %copy-done.16, bf16[8,4,128,384]{3,2,1,0:T(8,128)(2,1)S(1)} %bitcast.23, ...), custom_call_target="tpu_custom_call" | custom-call | flops 199999995904 | bytes 1966080 | tf_op jit(solution)/shard_map/pallas_call | solution.py:262
  78.2 0.0 collective-permute-done.2.x3
  78.2 3.5 %shard_map.99 = (bf16[320,384]{1,0:T(8,128)(2,1)S(1)}, f32[320,384]{1,0:T(8,128)S(1)}, f32[320,384]{1,0:T(8,128)S(1)}, bf16[320,1024]{1,0:T(8,128)(2,1)S(1)}) custom-call(s32[1]{0:T(128)} %bitcast.1.place_ref, bf16[2560,128]{1,0:T(8,128)(2,1)} %collective-permute-done.2.x3, f32[320,384]{1,0:T(8,128)S(1)} %get-tuple-element.23.g_in, ...), custom_call_target="tpu_custom_call" | custom-call | flops 199999995904 | bytes 1966080 | tf_op jit(solution)/shard_map/pallas_call | solution.py:262
  81.7 0.8 collective-permute-start.4
  82.4 0.6 shard_map.101.keep_ref
  83.1 1.2 shard_map.100
  84.3 1.1 copy-done.8
  85.4 0.9 copy-done.26
  86.2 0.0 collective-permute-done.4.came_ref
  86.2 0.1 shard_map.102.rest_0_
  86.3 0.9 copy-done.10
  87.2 1.6 all-to-all-done.2
  88.8 3.3 %collective-permute-start.5 = (bf16[320,1024]{1,0:T(8,128)(2,1)}, bf16[320,1024]{1,0:T(8,128)(2,1)S(1)}, u32[]{:S(2)}, u32[]{:S(2)}) collective-permute-start(bf16[320,1024]{1,0:T(8,128)(2,1)} %copy-done.10), channel_id=1, source_target_pairs={{0,2},{1,3},{2,0},{3,1},{4,6},{5,7},{6,4},{7,5},{8,10},{9,11},{10,... | collective-permute-start | bytes 1966088 | tf_op jit(solution)/shard_map/ppermute | solution.py:381
  92.1 3.4 %shard_map.104.part = f32[320,384]{1,0:T(8,128)S(1)} custom-call(s32[1]{0:T(128)} %bitcast.1.place_ref, bf16[2,2560,128]{2,1,0:T(8,128)(2,1)} %shard_map.103.c, bf16[384,4096]{1,0:T(8,128)(2,1)S(1)} %bitcast.20), custom_call_target="tpu_custom_call" | custom-call | flops 503316480 | bytes 1966080 | tf_op jit(solution)/shard_map/pallas_call | solution.py:262
  95.5 0.0 collective-permute-done.6.c
  95.5 0.0 copy-start.3
  95.5 2.0 %shard_map.105.dact_ref = f32[320,384]{1,0:T(8,128)S(1)} custom-call(s32[1]{0:T(128)} %bitcast.1.place_ref, bf16[2,2560,128]{2,1,0:T(8,128)(2,1)S(1)} %collective-permute-done.6.c, f32[320,384]{1,0:T(8,128)S(1)} %shard_map.104.part, bf16[384,4096]{1,0:T(8,128)(2,1)S(1)} %bitcast.21), custom_call_target="tpu_custom_call" | custom-call | flops 503316480 | bytes 1966080 | tf_op jit(solution)/shard_map/pallas_call | solution.py:262
  97.6 0.1 copy-done.3
  97.7 2.3 %shard_map.106 = (bf16[320,384]{1,0:T(8,128)(2,1)S(1)}, bf16[320,384]{1,0:T(8,128)(2,1)S(1)}, bf16[320,1024]{1,0:T(8,128)(2,1)S(1)}, f32[320,1024]{1,0:T(8,128)S(1)}) custom-call(s32[1]{0:T(128)} %bitcast.1.place_ref, f32[320,384]{1,0:T(8,128)S(1)} %shard_map.105.dact_ref, f32[320,384]{1,0:T(8,128)S(1)} %copy-done.18, f32[320,384]{1,0:T(8,128)S(1)} %copy-done.20, ...), custom_call_target="tpu_custom_call" | custom-call | flops 1006632960 | bytes 1966080 | tf_op jit(solution)/shard_map/pallas_call | solution.py:262
  100.0 0.3 collective-permute-start.7
  100.4 0.3 collective-permute-start.3
  100.6 2.2 %shard_map.110 = (bf16[320,1024]{1,0:T(8,128)(2,1)S(1)}, f32[320,1024]{1,0:T(8,128)S(1)}) custom-call(s32[1]{0:T(128)} %bitcast.1.place_ref, bf16[320,384]{1,0:T(8,128)(2,1)S(1)} %get-tuple-element.34.dgate_ref, bf16[320,384]{1,0:T(8,128)(2,1)S(1)} %get-tuple-element.35.dup_ref, bf16[4,1024,384]{2,1,0:T(8,128)(2,1)S(1)} %bitcast.26, ...), custom_call_target="tpu_custom_call" | custom-call | flops 1006632960 | bytes 1966080 | tf_op jit(solution)/shard_map/pallas_call | solution.py:262
  102.8 0.3 collective-permute-start.8
  103.2 4.5 %collective-permute-done.5.after.far_ref = bf16[320,1024]{1,0:T(8,128)(2,1)S(1)} collective-permute-done((bf16[320,1024]{1,0:T(8,128)(2,1)}, bf16[320,1024]{1,0:T(8,128)(2,1)S(1)}, u32[]{:S(2)}, u32[]{:S(2)}) %collective-permute-start.5) | collective-permute-done | bytes 655392 | tf_op jit(solution)/shard_map/ppermute | solution.py:381
  107.7 0.0 collective-permute-done.7.came_ref
  107.7 0.1 shard_map.107.after
  107.8 3.3 %collective-permute-start.9 = (bf16[320,1024]{1,0:T(8,128)(2,1)S(1)}, bf16[320,1024]{1,0:T(8,128)(2,1)}, u32[]{:S(2)}, u32[]{:S(2)}) collective-permute-start(bf16[320,1024]{1,0:T(8,128)(2,1)S(1)} %shard_map.107.after), channel_id=1, source_target_pairs={{0,2},{1,3},{2,0},{3,1},{4,6},{5,7},{6,4},{7,5},{8,10},{9,11},{10,... | collective-permute-start | bytes 1966088 | tf_op jit(solution)/shard_map/ppermute | solution.py:411
  111.2 1.6 shard_map.108.after
  112.8 5.7 %all-to-all-start.3 = ((bf16[64,40,128]{2,1,0:T(8,128)(2,1)}), bf16[64,40,128]{2,1,0:T(8,128)(2,1)}, u32[]{:S(2)}, u32[]{:S(2)}) async-start(bf16[64,40,128]{2,1,0:T(8,128)(2,1)} %bitcast.13), calls=%async_computation.3 | async-start | bytes 1310720 | tf_op jit(solution)/shard_map/all_to_all | solution.py:309
  118.5 12.3 %collective-permute-done.9.far_ref = bf16[320,1024]{1,0:T(8,128)(2,1)} collective-permute-done((bf16[320,1024]{1,0:T(8,128)(2,1)S(1)}, bf16[320,1024]{1,0:T(8,128)(2,1)}, u32[]{:S(2)}, u32[]{:S(2)}) %collective-permute-start.9) | collective-permute-done | bytes 655392 | tf_op jit(solution)/shard_map/ppermute | solution.py:411
  130.8 2.7 %shard_map.111 = bf16[2560,128]{1,0:T(8,128)(2,1)} custom-call(f32[320,1024]{1,0:T(8,128)S(1)} %get-tuple-element.36.keep_ref, bf16[320,1024]{1,0:T(8,128)(2,1)S(1)} %collective-permute-done.8.near_ref, bf16[320,1024]{1,0:T(8,128)(2,1)} %collective-permute-done.9.far_ref, bf16[2560,128]{1,0:T(8,128)(2,1)} %shard_map.108.after), custom_call_target="tpu_custom_call" | custom-call | flops 199999995904 | bytes 1966080 | tf_op jit(solution)/shard_map/pallas_call | solution.py:262
  133.5 5.2 %all-to-all-done.3 = bf16[64,40,128]{2,1,0:T(8,128)(2,1)} async-done(((bf16[64,40,128]{2,1,0:T(8,128)(2,1)}), bf16[64,40,128]{2,1,0:T(8,128)(2,1)}, u32[]{:S(2)}, u32[]{:S(2)}) %all-to-all-start.3) | async-done | bytes 655392 | tf_op jit(solution)/shard_map/all_to_all | solution.py:309
  138.7 5.9 %all-to-all-start.4 = ((bf16[64,40,128]{2,1,0:T(8,128)(2,1)}), bf16[64,40,128]{2,1,0:T(8,128)(2,1)S(1)}, u32[]{:S(2)}, u32[]{:S(2)}) async-start(bf16[64,40,128]{2,1,0:T(8,128)(2,1)} %bitcast.15), calls=%async_computation.4 | async-start | bytes 1310720 | tf_op jit(solution)/shard_map/all_to_all | solution.py:309
  144.6 0.1 copy.12.gates_ref
  144.7 2.7 %shard_map.109 = (bf16[128,1024]{1,0:T(8,128)(2,1)}, f32[128,2]{1,0:T(8,128)S(1)}) custom-call(s32[2,128]{1,0:T(2,128)S(1)} %bitcast.37, f32[128,2]{1,0:T(8,128)S(1)} %copy.12.gates_ref, bf16[128,1024]{1,0:T(8,128)(2,1)S(1)} %copy-done.12, bf16[2560,128]{1,0:T(8,128)(2,1)} %bitcast.14.rows_ref), custom_call_target="tpu_custom_call" | custom-call | flops 100000000 | bytes 1966080 | tf_op jit(solution)/shard_map/pallas_call | solution.py:262
  147.4 1.3 collective-permute-done.10
  148.7 1.5 collective-permute-start.11
  150.2 5.5 %collective-permute-done.11 = f32[128,2]{1,0:T(8,128)S(1)} collective-permute-done((f32[128,2]{1,0:T(8,128)S(1)}, f32[128,2]{1,0:T(8,128)S(1)}, u32[]{:S(2)}, u32[]{:S(2)}) %collective-permute-start.11) | collective-permute-done | bytes 1056 | tf_op jit(solution)/shard_map/ppermute | solution.py:428
  155.6 0.6 copy.13
  156.3 8.1 %all-to-all-done.4 = bf16[64,40,128]{2,1,0:T(8,128)(2,1)S(1)} async-done(((bf16[64,40,128]{2,1,0:T(8,128)(2,1)}), bf16[64,40,128]{2,1,0:T(8,128)(2,1)S(1)}, u32[]{:S(2)}, u32[]{:S(2)}) %all-to-all-start.4) | async-done | bytes 655392 | tf_op jit(solution)/shard_map/all_to_all | solution.py:309
  164.4 1.4 shard_map.112
  (48 shorter events, 0.1 us)
Async XLA Ops:
  0.6 12.4 %copy-start.22 = (s32[128,2]{0,1:T(2,128)S(1)}, s32[128,2]{0,1:T(2,128)}, u32[]{:S(2)}) copy-start(s32[128,2]{0,1:T(2,128)} %param.9) | copy-start | bytes 3076
  0.6 12.3 %all-to-all-start = ((bf16[8,128,128]{2,1,0:T(8,128)(2,1)}), bf16[8,128,128]{2,1,0:T(8,128)(2,1)S(1)}, u32[]{:S(2)}, u32[]{:S(2)}) async-start(bf16[8,128,128]{2,1,0:T(8,128)(2,1)} %bitcast.40), calls=%async_computation | async-start | bytes 524288 | tf_op jit(solution)/shard_map/all_to_all | solution.py:331
  5.8 0.9 copy-start.11
  6.7 0.7 copy-start.21
  7.4 0.7 copy-start.24
  8.7 4.9 %copy-start.7 = (bf16[2,2560,128]{2,1,0:T(8,128)(2,1)}, bf16[2,2560,128]{2,1,0:T(8,128)(2,1)S(1)}, u32[]{:S(2)}) copy-start(bf16[2,2560,128]{2,1,0:T(8,128)(2,1)S(1)} %shard_map.94.after) | copy-start | bytes 3932164
  13.6 40.4 %copy-start.1 = (bf16[1,4096,384]{2,1,0:T(8,128)(2,1)S(1)}, bf16[1,4096,384]{2,1,0:T(8,128)(2,1)}, u32[]{:S(2)}) copy-start(bf16[1,4096,384]{2,1,0:T(8,128)(2,1)} %param.11) | copy-start | bytes 9437188
  43.5 10.5 %collective-permute-start.1 = (bf16[2560,128]{1,0:T(8,128)(2,1)}, bf16[2560,128]{1,0:T(8,128)(2,1)}, u32[]{:S(2)}, u32[]{:S(2)}) collective-permute-start(bf16[2560,128]{1,0:T(8,128)(2,1)} %bitcast.5.x0), channel_id=1, source_target_pairs={{0,1},{1,0},{2,3},{3,2},{4,5},{5,4},{6,7},{7,6},{8,9},{9,8},{10,11... | collective-permute-start | bytes 1966088 | tf_op jit(solution)/shard_map/ppermute | solution.py:344
  43.5 25.9 %collective-permute-start = (bf16[2560,128]{1,0:T(8,128)(2,1)}, bf16[2560,128]{1,0:T(8,128)(2,1)}, u32[]{:S(2)}, u32[]{:S(2)}) collective-permute-start(bf16[2560,128]{1,0:T(8,128)(2,1)} %bitcast.5.x0), channel_id=1, source_target_pairs={{0,2},{1,3},{2,0},{3,1},{4,6},{5,7},{6,4},{7,5},{8,10},{9,11},{10,... | collective-permute-start | bytes 1966088 | tf_op jit(solution)/shard_map/ppermute | solution.py:345
  44.3 44.5 %all-to-all-start.2 = ((bf16[128,40,128]{2,1,0:T(8,128)(2,1)}), bf16[128,40,128]{2,1,0:T(8,128)(2,1)}, u32[]{:S(2)}, u32[]{:S(2)}) async-start(bf16[128,40,128]{2,1,0:T(8,128)(2,1)} %bitcast.32), calls=%async_computation.2 | async-start | bytes 2621440 | tf_op jit(solution)/shard_map/all_to_all | solution.py:352
  54.0 1.9 %copy-start.4 = (bf16[1,4096,384]{2,1,0:T(8,128)(2,1)S(1)}, bf16[1,4096,384]{2,1,0:T(8,128)(2,1)}, u32[]{:S(2)}) copy-start(bf16[1,4096,384]{2,1,0:T(8,128)(2,1)} %param.12) | copy-start | bytes 9437188
  60.2 0.8 copy-start.13
  61.0 0.8 copy-start.15
  69.4 8.7 %collective-permute-start.2 = (bf16[2560,128]{1,0:T(8,128)(2,1)}, bf16[2560,128]{1,0:T(8,128)(2,1)}, u32[]{:S(2)}, u32[]{:S(2)}) collective-permute-start(bf16[2560,128]{1,0:T(8,128)(2,1)} %shard_map.97.x2), channel_id=1, source_target_pairs={{0,1},{1,0},{2,3},{3,2},{4,5},{5,4},{6,7},{7,6},{8,9},{9,8},{10,11... | collective-permute-start | bytes 1966088 | tf_op jit(solution)/shard_map/ppermute | solution.py:361
  69.4 1.9 %copy-start.2 = (bf16[1,4096,384]{2,1,0:T(8,128)(2,1)S(1)}, bf16[1,4096,384]{2,1,0:T(8,128)(2,1)}, u32[]{:S(2)}) copy-start(bf16[1,4096,384]{2,1,0:T(8,128)(2,1)} %param.11) | copy-start | bytes 9437188
  71.3 1.9 %copy-start.5 = (bf16[1,4096,384]{2,1,0:T(8,128)(2,1)S(1)}, bf16[1,4096,384]{2,1,0:T(8,128)(2,1)}, u32[]{:S(2)}) copy-start(bf16[1,4096,384]{2,1,0:T(8,128)(2,1)} %param.12) | copy-start | bytes 9437188
  73.2 1.0 copy-start.14
  74.2 1.0 copy-start.16
  75.3 2.9 %copy-start = (bf16[1,384,4096]{2,1,0:T(8,128)(2,1)S(1)}, bf16[1,384,4096]{2,1,0:T(8,128)(2,1)}, u32[]{:S(2)}) copy-start(bf16[1,384,4096]{2,1,0:T(8,128)(2,1)} %param.13) | copy-start | bytes 9437188
  81.6 1.4 copy-start.17
  81.7 1.4 copy-start.19
  81.7 4.5 %collective-permute-start.4 = (bf16[320,1024]{1,0:T(8,128)(2,1)S(1)}, bf16[320,1024]{1,0:T(8,128)(2,1)S(1)}, u32[]{:S(2)}, u32[]{:S(2)}) collective-permute-start(bf16[320,1024]{1,0:T(8,128)(2,1)S(1)} %get-tuple-element.28), channel_id=1, source_target_pairs={{0,1},{1,0},{2,3},{3,2},{4,5},{5,4},{6,7},{7,6},{8,9},{9,8},{10,11... | collective-permute-start | bytes 1966088 | tf_op jit(solution)/shard_map/ppermute | solution.py:373
  84.3 1.1 copy-start.8
  85.4 0.9 copy-start.26
  86.3 0.9 copy-start.10
  88.8 6.8 %collective-permute-start.6 = (bf16[2,2560,128]{2,1,0:T(8,128)(2,1)}, bf16[2,2560,128]{2,1,0:T(8,128)(2,1)S(1)}, u32[]{:S(2)}, u32[]{:S(2)}) collective-permute-start(bf16[2,2560,128]{2,1,0:T(8,128)(2,1)} %shard_map.103.c), channel_id=1, source_target_pairs={{0,1},{1,0},{2,3},{3,2},{4,5},{5,4},{6,7},{7,6},{8,9},{9,8},{10,11... | collective-permute-start | bytes 3932168 | tf_op jit(solution)/shard_map/ppermute | solution.py:387
  88.8 19.0 %collective-permute-start.5 = (bf16[320,1024]{1,0:T(8,128)(2,1)}, bf16[320,1024]{1,0:T(8,128)(2,1)S(1)}, u32[]{:S(2)}, u32[]{:S(2)}) collective-permute-start(bf16[320,1024]{1,0:T(8,128)(2,1)} %copy-done.10), channel_id=1, source_target_pairs={{0,2},{1,3},{2,0},{3,1},{4,6},{5,7},{6,4},{7,5},{8,10},{9,11},{10,... | collective-permute-start | bytes 1966088 | tf_op jit(solution)/shard_map/ppermute | solution.py:381
  92.1 5.4 %copy-start.6 = (bf16[1,4096,384]{2,1,0:T(8,128)(2,1)S(1)}, bf16[1,4096,384]{2,1,0:T(8,128)(2,1)}, u32[]{:S(2)}) copy-start(bf16[1,4096,384]{2,1,0:T(8,128)(2,1)} %param.12) | copy-start | bytes 9437188
  95.5 2.1 %copy-start.18 = (f32[320,384]{1,0:T(8,128)S(1)}, f32[320,384]{1,0:T(8,128)}, u32[]{:S(2)}) copy-start(f32[320,384]{1,0:T(8,128)} %copy-done.17) | copy-start | bytes 1474564
  95.5 2.1 %copy-start.20 = (f32[320,384]{1,0:T(8,128)S(1)}, f32[320,384]{1,0:T(8,128)}, u32[]{:S(2)}) copy-start(f32[320,384]{1,0:T(8,128)} %copy-done.19) | copy-start | bytes 1474564
  95.5 2.2 %copy-start.3 = (bf16[1,4096,384]{2,1,0:T(8,128)(2,1)S(1)}, bf16[1,4096,384]{2,1,0:T(8,128)(2,1)}, u32[]{:S(2)}) copy-start(bf16[1,4096,384]{2,1,0:T(8,128)(2,1)} %param.11) | copy-start | bytes 9437188
  97.7 2.6 %copy-start.27 = (bf16[320,1024]{1,0:T(8,128)(2,1)S(1)}, bf16[320,1024]{1,0:T(8,128)(2,1)}, u32[]{:S(2)}) copy-start(bf16[320,1024]{1,0:T(8,128)(2,1)} %copy-done.26) | copy-start | bytes 1966084
  100.0 7.7 %collective-permute-start.7 = (bf16[320,1024]{1,0:T(8,128)(2,1)S(1)}, bf16[320,1024]{1,0:T(8,128)(2,1)S(1)}, u32[]{:S(2)}, u32[]{:S(2)}) collective-permute-start(bf16[320,1024]{1,0:T(8,128)(2,1)S(1)} %get-tuple-element.32), channel_id=1, source_target_pairs={{0,1},{1,0},{2,3},{3,2},{4,5},{5,4},{6,7},{7,6},{8,9},{9,8},{10,11... | collective-permute-start | bytes 1966088 | tf_op jit(solution)/shard_map/ppermute | solution.py:400
  100.4 10.8 %collective-permute-start.3 = (bf16[320,1024]{1,0:T(8,128)(2,1)S(1)}, bf16[320,1024]{1,0:T(8,128)(2,1)S(1)}, u32[]{:S(2)}, u32[]{:S(2)}) collective-permute-start(bf16[320,1024]{1,0:T(8,128)(2,1)S(1)} %copy-done.27), channel_id=1, source_target_pairs={{0,1},{1,0},{2,3},{3,2},{4,5},{5,4},{6,7},{7,6},{8,9},{9,8},{10,11... | collective-permute-start | bytes 1966088 | tf_op jit(solution)/shard_map/ppermute | solution.py:401
  102.8 15.6 %collective-permute-start.8 = (bf16[320,1024]{1,0:T(8,128)(2,1)S(1)}, bf16[320,1024]{1,0:T(8,128)(2,1)S(1)}, u32[]{:S(2)}, u32[]{:S(2)}) collective-permute-start(bf16[320,1024]{1,0:T(8,128)(2,1)S(1)} %get-tuple-element.37), channel_id=1, source_target_pairs={{0,1},{1,0},{2,3},{3,2},{4,5},{5,4},{6,7},{7,6},{8,9},{9,8},{10,11... | collective-permute-start | bytes 1966088 | tf_op jit(solution)/shard_map/ppermute | solution.py:406
  107.7 3.5 %copy-start.9 = (f32[320,1024]{1,0:T(8,128)S(1)}, f32[320,1024]{1,0:T(8,128)}, u32[]{:S(2)}) copy-start(f32[320,1024]{1,0:T(8,128)} %copy-done.8) | copy-start | bytes 3932164
  107.8 23.0 %collective-permute-start.9 = (bf16[320,1024]{1,0:T(8,128)(2,1)S(1)}, bf16[320,1024]{1,0:T(8,128)(2,1)}, u32[]{:S(2)}, u32[]{:S(2)}) collective-permute-start(bf16[320,1024]{1,0:T(8,128)(2,1)S(1)} %shard_map.107.after), channel_id=1, source_target_pairs={{0,2},{1,3},{2,0},{3,1},{4,6},{5,7},{6,4},{7,5},{8,10},{9,11},{10,... | collective-permute-start | bytes 1966088 | tf_op jit(solution)/shard_map/ppermute | solution.py:411
  112.8 25.9 %all-to-all-start.3 = ((bf16[64,40,128]{2,1,0:T(8,128)(2,1)}), bf16[64,40,128]{2,1,0:T(8,128)(2,1)}, u32[]{:S(2)}, u32[]{:S(2)}) async-start(bf16[64,40,128]{2,1,0:T(8,128)(2,1)} %bitcast.13), calls=%async_computation.3 | async-start | bytes 1310720 | tf_op jit(solution)/shard_map/all_to_all | solution.py:309
  133.5 11.1 %copy-start.25 = (f32[128,2]{0,1:T(2,128)S(1)}, f32[128,2]{0,1:T(2,128)}, u32[]{:S(2)}) copy-start(f32[128,2]{0,1:T(2,128)} %param.10) | copy-start | bytes 3076
  133.5 11.2 %copy-start.12 = (bf16[128,1024]{1,0:T(8,128)(2,1)S(1)}, bf16[128,1024]{1,0:T(8,128)(2,1)}, u32[]{:S(2)}) copy-start(bf16[128,1024]{1,0:T(8,128)(2,1)} %cot_ref.3) | copy-start | bytes 786436
  133.5 11.2 %copy-start.23 = (s32[128,2]{0,1:T(2,128)S(1)}, s32[128,2]{0,1:T(2,128)}, u32[]{:S(2)}) copy-start(s32[128,2]{0,1:T(2,128)} %param.9) | copy-start | bytes 3076
  138.7 25.7 %all-to-all-start.4 = ((bf16[64,40,128]{2,1,0:T(8,128)(2,1)}), bf16[64,40,128]{2,1,0:T(8,128)(2,1)S(1)}, u32[]{:S(2)}, u32[]{:S(2)}) async-start(bf16[64,40,128]{2,1,0:T(8,128)(2,1)} %bitcast.15), calls=%async_computation.4 | async-start | bytes 1310720 | tf_op jit(solution)/shard_map/all_to_all | solution.py:309
  147.4 1.3 collective-permute-start.10
  148.7 6.9 %collective-permute-start.11 = (f32[128,2]{1,0:T(8,128)S(1)}, f32[128,2]{1,0:T(8,128)S(1)}, u32[]{:S(2)}, u32[]{:S(2)}) collective-permute-start(f32[128,2]{1,0:T(8,128)S(1)} %add.6), channel_id=1, source_target_pairs={{0,2},{1,3},{2,0},{3,1},{4,6},{5,7},{6,4},{7,5},{8,10},{9,11},{10,... | collective-permute-start | bytes 3080 | tf_op jit(solution)/shard_map/ppermute | solution.py:428

commit v3 on v2

v3 whole, which is shorter than its diff:
```python
import functools

import jax
import jax.numpy as jnp
from jax import lax
from jax.experimental import pallas as pl
from jax.experimental.pallas import tpu as pltpu
from jax.sharding import PartitionSpec as P

BF = jnp.bfloat16
F32 = jnp.float32
LANES = 128
VMEM_BYTES = 20 * 1024 * 1024
RELAY = 4
SUMS = 2
LONG = 2 * 10**11


def nt(left, right):
    return lax.dot_general(
        left, right, (((1,), (1,)), ((), ())), preferred_element_type=F32
    )


def tn(left, right):
    return lax.dot_general(
        left, right, (((0,), (0,)), ((), ())), preferred_element_type=F32
    )


def slot_masks(routes, experts, capacity):
    picks, tokens = routes.shape
    expert = lax.broadcasted_iota(jnp.int32, (experts, tokens), 0)
    earlier = (
        lax.broadcasted_iota(jnp.int32, (tokens, tokens), 0)
        < lax.broadcasted_iota(jnp.int32, (tokens, tokens), 1)
    ).astype(F32).astype(BF)
    slot = lax.broadcasted_iota(jnp.int32, (experts * capacity, tokens), 0)
    taken = jnp.zeros((experts, 1), F32)
    masks = []
    for k in range(picks):
        named = routes[k : k + 1, :]
        chosen = (expert == named).astype(F32)
        before = jnp.dot(chosen.astype(BF), earlier, preferred_element_type=F32) + taken
        rank = jnp.sum(before * chosen, axis=0, keepdims=True)
        place = named * capacity + rank.astype(jnp.int32)
        masks.append((slot == place).astype(F32))
        taken = taken + jnp.sum(chosen, axis=1, keepdims=True)
    return masks


def tile_rows(values, blocks, wide_ref, out_ref):
    rows = wide_ref.shape[0] // blocks
    for f in range(blocks):
        wide_ref[pl.ds(f, rows, stride=blocks), :] = values(f)
    out_ref[...] = wide_ref[...].astype(BF)


def untile_rows(in_ref, blocks, wide_ref, out_ref):
    rows = wide_ref.shape[0] // blocks
    wide_ref[...] = in_ref[...].astype(F32)
    for f in range(blocks):
        out_ref[:, f * LANES : (f + 1) * LANES] = wide_ref[
            pl.ds(f, rows, stride=blocks), :
        ].astype(BF)


def pack_cot_kernel(
    experts, capacity, routes_ref, gates_ref, cot_ref, out_ref, token_ref, wide_ref
):
    masks = slot_masks(routes_ref[...], experts, capacity)
    both = functools.reduce(lambda a, b: a + b, masks)
    gate = functools.reduce(
        lambda a, b: a + b,
        [
            jnp.sum(m * gates_ref[k : k + 1, :], axis=1, keepdims=True)
            for k, m in enumerate(masks)
        ],
    )
    both = both.astype(BF)
    blocks = cot_ref.shape[1] // LANES

    def block(f):
        rows = jnp.dot(
            both, cot_ref[:, f * LANES : (f + 1) * LANES], preferred_element_type=F32
        )
        return rows * gate

    tile_rows(block, blocks, wide_ref, out_ref.at[0])
    out_ref[1] = out_ref[0]
    token_ref[...] = jnp.zeros_like(token_ref)


def pack_input_kernel(experts, capacity, routes_ref, x_ref, after, out_ref, wide_ref):
    masks = slot_masks(routes_ref[...], experts, capacity)
    both = functools.reduce(lambda a, b: a + b, masks).astype(BF)
    blocks = x_ref.shape[0]
    tile_rows(
        lambda f: jnp.dot(both, x_ref[f], preferred_element_type=F32),
        blocks,
        wide_ref,
        out_ref,
    )


def tie_kernel(x_ref, *rest):
    pass


def token_kernel(after, token_ref):
    token_ref[...] = jnp.zeros_like(token_ref)


def pieces_kernel(c, after, *outs):
    flat = c.shape[0] * c.shape[1] // len(outs)
    per = c.shape[1] // flat
    for i, out_ref in enumerate(outs):
        out_ref[...] = c[i // per, (i % per) * flat : (i % per + 1) * flat, :]


def untile_pieces(pieces, blocks, wide_ref, out_ref):
    at = 0
    for piece in pieces:
        wide_ref[at : at + piece.shape[0], :] = piece[...].astype(F32)
        at += piece.shape[0]
    rows = wide_ref.shape[0] // blocks
    for f in range(blocks):
        out_ref[:, f * LANES : (f + 1) * LANES] = wide_ref[
            pl.ds(f, rows, stride=blocks), :
        ].astype(BF)


def column_block(ref, index, width):
    return ref[:, pl.ds(pl.multiple_of(index * width, LANES), width)]


class Loads:
    def __init__(self, ref, indices, buffer, sems):
        width = buffer.shape[2]
        self.buffer = buffer
        self.copies = [
            pltpu.make_async_copy(
                ref.at[:, pl.ds(pl.multiple_of(index * width, LANES), width)],
                buffer.at[i],
                sems.at[i],
            )
            for i, index in enumerate(indices)
        ]
        for copy in self.copies:
            copy.start()

    def __getitem__(self, i):
        self.copies[i].wait()
        return self.buffer[i]


def dact_first_kernel(place_ref, *refs):
    *c, down, out_ref, wide, lhs, buffer, sems = refs
    core = place_ref[0] & 1
    w = Loads(down, (core, core + 2), buffer, sems)
    blocks = lhs.shape[1] // LANES
    half = len(c) // 2
    untile_pieces(c[:half], blocks, wide, lhs)
    out_ref[...] = nt(lhs[...], w[0])
    untile_pieces(c[half:], blocks, wide, lhs)
    out_ref[...] += nt(lhs[...], w[1])


def dact_last_kernel(place_ref, *refs):
    *c, part, down, out_ref, wide, lhs, buffer, sems = refs
    core = 1 - (place_ref[0] & 1)
    w = Loads(down, (core, core + 2), buffer, sems)
    blocks = lhs.shape[1] // LANES
    half = len(c) // 2
    untile_pieces(c[:half], blocks, wide, lhs)
    out_ref[...] = part[...] + nt(lhs[...], w[0])
    untile_pieces(c[half:], blocks, wide, lhs)
    out_ref[...] += nt(lhs[...], w[1])


def rows_block(ref, index, width):
    return ref[:, index].reshape(width, -1)


def pre_first_kernel(place_ref, x0, x1, gate, up, g_ref, u_ref, token_ref, wide, lhs):
    ep = place_ref[0]
    width = lhs.shape[1]
    untile_rows(x0, width // LANES, wide, lhs)
    g_ref[...] = jnp.dot(lhs[...], rows_block(gate, ep, width), preferred_element_type=F32)
    u_ref[...] = jnp.dot(lhs[...], rows_block(up, ep, width), preferred_element_type=F32)
    untile_rows(x1, width // LANES, wide, lhs)
    g_ref[...] += jnp.dot(lhs[...], rows_block(gate, ep ^ 1, width), preferred_element_type=F32)
    u_ref[...] += jnp.dot(lhs[...], rows_block(up, ep ^ 1, width), preferred_element_type=F32)
    token_ref[...] = jnp.zeros_like(token_ref)


def pre_next_kernel(place_ref, x2, g_in, u_in, gate, up, g_ref, u_ref, wide, lhs):
    ep = place_ref[0] ^ 2
    width = lhs.shape[1]
    untile_rows(x2, width // LANES, wide, lhs)
    g_ref[...] = g_in[...] + jnp.dot(
        lhs[...], rows_block(gate, ep, width), preferred_element_type=F32
    )
    u_ref[...] = u_in[...] + jnp.dot(
        lhs[...], rows_block(up, ep, width), preferred_element_type=F32
    )


def forward_kernel(
    place_ref, x3, g_in, u_in, gate, up, down,
    act_ref, silu_ref, dsilu_ref, send_ref, wide, lhs,
):
    ep = place_ref[0] ^ 3
    width = lhs.shape[1]
    untile_rows(x3, width // LANES, wide, lhs)
    pre_gate = g_in[...] + jnp.dot(
        lhs[...], rows_block(gate, ep, width), preferred_element_type=F32
    )
    pre_up = u_in[...] + jnp.dot(
        lhs[...], rows_block(up, ep, width), preferred_element_type=F32
    )
    sigmoid = jax.nn.sigmoid(pre_gate)
    silu = pre_gate * sigmoid
    silu_ref[...] = silu
    dsilu_ref[...] = pre_up * sigmoid * (1.0 + pre_gate * (1.0 - sigmoid))
    act_ref[...] = (silu * pre_up).astype(BF)
    send_ref[...] = jnp.dot(
        act_ref[...], column_block(down, ep, width), preferred_element_type=F32
    ).astype(BF)


def keep_kernel(place_ref, act_ref, down, keep_ref):
    keep_ref[...] = jnp.dot(
        act_ref[...],
        column_block(down, place_ref[0] ^ 2, keep_ref.shape[1]),
        preferred_element_type=F32,
    ).astype(BF)


def grad_block(dgate_ref, dup_ref, gate, up, index):
    return nt(dgate_ref[...], gate[index]) + nt(dup_ref[...], up[index])


def grad_kernel(
    place_ref, dact_ref, silu_ref, dsilu_ref, gate, up, dgate_ref, dup_ref, keep_ref, *sends
):
    ep = place_ref[0]
    d_act = dact_ref[...]
    dgate_ref[...] = (d_act * dsilu_ref[...]).astype(BF)
    dup_ref[...] = (d_act * silu_ref[...]).astype(BF)
    send = grad_block(dgate_ref, dup_ref, gate, up, ep ^ 3).astype(BF)
    for i, send_ref in enumerate(sends):
        part = send_ref.shape[1]
        send_ref[...] = send[:, i * part : (i + 1) * part]
    keep_ref[...] = grad_block(dgate_ref, dup_ref, gate, up, ep ^ 2).astype(BF)


def own_out_kernel(place_ref, act_ref, down, after, send_ref, keep_ref, token_ref):
    token_ref[...] = jnp.zeros_like(token_ref)
    ep = place_ref[0]
    width = send_ref.shape[1]
    send_ref[...] = jnp.dot(
        act_ref[...], column_block(down, ep ^ 1, width), preferred_element_type=F32
    ).astype(BF)
    keep_ref[...] = jnp.dot(
        act_ref[...], column_block(down, ep, width), preferred_element_type=F32
    ).astype(BF)


def own_grad_kernel(place_ref, dgate_ref, dup_ref, gate, up, after, send_ref, keep_ref):
    ep = place_ref[0]
    send_ref[...] = grad_block(dgate_ref, dup_ref, gate, up, ep ^ 1).astype(BF)
    keep_ref[...] = grad_block(dgate_ref, dup_ref, gate, up, ep).astype(BF)


def chip_sum_kernel(keep_ref, came_ref, after, out_ref, token_ref):
    token_ref[...] = jnp.zeros_like(token_ref)
    out_ref[...] = (keep_ref[...].astype(F32) + came_ref[...].astype(F32)).astype(BF)


def grad_sum_kernel(keep_ref, *refs):
    *came, after, out_ref, token_ref = refs
    token_ref[...] = jnp.zeros_like(token_ref)
    for i, ref in enumerate(came):
        cols = slice(i * ref.shape[1], (i + 1) * ref.shape[1])
        out_ref[:, cols] = (keep_ref[:, cols].astype(F32) + ref[...].astype(F32)).astype(BF)


def finish_kernel(keep_ref, near_ref, far_ref, after, out_ref, token_ref, wide_ref):
    token_ref[...] = jnp.zeros_like(token_ref)

    def block(f):
        cols = slice(f * LANES, (f + 1) * LANES)
        parts = [ref[:, cols].astype(F32) for ref in (keep_ref, near_ref, far_ref)]
        return parts[0] + parts[1] + parts[2]

    tile_rows(block, keep_ref.shape[1] // LANES, wide_ref, out_ref)


def combine_out_kernel(
    experts, capacity, routes_ref, gates_ref, cot_ref, rows_ref, out_ref, grad_ref, wide, lhs
):
    masks = slot_masks(routes_ref[...], experts, capacity)
    untile_rows(rows_ref, lhs.shape[1] // LANES, wide, lhs)
    cot = cot_ref[...].astype(F32)
    total = None
    grads = []
    for k, m in enumerate(masks):
        picked = tn(m.astype(BF), lhs[...])
        term = gates_ref[:, k : k + 1] * picked
        total = term if total is None else total + term
        grads.append(jnp.sum(cot * picked, axis=1, keepdims=True))
    out_ref[...] = total.astype(BF)
    grad_ref[...] = jnp.concatenate(grads, axis=1)


def combine_grad_kernel(experts, capacity, routes_ref, rows_ref, out_ref, wide, lhs):
    masks = slot_masks(routes_ref[...], experts, capacity)
    both = functools.reduce(lambda a, b: a + b, masks).astype(BF)
    untile_rows(rows_ref, lhs.shape[1] // LANES, wide, lhs)
    out_ref[...] = tn(both, lhs[...]).astype(BF)


SMEM = pl.BlockSpec(memory_space=pltpu.SMEM)
VMEM = pl.BlockSpec(memory_space=pltpu.VMEM)
ANY = pl.BlockSpec(memory_space=pl.ANY)
HBM = pl.BlockSpec(memory_space=pltpu.HBM)


def call(kernel, specs, outs, scratch, flops, moved, *operands):
    single = not isinstance(outs, (list, tuple))
    return pl.pallas_call(
        kernel,
        out_shape=outs,
        in_specs=specs,
        out_specs=VMEM if single else [VMEM] * len(outs),
        scratch_shapes=scratch,
        compiler_params=pltpu.CompilerParams(vmem_limit_bytes=VMEM_BYTES),
        cost_estimate=pl.CostEstimate(flops=flops, bytes_accessed=moved, transcendentals=0),
    )(*operands)


def tie(x, *after):
    return pl.pallas_call(
        tie_kernel,
        out_shape=jax.ShapeDtypeStruct(x.shape, x.dtype),
        in_specs=[ANY] * (1 + len(after)),
        out_specs=ANY,
        input_output_aliases={0: 0},
        compiler_params=pltpu.CompilerParams(vmem_limit_bytes=1024 * 1024),
    )(x, *after)


def local(layer_input, output_cot, routes, gate_values, gate_weight, up_weight, down_weight):
    tokens, picks = routes.shape
    experts = lax.axis_size(("cp", "tp"))
    tp = lax.axis_size("tp")
    ep_size = lax.axis_size("ep")
    capacity = max(2, tokens * picks * 5 // (4 * experts))
    slots = experts * capacity
    width = output_cot.shape[1]
    blocks = width // LANES
    hidden = gate_weight.shape[2]
    tiled = slots * blocks
    place = lax.axis_index("ep").astype(jnp.int32).reshape(1)
    routes_t = routes.T
    gates_t = gate_values.T
    down_w = down_weight[0]
    gate_x = gate_weight.reshape(tp, ep_size, LANES, hidden)
    up_x = up_weight.reshape(tp, ep_size, LANES, hidden)
    gate_q = gate_weight.reshape(ep_size, width, hidden)
    up_q = up_weight.reshape(ep_size, width, hidden)
    shape = jax.ShapeDtypeStruct
    wide = pltpu.VMEM((tiled, LANES), F32)
    lhs = pltpu.VMEM((slots, width), BF)
    near = [(i, i ^ 1) for i in range(ep_size)]
    far = [(i, i ^ 2) for i in range(ep_size)]

    def exchange(rows):
        return lax.all_to_all(
            rows.reshape(experts, capacity * blocks, LANES),
            ("cp", "tp"),
            split_axis=0,
            concat_axis=0,
            tiled=True,
        ).reshape(tiled, LANES)

    moved = slots * width * 6
    dot_flops = 2 * slots * width * hidden
    acc = shape((slots, hidden), F32)
    send_t = shape((slots, width), BF)
    keep_t = shape((slots, width), BF)
    hid = shape((slots, hidden), BF)
    rows_t = shape((tiled, LANES), BF)

    token = shape((8, LANES), F32)
    loads = [pltpu.VMEM((2, hidden, width), BF), pltpu.SemaphoreType.DMA((2,))]

    x_cols = lax.all_to_all(
        layer_input.reshape(tp, tokens, LANES), "tp", split_axis=0, concat_axis=0, tiled=True
    )
    cot_rows, cot_token = call(
        functools.partial(pack_cot_kernel, experts, capacity),
        [VMEM] * 3, [shape((2, tiled, LANES), BF), token], [wide], 10**8, moved,
        routes_t, gates_t, output_cot,
    )
    x_rows = call(
        functools.partial(pack_input_kernel, experts, capacity),
        [VMEM] * 3, rows_t, [wide], 10**8, moved, routes_t, x_cols, cot_token,
    )
    x0 = exchange(x_rows)
    x1 = lax.ppermute(x0, "ep", near)
    x2 = lax.ppermute(x0, "ep", far)
    chips = experts // tp
    groups = [
        [(z * tp + t) * ep_size + half * 2 + core
         for half in range(2) for z in range(chips) for t in range(tp)]
        for core in range(2)
    ]
    cot_here = lax.all_to_all(
        cot_rows.reshape(2 * experts, capacity * blocks, LANES),
        ("cp", "tp", "ep"), split_axis=0, concat_axis=0, tiled=True, axis_index_groups=groups,
    ).reshape(2, tiled, LANES)
    *pre, p_token = call(
        pre_first_kernel, [SMEM] + [VMEM] * 4, [acc, acc, token],
        [wide, lhs], 4 * dot_flops, moved, place, x0, x1, gate_x, up_x,
    )
    x2 = tie(x2, p_token)
    x3 = lax.ppermute(x2, "ep", near)
    pre = call(
        pre_next_kernel, [SMEM] + [VMEM] * 3 + [VMEM] * 2, [acc, acc],
        [wide, lhs], LONG, moved, place, x2, *pre, gate_x, up_x,
    )
    act, silu, dsilu, out_send = call(
        forward_kernel, [SMEM] + [VMEM] * 3 + [VMEM] * 3, [hid, acc, acc, send_t],
        [wide, lhs],
        LONG, moved, place, x3, *pre, gate_x, up_x, down_w,
    )
    out_came = lax.ppermute(out_send, "ep", near)
    out_keep = call(
        keep_kernel, [SMEM, VMEM, VMEM], keep_t, [], dot_flops, moved,
        place, act, down_w,
    )
    out_sum, out_token = call(
        chip_sum_kernel, [VMEM] * 2 + [ANY], [send_t, token], [], 10**6, moved,
        out_keep, out_came, p_token,
    )
    out_far = lax.ppermute(out_sum, "ep", far)
    out_send2, out_keep2, own_token = call(
        own_out_kernel, [SMEM, VMEM, VMEM, ANY], [send_t, keep_t, token], [],
        2 * dot_flops, moved, place, act, down_w, out_token,
    )
    cot_here = call(
        pieces_kernel, [VMEM, ANY], [shape((2 * tiled // RELAY, LANES), BF)] * RELAY, [],
        10**6, moved, cot_here, own_token,
    )
    cot_there = [lax.ppermute(piece, "ep", near) for piece in cot_here]
    d_part = call(
        dact_first_kernel, [SMEM] + [VMEM] * RELAY + [HBM], acc, [wide, lhs, *loads],
        2 * dot_flops, moved, place, *cot_here, down_w,
    )
    far_token = call(token_kernel, [ANY], token, [], LONG, 10**4, out_far)
    d_act = call(
        dact_last_kernel, [SMEM] + [VMEM] * (RELAY + 1) + [HBM], acc, [wide, lhs, *loads],
        2 * dot_flops, moved, place, *cot_there, d_part, down_w,
    )
    d_gate, d_up, grad_keep, *grad_sends = call(
        grad_kernel, [SMEM] + [VMEM] * 3 + [VMEM] * 2, [hid, hid, keep_t] + [shape((slots, width // SUMS), BF)] * SUMS, [],
        4 * dot_flops, moved, place, d_act, silu, dsilu, gate_q, up_q,
    )
    grad_came = [lax.ppermute(send, "ep", near) for send in grad_sends]
    out_near = lax.ppermute(out_send2, "ep", near)
    out_rows, rows_token = call(
        finish_kernel, [VMEM] * 3 + [ANY], [rows_t, token], [wide], 10**6, moved,
        out_keep2, out_near, out_far, far_token,
    )
    grad_sum, g_token = call(
        grad_sum_kernel, [VMEM] * (SUMS + 1) + [ANY], [send_t, token], [], 10**6, moved,
        grad_keep, *grad_came, rows_token,
    )
    grad_far = lax.ppermute(grad_sum, "ep", far)
    grad_send2, grad_keep2 = call(
        own_grad_kernel, [SMEM] + [VMEM] * 4 + [ANY], [send_t, keep_t], [],
        4 * dot_flops, moved, place, d_gate, d_up, gate_q, up_q, g_token,
    )
    grad_near = lax.ppermute(grad_send2, "ep", near)
    out_back = exchange(out_rows)
    last_token = call(token_kernel, [ANY], token, [], LONG, 10**4, grad_far)
    grad_rows, _ = call(
        finish_kernel, [VMEM] * 3 + [ANY], [rows_t, token], [wide], 10**6, moved,
        grad_keep2, grad_near, grad_far, last_token,
    )
    grad_back = exchange(grad_rows)
    moe_output, gate_grad = call(
        functools.partial(combine_out_kernel, experts, capacity), [VMEM] * 4,
        [shape((tokens, width), BF), shape((tokens, picks), F32)], [wide, lhs], 10**8, moved,
        routes_t, gate_values, output_cot, out_back,
    )
    gate_grad = gate_grad + lax.ppermute(gate_grad, "ep", near)
    gate_grad = gate_grad + lax.ppermute(gate_grad, "ep", far)
    input_grad = call(
        functools.partial(combine_grad_kernel, experts, capacity), [VMEM] * 2,
        shape((tokens, width), BF), [wide, lhs], 10**8, moved,
        routes_t, grad_back,
    )
    return (moe_output, input_grad, gate_grad)


def solution(mesh):
    placed = (
        P("cp", ("tp", "ep")),
        P(("cp", "tp"), "ep"),
        P(("cp", "tp"), None),
        P(("cp", "tp"), None),
        P(("cp", "tp"), None, "ep"),
        P(("cp", "tp"), None, "ep"),
        P(("cp", "tp"), "ep", None),
    )
    return jax.shard_map(
        local,
        mesh=mesh,
        in_specs=placed,
        out_specs=(P(("cp", "tp"), "ep"), P(("cp", "tp"), "ep"), P(("cp", "tp"), None)),
        check_vma=False,
    )
```

time: 167 us -> 165 us (0.988)
  starting transfers between devices: 37 us -> 34.2 us
  local copies, waits for them, and re-layouts: 15.4 us -> 13 us
  waiting for transfers between devices: 50.5 us -> 52.6 us
    all_to_all x1, waiting for transfers between devices: 1.56 us -> 8.98 us  [local(): lax.all_to_all(cot_rows.reshape(2 * experts, capacity * blocks, LANES), (...]
    ppermute x1, waiting for transfers between devices: 4.55 us -> 0.01 us  [local(): out_far = lax.ppermute(out_sum, 'ep', far)]
    all_to_all x2, waiting for transfers between devices: 13.4 us -> 9.8 us  [exchange(): lax.all_to_all(rows.reshape(experts, capacity * blocks, LANES), ('cp', 't...]
    ppermute x1, starting transfers between devices: 3.34 us -> 0.01 us  [local(): out_far = lax.ppermute(out_sum, 'ep', far)]
    ppermute x1, waiting for transfers between devices: 7.65 us -> 10.4 us  [local(): x2 = lax.ppermute(x0, 'ep', far)]
    unnamed x58 -> x54, local copies, waits for them, and re-layouts: 15.4 us -> 13 us
    pallas_call x17 -> x20, Pallas kernels: 32.1 us -> 32.6 us  [call(): pl.pallas_call(kernel, out_shape=outs, in_specs=specs, out_specs=VMEM if...]
  transfers between devices with their start and end apart: 16 -> 20, of which waited for: 9 -> 10; matrix products, arithmetic and copies ran while one was open for 0% -> 0% of each run, Pallas kernels for 18% -> 17%
where the time goes in v3:
time: 165 us; the launch traced here: 164 us
  waiting for transfers between devices  52.6 us (32%)
  starting transfers between devices  34.2 us (21%)
  Pallas kernels  32.6 us (20%)
  blocking collectives  30.2 us (18%)
  local copies, waits for them, and re-layouts  13 us (8%)
    pallas_call x20, Pallas kernels, call(): pl.pallas_call(kernel, out_shape=outs, in_specs=specs, out_specs=VMEM if...  32.6 us
    all_to_all x1, blocking collectives, exchange(): lax.all_to_all(rows.reshape(experts, capacity * blocks, LANES), ('cp', 't...  30.2 us
    unnamed x54, local copies, waits for them, and re-layouts  13 us
    ppermute x1, waiting for transfers between devices, local(): grad_far = lax.ppermute(grad_sum, 'ep', far)  11.6 us
    all_to_all x2, starting transfers between devices, exchange(): lax.all_to_all(rows.reshape(experts, capacity * blocks, LANES), ('cp', 't...  11.3 us
    ppermute x1, waiting for transfers between devices, local(): x2 = lax.ppermute(x0, 'ep', far)  10.4 us
    all_to_all x2, waiting for transfers between devices, exchange(): lax.all_to_all(rows.reshape(experts, capacity * blocks, LANES), ('cp', 't...  9.8 us
    all_to_all x1, starting transfers between devices, local(): lax.all_to_all(cot_rows.reshape(2 * experts, capacity * blocks, LANES), (...  9.67 us
  transfers between devices with their start and end apart: 20, of which 10 were waited for; matrix products, arithmetic and copies ran while one was open for 0% of the time, Pallas kernels for 17%

profile of v3, /device:TPU:4, one launch (start us, length us, event | category | flops | bytes accessed | tf_op | source)
XLA Modules:
  0.0 163.8 jit_solution(8388517349886268011)
XLA Ops:
  0.6 0.0 copy-start.1
  0.6 5.4 %all-to-all-start = ((bf16[8,128,128]{2,1,0:T(8,128)(2,1)}), bf16[8,128,128]{2,1,0:T(8,128)(2,1)S(1)}, u32[]{:S(2)}, u32[]{:S(2)}) async-start(bf16[8,128,128]{2,1,0:T(8,128)(2,1)} %bitcast.41), calls=%async_computation | async-start | bytes 524288 | tf_op jit(solution)/shard_map/all_to_all | solution.py:399
  6.0 0.9 copy-done.17
  7.0 0.7 copy-done.21
  7.7 0.7 copy-done.24
  8.3 0.6 shard_map.94
  9.0 1.1 copy-done.9
  10.1 3.2 %all-to-all-done.x_ref = bf16[8,128,128]{2,1,0:T(8,128)(2,1)S(1)} async-done(((bf16[8,128,128]{2,1,0:T(8,128)(2,1)}), bf16[8,128,128]{2,1,0:T(8,128)(2,1)S(1)}, u32[]{:S(2)}, u32[]{:S(2)}) %all-to-all-start) | async-done | bytes 262176 | tf_op jit(solution)/shard_map/all_to_all | solution.py:399
  13.2 0.7 copy-done.22
  13.9 0.6 shard_map.95
  14.5 30.2 %all_to_all.25 = bf16[64,40,128]{2,1,0:T(8,128)(2,1)} all-to-all(bf16[64,40,128]{2,1,0:T(8,128)(2,1)S(1)} %bitcast.33), channel_id=1, replica_groups=mesh['cp'=8,'tp'=8,'ep'=4] {'cp','tp'}, dimensions={0} | all-to-all | bytes 1310720 | tf_op jit(solution)/shard_map/all_to_all | solution.py:380
  44.7 0.8 collective-permute-start
  45.5 9.7 %all-to-all-start.3 = ((bf16[128,40,128]{2,1,0:T(8,128)(2,1)}), bf16[128,40,128]{2,1,0:T(8,128)(2,1)}, u32[]{:S(2)}, u32[]{:S(2)}) async-start(bf16[128,40,128]{2,1,0:T(8,128)(2,1)} %bitcast.34), calls=%async_computation.3 | async-start | bytes 2621440 | tf_op jit(solution)/shard_map/all_to_all | solution.py:420
  55.2 0.0 copy-start.5
  55.3 1.9 %copy-done.5 = bf16[1,4096,384]{2,1,0:T(8,128)(2,1)S(1)} copy-done((bf16[1,4096,384]{2,1,0:T(8,128)(2,1)S(1)}, bf16[1,4096,384]{2,1,0:T(8,128)(2,1)}, u32[]{:S(2)}) %copy-start.5) | copy-done | bytes 3145752
  57.1 3.1 %shard_map.96 = (f32[320,384]{1,0:T(8,128)S(1)}, f32[320,384]{1,0:T(8,128)S(1)}, f32[8,128]{1,0:T(8,128)S(1)}) custom-call(s32[1]{0:T(128)} %bitcast.1.place_ref, bf16[2560,128]{1,0:T(8,128)(2,1)} %bitcast.5.x0, bf16[2560,128]{1,0:T(8,128)(2,1)} %collective-permute-done.1.x1, bf16[8,4,128,384]{3,2,1,0:T(8,128)(2,1)S(1)} %bitcast.22, ...), custom_call_target="tpu_custom_call" | custom-call | flops 1006632960 | bytes 1966080 | tf_op jit(solution)/shard_map/pallas_call | solution.py:332
  60.3 10.4 %collective-permute-done.x_ref = bf16[2560,128]{1,0:T(8,128)(2,1)} collective-permute-done((bf16[2560,128]{1,0:T(8,128)(2,1)}, bf16[2560,128]{1,0:T(8,128)(2,1)}, u32[]{:S(2)}, u32[]{:S(2)}) %collective-permute-start) | collective-permute-done | bytes 655392 | tf_op jit(solution)/shard_map/ppermute | solution.py:413
  70.7 0.0 copy-start
  70.7 2.2 %shard_map.98 = (f32[320,384]{1,0:T(8,128)S(1)}, f32[320,384]{1,0:T(8,128)S(1)}) custom-call(s32[1]{0:T(128)} %bitcast.1.place_ref, bf16[2560,128]{1,0:T(8,128)(2,1)} %shard_map.97.x2, f32[320,384]{1,0:T(8,128)S(1)} %get-tuple-element.39.g_in, f32[320,384]{1,0:T(8,128)S(1)} %get-tuple-element.40.u_in, bf16[8,4,128,384]{3,2,1,0:T(8,128)(2,1)S(1)} %bitcast.23, ...), custom_call_target="tpu_custom_call" | custom-call | flops 199999995904 | bytes 1966080 | tf_op jit(solution)/shard_map/pallas_call | solution.py:332
  72.9 0.2 collective-permute-done.2.x3
  73.1 2.5 %shard_map.99 = (bf16[320,384]{1,0:T(8,128)(2,1)S(1)}, f32[320,384]{1,0:T(8,128)S(1)}, f32[320,384]{1,0:T(8,128)S(1)}, bf16[320,1024]{1,0:T(8,128)(2,1)S(1)}) custom-call(s32[1]{0:T(128)} %bitcast.1.place_ref, bf16[2560,128]{1,0:T(8,128)(2,1)} %collective-permute-done.2.x3, f32[320,384]{1,0:T(8,128)S(1)} %get-tuple-element.41.g_in, ...), custom_call_target="tpu_custom_call" | custom-call | flops 199999995904 | bytes 1966080 | tf_op jit(solution)/shard_map/pallas_call | solution.py:332
  75.7 0.4 collective-permute-start.3
  76.1 0.5 shard_map.100.keep_ref
  76.6 1.3 collective-permute-done.3.came_ref
  77.8 1.0 shard_map.101
  78.9 1.4 shard_map.102
  80.2 0.8 copy-done.11
  81.1 9.0 %all-to-all-done.3 = bf16[128,40,128]{2,1,0:T(8,128)(2,1)} async-done(((bf16[128,40,128]{2,1,0:T(8,128)(2,1)}), bf16[128,40,128]{2,1,0:T(8,128)(2,1)}, u32[]{:S(2)}, u32[]{:S(2)}) %all-to-all-start.3) | async-done | bytes 1310752 | tf_op jit(solution)/shard_map/all_to_all | solution.py:420
  90.0 1.4 shard_map.106
  91.4 0.3 collective-permute-start.6
  91.7 0.5 collective-permute-start.7
  92.2 0.1 collective-permute-start.8
  92.3 0.4 collective-permute-start.9
  92.7 1.9 %shard_map.107.refs_4_ = f32[320,384]{1,0:T(8,128)S(1)} custom-call(s32[1]{0:T(128)} %bitcast.1.place_ref, bf16[1280,128]{1,0:T(8,128)(2,1)S(1)} %get-tuple-element.53.refs_0_, bf16[1280,128]{1,0:T(8,128)(2,1)S(1)} %get-tuple-element.54.refs_1_, bf16[1280,128]{1,0:T(8,128)(2,1)S(1)} %get-tuple-element.55.refs_2_, ...), custom_call_target="tpu_custom_call" | custom-call | flops 503316480 | bytes 1966080 | tf_op jit(solution)/shard_map/pallas_call | solution.py:332
  94.7 0.0 copy-start.3
  94.7 0.2 collective-permute-start.4
  94.9 2.0 %shard_map.108.dact_ref = f32[320,384]{1,0:T(8,128)S(1)} custom-call(s32[1]{0:T(128)} %bitcast.1.place_ref, bf16[1280,128]{1,0:T(8,128)(2,1)S(1)} %collective-permute-done.6.refs_0_, bf16[1280,128]{1,0:T(8,128)(2,1)S(1)} %collective-permute-done.7.refs_1_, bf16[1280,128]{1,0:T(8,128)(2,1)S(1)} %collective-permute-done.8.refs_2_, ...), custom_call_target="tpu_custom_call" | custom-call | flops 503316480 | bytes 1966080 | tf_op jit(solution)/shard_map/pallas_call | solution.py:332
  97.0 2.1 %shard_map.109 = (bf16[320,384]{1,0:T(8,128)(2,1)S(1)}, bf16[320,384]{1,0:T(8,128)(2,1)S(1)}, bf16[320,1024]{1,0:T(8,128)(2,1)S(1)}, bf16[320,512]{1,0:T(8,128)(2,1)}, bf16[320,512]{1,0:T(8,128)(2,1)}) custom-call(s32[1]{0:T(128)} %bitcast.1.place_ref, f32[320,384]{1,0:T(8,128)S(1)} %shard_map.108.dact_ref, f32[320,384]{1,0:T(8,128)S(1)} %copy-done.14, ...), custom_call_target="tpu_custom_call" | custom-call | flops 1006632960 | bytes 1966080 | tf_op jit(solution)/shard_map/pallas_call | solution.py:332
  99.1 0.7 copy-done.19
  99.8 0.4 collective-permute-start.10
  100.2 0.1 collective-permute-start.11
  100.3 1.1 copy-done.12
  101.4 2.3 %shard_map.104 = (bf16[2560,128]{1,0:T(8,128)(2,1)S(1)}, f32[8,128]{1,0:T(8,128)S(1)}) custom-call(bf16[320,1024]{1,0:T(8,128)(2,1)S(1)} %copy-done.12, bf16[320,1024]{1,0:T(8,128)(2,1)} %collective-permute-done.4.near_ref, bf16[320,1024]{1,0:T(8,128)(2,1)} %collective-permute-done.5.after.far_ref, f32[8,128]{1,0:T(8,128)S(1)} %shard_map.103.after), custom_call_target="tpu_custom_call" | custom-call | flops 1000000 | bytes 1966080 | tf_op jit(solution)/shard_map/pallas_call | solution.py:332
  103.7 0.8 copy-done.10
  104.5 2.1 %shard_map.110 = (bf16[320,1024]{1,0:T(8,128)(2,1)}, f32[8,128]{1,0:T(8,128)S(1)}) custom-call(bf16[320,1024]{1,0:T(8,128)(2,1)S(1)} %get-tuple-element.61.keep_ref, bf16[320,512]{1,0:T(8,128)(2,1)} %collective-permute-done.10.refs_0_, bf16[320,512]{1,0:T(8,128)(2,1)} %collective-permute-done.11.refs_1_, f32[8,128]{1,0:T(8,128)S(1)} %get-tuple-element.64.refs_2_), custom_call_target="tpu_custom_call" | custom-call | flops 1000000 | bytes 1966080 | tf_op jit(solution)/shard_map/pallas_call | solution.py:332
  106.6 3.4 %collective-permute-start.13 = (bf16[320,1024]{1,0:T(8,128)(2,1)}, bf16[320,1024]{1,0:T(8,128)(2,1)}, u32[]{:S(2)}, u32[]{:S(2)}) collective-permute-start(bf16[320,1024]{1,0:T(8,128)(2,1)} %get-tuple-element.68), channel_id=1, source_target_pairs={{0,2},{1,3},{2,0},{3,1},{4,6},{5,7},{6,4},{7,5},{8,10},{9,11},{10,... | collective-permute-start | bytes 1966088 | tf_op jit(solution)/shard_map/ppermute | solution.py:481
  110.0 5.5 %all-to-all-start.2 = ((bf16[64,40,128]{2,1,0:T(8,128)(2,1)}), bf16[64,40,128]{2,1,0:T(8,128)(2,1)}, u32[]{:S(2)}, u32[]{:S(2)}) async-start(bf16[64,40,128]{2,1,0:T(8,128)(2,1)} %bitcast.35), calls=%async_computation.2 | async-start | bytes 1310720 | tf_op jit(solution)/shard_map/all_to_all | solution.py:380
  115.5 0.0 copy-start.8
  115.5 1.9 %copy-done.8 = bf16[1,4096,384]{2,1,0:T(8,128)(2,1)S(1)} copy-done((bf16[1,4096,384]{2,1,0:T(8,128)(2,1)S(1)}, bf16[1,4096,384]{2,1,0:T(8,128)(2,1)}, u32[]{:S(2)}) %copy-start.8) | copy-done | bytes 3145752
  117.4 0.9 copy-done.20
  118.3 1.7 %shard_map.111 = (bf16[320,1024]{1,0:T(8,128)(2,1)}, bf16[320,1024]{1,0:T(8,128)(2,1)S(1)}) custom-call(s32[1]{0:T(128)} %bitcast.1.place_ref, bf16[320,384]{1,0:T(8,128)(2,1)S(1)} %get-tuple-element.59.dgate_ref, bf16[320,384]{1,0:T(8,128)(2,1)S(1)} %copy-done.20, bf16[4,1024,384]{2,1,0:T(8,128)(2,1)S(1)} %bitcast.26, bf16[4,1024,384]{2,1,0:T(8,128)(2,1)S(1)} %bitcast.31, ...), custom_call_target="tpu_custom_call" | custom-call | flops 1006632960 | bytes 1966080 | tf_op jit(solution)/shard_map/pallas_call | solution.py:332
  120.1 0.3 collective-permute-start.12
  120.3 11.6 %collective-permute-done.13.after.far_ref = bf16[320,1024]{1,0:T(8,128)(2,1)} collective-permute-done((bf16[320,1024]{1,0:T(8,128)(2,1)}, bf16[320,1024]{1,0:T(8,128)(2,1)}, u32[]{:S(2)}, u32[]{:S(2)}) %collective-permute-start.13) | collective-permute-done | bytes 655392 | tf_op jit(solution)/shard_map/ppermute | solution.py:481
  132.0 3.1 %shard_map.113 = (bf16[2560,128]{1,0:T(8,128)(2,1)}, f32[8,128]{1,0:T(8,128)}) custom-call(bf16[320,1024]{1,0:T(8,128)(2,1)S(1)} %get-tuple-element.66.keep_ref, bf16[320,1024]{1,0:T(8,128)(2,1)} %collective-permute-done.12.near_ref, bf16[320,1024]{1,0:T(8,128)(2,1)} %collective-permute-done.13.after.far_ref, f32[8,128]{1,0:T(8,128)S(1)} %shard_map.112.after), custom_call_target="tpu_custom_call" | custom-call | flops 1000000 | bytes 1966080 | tf_op jit(solution)/shard_map/pallas_call | solution.py:332
  135.1 1.4 all-to-all-done.2
  136.4 5.9 %all-to-all-start.4 = ((bf16[64,40,128]{2,1,0:T(8,128)(2,1)}), bf16[64,40,128]{2,1,0:T(8,128)(2,1)S(1)}, u32[]{:S(2)}, u32[]{:S(2)}) async-start(bf16[64,40,128]{2,1,0:T(8,128)(2,1)} %bitcast.15), calls=%async_computation.4 | async-start | bytes 1310720 | tf_op jit(solution)/shard_map/all_to_all | solution.py:380
  142.3 0.1 copy.11.gates_ref
  142.4 2.7 %shard_map.105 = (bf16[128,1024]{1,0:T(8,128)(2,1)}, f32[128,2]{1,0:T(8,128)S(1)}) custom-call(s32[2,128]{1,0:T(2,128)S(1)} %bitcast.38, f32[128,2]{1,0:T(8,128)S(1)} %copy.11.gates_ref, bf16[128,1024]{1,0:T(8,128)(2,1)S(1)} %copy-done.18, bf16[2560,128]{1,0:T(8,128)(2,1)} %bitcast.10.rows_ref), custom_call_target="tpu_custom_call" | custom-call | flops 100000000 | bytes 1966080 | tf_op jit(solution)/shard_map/pallas_call | solution.py:332
  145.1 1.3 collective-permute-done.14
  146.4 0.9 collective-permute-start.15
  147.3 5.9 %collective-permute-done.15 = f32[128,2]{1,0:T(8,128)S(1)} collective-permute-done((f32[128,2]{1,0:T(8,128)S(1)}, f32[128,2]{1,0:T(8,128)S(1)}, u32[]{:S(2)}, u32[]{:S(2)}) %collective-permute-start.15) | collective-permute-done | bytes 1056 | tf_op jit(solution)/shard_map/ppermute | solution.py:500
  153.3 0.6 copy.12
  153.9 8.4 %all-to-all-done.4 = bf16[64,40,128]{2,1,0:T(8,128)(2,1)S(1)} async-done(((bf16[64,40,128]{2,1,0:T(8,128)(2,1)}), bf16[64,40,128]{2,1,0:T(8,128)(2,1)S(1)}, u32[]{:S(2)}, u32[]{:S(2)}) %all-to-all-start.4) | async-done | bytes 655392 | tf_op jit(solution)/shard_map/all_to_all | solution.py:380
  162.4 1.4 shard_map.114
  (54 shorter events, 0.1 us)
Async XLA Ops:
  0.6 54.6 %copy-start.1 = (bf16[1,4096,384]{2,1,0:T(8,128)(2,1)S(1)}, bf16[1,4096,384]{2,1,0:T(8,128)(2,1)}, u32[]{:S(2)}) copy-start(bf16[1,4096,384]{2,1,0:T(8,128)(2,1)} %param.11) | copy-start | bytes 9437188
  0.6 12.6 %all-to-all-start = ((bf16[8,128,128]{2,1,0:T(8,128)(2,1)}), bf16[8,128,128]{2,1,0:T(8,128)(2,1)S(1)}, u32[]{:S(2)}, u32[]{:S(2)}) async-start(bf16[8,128,128]{2,1,0:T(8,128)(2,1)} %bitcast.41), calls=%async_computation | async-start | bytes 524288 | tf_op jit(solution)/shard_map/all_to_all | solution.py:399
  6.0 0.9 copy-start.17
  7.0 0.7 copy-start.21
  7.7 0.7 copy-start.24
  9.0 1.1 copy-start.9
  13.2 0.7 copy-start.22
  44.7 10.5 %collective-permute-start.1 = (bf16[2560,128]{1,0:T(8,128)(2,1)}, bf16[2560,128]{1,0:T(8,128)(2,1)}, u32[]{:S(2)}, u32[]{:S(2)}) collective-permute-start(bf16[2560,128]{1,0:T(8,128)(2,1)} %bitcast.5.x0), channel_id=1, source_target_pairs={{0,1},{1,0},{2,3},{3,2},{4,5},{5,4},{6,7},{7,6},{8,9},{9,8},{10,11... | collective-permute-start | bytes 1966088 | tf_op jit(solution)/shard_map/ppermute | solution.py:412
  44.7 25.9 %collective-permute-start = (bf16[2560,128]{1,0:T(8,128)(2,1)}, bf16[2560,128]{1,0:T(8,128)(2,1)}, u32[]{:S(2)}, u32[]{:S(2)}) collective-permute-start(bf16[2560,128]{1,0:T(8,128)(2,1)} %bitcast.5.x0), channel_id=1, source_target_pairs={{0,2},{1,3},{2,0},{3,1},{4,6},{5,7},{6,4},{7,5},{8,10},{9,11},{10,... | collective-permute-start | bytes 1966088 | tf_op jit(solution)/shard_map/ppermute | solution.py:413
  45.5 44.5 %all-to-all-start.3 = ((bf16[128,40,128]{2,1,0:T(8,128)(2,1)}), bf16[128,40,128]{2,1,0:T(8,128)(2,1)}, u32[]{:S(2)}, u32[]{:S(2)}) async-start(bf16[128,40,128]{2,1,0:T(8,128)(2,1)} %bitcast.34), calls=%async_computation.3 | async-start | bytes 2621440 | tf_op jit(solution)/shard_map/all_to_all | solution.py:420
  55.2 1.9 %copy-start.5 = (bf16[1,4096,384]{2,1,0:T(8,128)(2,1)S(1)}, bf16[1,4096,384]{2,1,0:T(8,128)(2,1)}, u32[]{:S(2)}) copy-start(bf16[1,4096,384]{2,1,0:T(8,128)(2,1)} %param.12) | copy-start | bytes 9437188
  57.1 13.5 %copy-start.2 = (bf16[1,4096,384]{2,1,0:T(8,128)(2,1)S(1)}, bf16[1,4096,384]{2,1,0:T(8,128)(2,1)}, u32[]{:S(2)}) copy-start(bf16[1,4096,384]{2,1,0:T(8,128)(2,1)} %param.11) | copy-start | bytes 9437188
  57.1 13.5 %copy-start.6 = (bf16[1,4096,384]{2,1,0:T(8,128)(2,1)S(1)}, bf16[1,4096,384]{2,1,0:T(8,128)(2,1)}, u32[]{:S(2)}) copy-start(bf16[1,4096,384]{2,1,0:T(8,128)(2,1)} %param.12) | copy-start | bytes 9437188
  70.7 2.4 %collective-permute-start.2 = (bf16[2560,128]{1,0:T(8,128)(2,1)}, bf16[2560,128]{1,0:T(8,128)(2,1)}, u32[]{:S(2)}, u32[]{:S(2)}) collective-permute-start(bf16[2560,128]{1,0:T(8,128)(2,1)} %shard_map.97.x2), channel_id=1, source_target_pairs={{0,1},{1,0},{2,3},{3,2},{4,5},{5,4},{6,7},{7,6},{8,9},{9,8},{10,11... | collective-permute-start | bytes 1966088 | tf_op jit(solution)/shard_map/ppermute | solution.py:429
  70.7 2.4 %copy-start = (bf16[1,384,4096]{2,1,0:T(8,128)(2,1)S(1)}, bf16[1,384,4096]{2,1,0:T(8,128)(2,1)}, u32[]{:S(2)}) copy-start(bf16[1,384,4096]{2,1,0:T(8,128)(2,1)} %param.13) | copy-start | bytes 9437188
  75.6 3.2 %copy-start.13 = (f32[320,384]{1,0:T(8,128)}, f32[320,384]{1,0:T(8,128)S(1)}, u32[]{:S(2)}) copy-start(f32[320,384]{1,0:T(8,128)S(1)} %get-tuple-element.57.silu_ref) | copy-start | bytes 1474564
  75.6 3.2 %copy-start.15 = (f32[320,384]{1,0:T(8,128)}, f32[320,384]{1,0:T(8,128)S(1)}, u32[]{:S(2)}) copy-start(f32[320,384]{1,0:T(8,128)S(1)} %get-tuple-element.58.dsilu_ref) | copy-start | bytes 1474564
  75.7 2.2 %collective-permute-start.3 = (bf16[320,1024]{1,0:T(8,128)(2,1)S(1)}, bf16[320,1024]{1,0:T(8,128)(2,1)S(1)}, u32[]{:S(2)}, u32[]{:S(2)}) collective-permute-start(bf16[320,1024]{1,0:T(8,128)(2,1)S(1)} %get-tuple-element.44), channel_id=1, source_target_pairs={{0,1},{1,0},{2,3},{3,2},{4,5},{5,4},{6,7},{7,6},{8,9},{9,8},{10,11... | collective-permute-start | bytes 1966088 | tf_op jit(solution)/shard_map/ppermute | solution.py:439
  78.8 21.5 %collective-permute-start.5 = (bf16[320,1024]{1,0:T(8,128)(2,1)}, bf16[320,1024]{1,0:T(8,128)(2,1)}, u32[]{:S(2)}, u32[]{:S(2)}) collective-permute-start(bf16[320,1024]{1,0:T(8,128)(2,1)} %get-tuple-element.48), channel_id=1, source_target_pairs={{0,2},{1,3},{2,0},{3,1},{4,6},{5,7},{6,4},{7,5},{8,10},{9,11},{10,... | collective-permute-start | bytes 1966088 | tf_op jit(solution)/shard_map/ppermute | solution.py:448
  80.2 0.9 copy-start.11
  91.4 3.3 %collective-permute-start.6 = (bf16[1280,128]{1,0:T(8,128)(2,1)S(1)}, bf16[1280,128]{1,0:T(8,128)(2,1)S(1)}, u32[]{:S(2)}, u32[]{:S(2)}) collective-permute-start(bf16[1280,128]{1,0:T(8,128)(2,1)S(1)} %get-tuple-element.53.refs_0_), channel_id=1, source_target_pairs={{0,1},{1,0},{2,3},{3,2},{4,5},{5,4},{6,7},{7,6},{8,9},{9,8},{10,11... | collective-permute-start | bytes 983048 | tf_op jit(solution)/shard_map/ppermute | solution.py:457
  91.7 3.2 %collective-permute-start.7 = (bf16[1280,128]{1,0:T(8,128)(2,1)S(1)}, bf16[1280,128]{1,0:T(8,128)(2,1)S(1)}, u32[]{:S(2)}, u32[]{:S(2)}) collective-permute-start(bf16[1280,128]{1,0:T(8,128)(2,1)S(1)} %get-tuple-element.54.refs_1_), channel_id=1, source_target_pairs={{0,1},{1,0},{2,3},{3,2},{4,5},{5,4},{6,7},{7,6},{8,9},{9,8},{10,11... | collective-permute-start | bytes 983048 | tf_op jit(solution)/shard_map/ppermute | solution.py:457
  92.2 2.7 %collective-permute-start.8 = (bf16[1280,128]{1,0:T(8,128)(2,1)S(1)}, bf16[1280,128]{1,0:T(8,128)(2,1)S(1)}, u32[]{:S(2)}, u32[]{:S(2)}) collective-permute-start(bf16[1280,128]{1,0:T(8,128)(2,1)S(1)} %get-tuple-element.55.refs_2_), channel_id=1, source_target_pairs={{0,1},{1,0},{2,3},{3,2},{4,5},{5,4},{6,7},{7,6},{8,9},{9,8},{10,11... | collective-permute-start | bytes 983048 | tf_op jit(solution)/shard_map/ppermute | solution.py:457
  92.3 2.6 %collective-permute-start.9 = (bf16[1280,128]{1,0:T(8,128)(2,1)S(1)}, bf16[1280,128]{1,0:T(8,128)(2,1)S(1)}, u32[]{:S(2)}, u32[]{:S(2)}) collective-permute-start(bf16[1280,128]{1,0:T(8,128)(2,1)S(1)} %get-tuple-element.56.refs_3_), channel_id=1, source_target_pairs={{0,1},{1,0},{2,3},{3,2},{4,5},{5,4},{6,7},{7,6},{8,9},{9,8},{10,11... | collective-permute-start | bytes 983048 | tf_op jit(solution)/shard_map/ppermute | solution.py:457
  92.7 4.2 %copy-start.7 = (bf16[1,4096,384]{2,1,0:T(8,128)(2,1)S(1)}, bf16[1,4096,384]{2,1,0:T(8,128)(2,1)}, u32[]{:S(2)}) copy-start(bf16[1,4096,384]{2,1,0:T(8,128)(2,1)} %param.12) | copy-start | bytes 9437188
  94.7 2.3 %copy-start.3 = (bf16[1,4096,384]{2,1,0:T(8,128)(2,1)S(1)}, bf16[1,4096,384]{2,1,0:T(8,128)(2,1)}, u32[]{:S(2)}) copy-start(bf16[1,4096,384]{2,1,0:T(8,128)(2,1)} %param.11) | copy-start | bytes 9437188
  94.7 2.3 %copy-start.14 = (f32[320,384]{1,0:T(8,128)S(1)}, f32[320,384]{1,0:T(8,128)}, u32[]{:S(2)}) copy-start(f32[320,384]{1,0:T(8,128)} %copy-done.13) | copy-start | bytes 1474564
  94.7 2.3 %copy-start.16 = (f32[320,384]{1,0:T(8,128)S(1)}, f32[320,384]{1,0:T(8,128)}, u32[]{:S(2)}) copy-start(f32[320,384]{1,0:T(8,128)} %copy-done.15) | copy-start | bytes 1474564
  94.7 5.6 %collective-permute-start.4 = (bf16[320,1024]{1,0:T(8,128)(2,1)}, bf16[320,1024]{1,0:T(8,128)(2,1)}, u32[]{:S(2)}, u32[]{:S(2)}) collective-permute-start(bf16[320,1024]{1,0:T(8,128)(2,1)} %get-tuple-element.47), channel_id=1, source_target_pairs={{0,1},{1,0},{2,3},{3,2},{4,5},{5,4},{6,7},{7,6},{8,9},{9,8},{10,11... | collective-permute-start | bytes 1966088 | tf_op jit(solution)/shard_map/ppermute | solution.py:472
  99.1 0.7 copy-start.19
  99.8 4.7 %collective-permute-start.10 = (bf16[320,512]{1,0:T(8,128)(2,1)}, bf16[320,512]{1,0:T(8,128)(2,1)}, u32[]{:S(2)}, u32[]{:S(2)}) collective-permute-start(bf16[320,512]{1,0:T(8,128)(2,1)} %get-tuple-element.62), channel_id=1, source_target_pairs={{0,1},{1,0},{2,3},{3,2},{4,5},{5,4},{6,7},{7,6},{8,9},{9,8},{10,11... | collective-permute-start | bytes 983048 | tf_op jit(solution)/shard_map/ppermute | solution.py:471
  100.2 4.3 %collective-permute-start.11 = (bf16[320,512]{1,0:T(8,128)(2,1)}, bf16[320,512]{1,0:T(8,128)(2,1)}, u32[]{:S(2)}, u32[]{:S(2)}) collective-permute-start(bf16[320,512]{1,0:T(8,128)(2,1)} %get-tuple-element.63), channel_id=1, source_target_pairs={{0,1},{1,0},{2,3},{3,2},{4,5},{5,4},{6,7},{7,6},{8,9},{9,8},{10,11... | collective-permute-start | bytes 983048 | tf_op jit(solution)/shard_map/ppermute | solution.py:471
  100.3 1.1 copy-start.12
  100.3 15.2 %copy-start.4 = (bf16[1,4096,384]{2,1,0:T(8,128)(2,1)S(1)}, bf16[1,4096,384]{2,1,0:T(8,128)(2,1)}, u32[]{:S(2)}) copy-start(bf16[1,4096,384]{2,1,0:T(8,128)(2,1)} %param.11) | copy-start | bytes 9437188
  103.7 0.8 copy-start.10
  106.6 25.4 %collective-permute-start.13 = (bf16[320,1024]{1,0:T(8,128)(2,1)}, bf16[320,1024]{1,0:T(8,128)(2,1)}, u32[]{:S(2)}, u32[]{:S(2)}) collective-permute-start(bf16[320,1024]{1,0:T(8,128)(2,1)} %get-tuple-element.68), channel_id=1, source_target_pairs={{0,2},{1,3},{2,0},{3,1},{4,6},{5,7},{6,4},{7,5},{8,10},{9,11},{10,... | collective-permute-start | bytes 1966088 | tf_op jit(solution)/shard_map/ppermute | solution.py:481
  110.0 26.4 %all-to-all-start.2 = ((bf16[64,40,128]{2,1,0:T(8,128)(2,1)}), bf16[64,40,128]{2,1,0:T(8,128)(2,1)}, u32[]{:S(2)}, u32[]{:S(2)}) async-start(bf16[64,40,128]{2,1,0:T(8,128)(2,1)} %bitcast.35), calls=%async_computation.2 | async-start | bytes 1310720 | tf_op jit(solution)/shard_map/all_to_all | solution.py:380
  115.5 1.9 %copy-start.8 = (bf16[1,4096,384]{2,1,0:T(8,128)(2,1)S(1)}, bf16[1,4096,384]{2,1,0:T(8,128)(2,1)}, u32[]{:S(2)}) copy-start(bf16[1,4096,384]{2,1,0:T(8,128)(2,1)} %param.12) | copy-start | bytes 9437188
  117.4 0.9 copy-start.20
  120.1 11.9 %collective-permute-start.12 = (bf16[320,1024]{1,0:T(8,128)(2,1)}, bf16[320,1024]{1,0:T(8,128)(2,1)}, u32[]{:S(2)}, u32[]{:S(2)}) collective-permute-start(bf16[320,1024]{1,0:T(8,128)(2,1)} %get-tuple-element.67), channel_id=1, source_target_pairs={{0,1},{1,0},{2,3},{3,2},{4,5},{5,4},{6,7},{7,6},{8,9},{9,8},{10,11... | collective-permute-start | bytes 1966088 | tf_op jit(solution)/shard_map/ppermute | solution.py:486
  131.9 10.4 %copy-start.25 = (f32[128,2]{0,1:T(2,128)S(1)}, f32[128,2]{0,1:T(2,128)}, u32[]{:S(2)}) copy-start(f32[128,2]{0,1:T(2,128)} %param.10) | copy-start | bytes 3076
  131.9 10.5 %copy-start.18 = (bf16[128,1024]{1,0:T(8,128)(2,1)S(1)}, bf16[128,1024]{1,0:T(8,128)(2,1)}, u32[]{:S(2)}) copy-start(bf16[128,1024]{1,0:T(8,128)(2,1)} %cot_ref.3) | copy-start | bytes 786436
  131.9 10.5 %copy-start.23 = (s32[128,2]{0,1:T(2,128)S(1)}, s32[128,2]{0,1:T(2,128)}, u32[]{:S(2)}) copy-start(s32[128,2]{0,1:T(2,128)} %param.9) | copy-start | bytes 3076
  136.4 25.9 %all-to-all-start.4 = ((bf16[64,40,128]{2,1,0:T(8,128)(2,1)}), bf16[64,40,128]{2,1,0:T(8,128)(2,1)S(1)}, u32[]{:S(2)}, u32[]{:S(2)}) async-start(bf16[64,40,128]{2,1,0:T(8,128)(2,1)} %bitcast.15), calls=%async_computation.4 | async-start | bytes 1310720 | tf_op jit(solution)/shard_map/all_to_all | solution.py:380
  145.1 1.3 collective-permute-start.14
  146.4 6.9 %collective-permute-start.15 = (f32[128,2]{1,0:T(8,128)S(1)}, f32[128,2]{1,0:T(8,128)S(1)}, u32[]{:S(2)}, u32[]{:S(2)}) collective-permute-start(f32[128,2]{1,0:T(8,128)S(1)} %add.6), channel_id=1, source_target_pairs={{0,2},{1,3},{2,0},{3,1},{4,6},{5,7},{6,4},{7,5},{8,10},{9,11},{10,... | collective-permute-start | bytes 3080 | tf_op jit(solution)/shard_map/ppermute | solution.py:500

commit v4 on v3

--- a/solution.py
+++ b/solution.py
@@ -111,11 +111,26 @@
     token_ref[...] = jnp.zeros_like(token_ref)
 
 
-def pieces_kernel(c, after, *outs):
+def split_kernel(x_ref, *outs):
+    rows = outs[0].shape[0]
+    for i, out_ref in enumerate(outs):
+        out_ref[...] = x_ref[i * rows : (i + 1) * rows, :]
+
+
+def pieces_kernel(c, after, *refs):
+    *outs, sems = refs
     flat = c.shape[0] * c.shape[1] // len(outs)
     per = c.shape[1] // flat
-    for i, out_ref in enumerate(outs):
-        out_ref[...] = c[i // per, (i % per) * flat : (i % per + 1) * flat, :]
+    copies = [
+        pltpu.make_async_copy(
+            c.at[i // per, pl.ds((i % per) * flat, flat)], out_ref, sems.at[i]
+        )
+        for i, out_ref in enumerate(outs)
+    ]
+    for copy in copies:
+        copy.start()
+    for copy in copies:
+        copy.wait()
 
 
 def untile_pieces(pieces, blocks, wide_ref, out_ref):
@@ -155,9 +170,9 @@
 
 
 def dact_first_kernel(place_ref, *refs):
-    *c, down, out_ref, wide, lhs, buffer, sems = refs
+    *c, down, out_ref, wide, lhs = refs
     core = place_ref[0] & 1
-    w = Loads(down, (core, core + 2), buffer, sems)
+    w = [column_block(down, core + 2 * j, lhs.shape[1]) for j in range(2)]
     blocks = lhs.shape[1] // LANES
     half = len(c) // 2
     untile_pieces(c[:half], blocks, wide, lhs)
@@ -167,9 +182,9 @@
 
 
 def dact_last_kernel(place_ref, *refs):
-    *c, part, down, out_ref, wide, lhs, buffer, sems = refs
+    *c, part, down, out_ref, wide, lhs = refs
     core = 1 - (place_ref[0] & 1)
-    w = Loads(down, (core, core + 2), buffer, sems)
+    w = [column_block(down, core + 2 * j, lhs.shape[1]) for j in range(2)]
     blocks = lhs.shape[1] // LANES
     half = len(c) // 2
     untile_pieces(c[:half], blocks, wide, lhs)
@@ -182,15 +197,25 @@
     return ref[:, index].reshape(width, -1)
 
 
-def pre_first_kernel(place_ref, x0, x1, gate, up, g_ref, u_ref, token_ref, wide, lhs):
+def pre_first_kernel(place_ref, x0, gate, up, g_ref, u_ref, wide, lhs):
     ep = place_ref[0]
     width = lhs.shape[1]
     untile_rows(x0, width // LANES, wide, lhs)
     g_ref[...] = jnp.dot(lhs[...], rows_block(gate, ep, width), preferred_element_type=F32)
     u_ref[...] = jnp.dot(lhs[...], rows_block(up, ep, width), preferred_element_type=F32)
-    untile_rows(x1, width // LANES, wide, lhs)
-    g_ref[...] += jnp.dot(lhs[...], rows_block(gate, ep ^ 1, width), preferred_element_type=F32)
-    u_ref[...] += jnp.dot(lhs[...], rows_block(up, ep ^ 1, width), preferred_element_type=F32)
+
+
+def pre_beside_kernel(place_ref, *refs):
+    *x1, g_in, u_in, gate, up, g_ref, u_ref, token_ref, wide, lhs = refs
+    ep = place_ref[0] ^ 1
+    width = lhs.shape[1]
+    untile_pieces(x1, width // LANES, wide, lhs)
+    g_ref[...] = g_in[...] + jnp.dot(
+        lhs[...], rows_block(gate, ep, width), preferred_element_type=F32
+    )
+    u_ref[...] = u_in[...] + jnp.dot(
+        lhs[...], rows_block(up, ep, width), preferred_element_type=F32
+    )
     token_ref[...] = jnp.zeros_like(token_ref)
 
 
@@ -278,12 +303,25 @@
     out_ref[...] = (keep_ref[...].astype(F32) + came_ref[...].astype(F32)).astype(BF)
 
 
-def grad_sum_kernel(keep_ref, *refs):
-    *came, after, out_ref, token_ref = refs
+def finish_out_kernel(keep_ref, near_ref, far_ref, grad_ref, *refs):
+    *came, after, out_ref, sum_ref, token_ref, wide_ref, sum_buf, rows_buf, sems = refs
     token_ref[...] = jnp.zeros_like(token_ref)
     for i, ref in enumerate(came):
         cols = slice(i * ref.shape[1], (i + 1) * ref.shape[1])
-        out_ref[:, cols] = (keep_ref[:, cols].astype(F32) + ref[...].astype(F32)).astype(BF)
+        sum_buf[:, cols] = (grad_ref[:, cols].astype(F32) + ref[...].astype(F32)).astype(BF)
+    sum_copy = pltpu.make_async_copy(sum_buf, sum_ref, sems.at[0])
+    sum_copy.start()
+
+    def block(f):
+        cols = slice(f * LANES, (f + 1) * LANES)
+        parts = [ref[:, cols].astype(F32) for ref in (keep_ref, near_ref, far_ref)]
+        return parts[0] + parts[1] + parts[2]
+
+    tile_rows(block, keep_ref.shape[1] // LANES, wide_ref, rows_buf)
+    rows_copy = pltpu.make_async_copy(rows_buf, out_ref, sems.at[1])
+    rows_copy.start()
+    sum_copy.wait()
+    rows_copy.wait()
 
 
 def finish_kernel(keep_ref, near_ref, far_ref, after, out_ref, token_ref, wide_ref):
@@ -327,13 +365,13 @@
 HBM = pl.BlockSpec(memory_space=pltpu.HBM)
 
 
-def call(kernel, specs, outs, scratch, flops, moved, *operands):
+def call(kernel, specs, outs, scratch, flops, moved, *operands, place_outs=None):
     single = not isinstance(outs, (list, tuple))
     return pl.pallas_call(
         kernel,
         out_shape=outs,
         in_specs=specs,
-        out_specs=VMEM if single else [VMEM] * len(outs),
+        out_specs=place_outs or (VMEM if single else [VMEM] * len(outs)),
         scratch_shapes=scratch,
         compiler_params=pltpu.CompilerParams(vmem_limit_bytes=VMEM_BYTES),
         cost_estimate=pl.CostEstimate(flops=flops, bytes_accessed=moved, transcendentals=0),
@@ -409,7 +447,6 @@
         [VMEM] * 3, rows_t, [wide], 10**8, moved, routes_t, x_cols, cot_token,
     )
     x0 = exchange(x_rows)
-    x1 = lax.ppermute(x0, "ep", near)
     x2 = lax.ppermute(x0, "ep", far)
     chips = experts // tp
     groups = [
@@ -421,20 +458,28 @@
         cot_rows.reshape(2 * experts, capacity * blocks, LANES),
         ("cp", "tp", "ep"), split_axis=0, concat_axis=0, tiled=True, axis_index_groups=groups,
     ).reshape(2, tiled, LANES)
+    pre = call(
+        pre_first_kernel, [SMEM] + [VMEM] * 3, [acc, acc], [wide, lhs],
+        2 * dot_flops, moved, place, x0, gate_x, up_x,
+    )
+    x1 = call(
+        split_kernel, [VMEM], [shape((tiled // RELAY, LANES), BF)] * RELAY, [], 10**6, moved, x0
+    )
+    x1 = [lax.ppermute(piece, "ep", near) for piece in x1]
     *pre, p_token = call(
-        pre_first_kernel, [SMEM] + [VMEM] * 4, [acc, acc, token],
-        [wide, lhs], 4 * dot_flops, moved, place, x0, x1, gate_x, up_x,
+        pre_beside_kernel, [SMEM] + [VMEM] * (RELAY + 4), [acc, acc, token], [wide, lhs],
+        2 * dot_flops, moved, place, *x1, *pre, gate_x, up_x,
     )
     x2 = tie(x2, p_token)
     x3 = lax.ppermute(x2, "ep", near)
     pre = call(
         pre_next_kernel, [SMEM] + [VMEM] * 3 + [VMEM] * 2, [acc, acc],
-        [wide, lhs], LONG, moved, place, x2, *pre, gate_x, up_x,
+        [wide, lhs], 12000000000, moved, place, x2, *pre, gate_x, up_x,
     )
     act, silu, dsilu, out_send = call(
         forward_kernel, [SMEM] + [VMEM] * 3 + [VMEM] * 3, [hid, acc, acc, send_t],
         [wide, lhs],
-        LONG, moved, place, x3, *pre, gate_x, up_x, down_w,
+        3 * dot_flops, moved, place, x3, *pre, gate_x, up_x, down_w,
     )
     out_came = lax.ppermute(out_send, "ep", near)
     out_keep = call(
@@ -451,17 +496,18 @@
         2 * dot_flops, moved, place, act, down_w, out_token,
     )
     cot_here = call(
-        pieces_kernel, [VMEM, ANY], [shape((2 * tiled // RELAY, LANES), BF)] * RELAY, [],
-        10**6, moved, cot_here, own_token,
+        pieces_kernel, [ANY, ANY], [shape((2 * tiled // RELAY, LANES), BF)] * RELAY,
+        [pltpu.SemaphoreType.DMA((RELAY,))], 10**6, moved, cot_here, own_token,
+        place_outs=[ANY] * RELAY,
     )
     cot_there = [lax.ppermute(piece, "ep", near) for piece in cot_here]
     d_part = call(
-        dact_first_kernel, [SMEM] + [VMEM] * RELAY + [HBM], acc, [wide, lhs, *loads],
+        dact_first_kernel, [SMEM] + [VMEM] * (RELAY + 1), acc, [wide, lhs],
         2 * dot_flops, moved, place, *cot_here, down_w,
     )
     far_token = call(token_kernel, [ANY], token, [], LONG, 10**4, out_far)
     d_act = call(
-        dact_last_kernel, [SMEM] + [VMEM] * (RELAY + 1) + [HBM], acc, [wide, lhs, *loads],
+        dact_last_kernel, [SMEM] + [VMEM] * (RELAY + 2), acc, [wide, lhs],
         2 * dot_flops, moved, place, *cot_there, d_part, down_w,
     )
     d_gate, d_up, grad_keep, *grad_sends = call(
@@ -470,13 +516,12 @@
     )
     grad_came = [lax.ppermute(send, "ep", near) for send in grad_sends]
     out_near = lax.ppermute(out_send2, "ep", near)
-    out_rows, rows_token = call(
-        finish_kernel, [VMEM] * 3 + [ANY], [rows_t, token], [wide], 10**6, moved,
-        out_keep2, out_near, out_far, far_token,
-    )
-    grad_sum, g_token = call(
-        grad_sum_kernel, [VMEM] * (SUMS + 1) + [ANY], [send_t, token], [], 10**6, moved,
-        grad_keep, *grad_came, rows_token,
+    out_rows, grad_sum, g_token = call(
+        finish_out_kernel, [VMEM] * (SUMS + 4) + [ANY], [rows_t, send_t, token],
+        [wide, pltpu.VMEM((slots, width), BF), pltpu.VMEM((tiled, LANES), BF),
+         pltpu.SemaphoreType.DMA((2,))],
+        10**6, 2 * moved, out_keep2, out_near, out_far, grad_keep, *grad_came, far_token,
+        place_outs=[ANY, ANY, VMEM],
     )
     grad_far = lax.ppermute(grad_sum, "ep", far)
     grad_send2, grad_keep2 = call(

time: 165 us -> 162 us (0.982)
  waiting for transfers between devices: 52.6 us -> 48.3 us
  starting transfers between devices: 34.2 us -> 36 us
    ppermute x1, waiting for transfers between devices: 10.4 us -> 0.01 us  [local(): x2 = lax.ppermute(x0, 'ep', far)]
    all_to_all x1, waiting for transfers between devices: 8.98 us -> 13.7 us  [local(): lax.all_to_all(cot_rows.reshape(2 * experts, capacity * blocks, LANES), (...]
    ppermute x2, waiting for transfers between devices: 0.01 us -> 1.75 us  [local(): grad_came = [lax.ppermute(send, 'ep', near) for send in grad_sends]]
    unnamed x54 -> x48, local copies, waits for them, and re-layouts: 13 us -> 13.7 us
    pallas_call x20 -> x21, Pallas kernels: 32.6 us -> 32 us  [call(): pl.pallas_call(kernel, out_shape=outs, in_specs=specs, out_specs=place_ou...]
  transfers between devices with their start and end apart: 20 -> 23, of which waited for: 10 -> 11; matrix products, arithmetic and copies ran while one was open for 0% -> 0% of each run, Pallas kernels for 17% -> 17%
where the time goes in v4:
time: 162 us; the launch traced here: 161 us
  waiting for transfers between devices  48.3 us (30%)
  starting transfers between devices  36 us (22%)
  Pallas kernels  32 us (20%)
  blocking collectives  30.2 us (19%)
  local copies, waits for them, and re-layouts  13.7 us (8%)
    pallas_call x21, Pallas kernels, call(): pl.pallas_call(kernel, out_shape=outs, in_specs=specs, out_specs=place_ou...  32 us
    all_to_all x1, blocking collectives, exchange(): lax.all_to_all(rows.reshape(experts, capacity * blocks, LANES), ('cp', 't...  30.2 us
    unnamed x48, local copies, waits for them, and re-layouts  13.7 us
    all_to_all x1, waiting for transfers between devices, local(): lax.all_to_all(cot_rows.reshape(2 * experts, capacity * blocks, LANES), (...  13.7 us
    ppermute x1, waiting for transfers between devices, local(): grad_far = lax.ppermute(grad_sum, 'ep', far)  11.6 us
    all_to_all x2, starting transfers between devices, exchange(): lax.all_to_all(rows.reshape(experts, capacity * blocks, LANES), ('cp', 't...  11.5 us
    all_to_all x2, waiting for transfers between devices, exchange(): lax.all_to_all(rows.reshape(experts, capacity * blocks, LANES), ('cp', 't...  9.93 us
    all_to_all x1, starting transfers between devices, local(): lax.all_to_all(cot_rows.reshape(2 * experts, capacity * blocks, LANES), (...  9.67 us
  transfers between devices with their start and end apart: 23, of which 11 were waited for; matrix products, arithmetic and copies ran while one was open for 0% of the time, Pallas kernels for 17%

profile of v4, /device:TPU:4, one launch (start us, length us, event | category | flops | bytes accessed | tf_op | source)
XLA Modules:
  0.0 161.2 jit_solution(16170029975555720983)
XLA Ops:
  0.6 5.4 %all-to-all-start = ((bf16[8,128,128]{2,1,0:T(8,128)(2,1)}), bf16[8,128,128]{2,1,0:T(8,128)(2,1)S(1)}, u32[]{:S(2)}, u32[]{:S(2)}) async-start(bf16[8,128,128]{2,1,0:T(8,128)(2,1)} %bitcast.43), calls=%async_computation | async-start | bytes 524288 | tf_op jit(solution)/shard_map/all_to_all | solution.py:437
  6.0 0.9 copy-done.14
  7.0 0.7 copy-done.18
  7.7 0.7 copy-done.21
  8.3 0.6 shard_map.94
  9.0 1.1 copy-done.6
  10.1 3.2 %all-to-all-done.x_ref = bf16[8,128,128]{2,1,0:T(8,128)(2,1)S(1)} async-done(((bf16[8,128,128]{2,1,0:T(8,128)(2,1)}), bf16[8,128,128]{2,1,0:T(8,128)(2,1)S(1)}, u32[]{:S(2)}, u32[]{:S(2)}) %all-to-all-start) | async-done | bytes 262176 | tf_op jit(solution)/shard_map/all_to_all | solution.py:437
  13.2 0.7 copy-done.19
  13.9 0.6 shard_map.95
  14.5 30.2 %all_to_all.25 = bf16[64,40,128]{2,1,0:T(8,128)(2,1)} all-to-all(bf16[64,40,128]{2,1,0:T(8,128)(2,1)S(1)} %bitcast.35), channel_id=1, replica_groups=mesh['cp'=8,'tp'=8,'ep'=4] {'cp','tp'}, dimensions={0} | all-to-all | bytes 1310720 | tf_op jit(solution)/shard_map/all_to_all | solution.py:418
  44.7 0.8 collective-permute-start
  45.5 9.7 %all-to-all-start.2 = ((bf16[128,40,128]{2,1,0:T(8,128)(2,1)}), bf16[128,40,128]{2,1,0:T(8,128)(2,1)}, u32[]{:S(2)}, u32[]{:S(2)}) async-start(bf16[128,40,128]{2,1,0:T(8,128)(2,1)} %bitcast.36), calls=%async_computation.2 | async-start | bytes 2621440 | tf_op jit(solution)/shard_map/all_to_all | solution.py:457
  55.2 1.9 %shard_map.96 = (bf16[640,128]{1,0:T(8,128)(2,1)}, bf16[640,128]{1,0:T(8,128)(2,1)}, bf16[640,128]{1,0:T(8,128)(2,1)}, bf16[640,128]{1,0:T(8,128)(2,1)}) custom-call(bf16[2560,128]{1,0:T(8,128)(2,1)} %bitcast.5.x_ref.x0), custom_call_target="tpu_custom_call" | custom-call | flops 1000000 | bytes 1966080 | tf_op jit(solution)/shard_map/pallas_call | solution.py:370
  57.1 0.5 collective-permute-start.2
  57.7 0.5 collective-permute-start.4
  58.2 1.9 %copy-done.1 = bf16[1,4096,384]{2,1,0:T(8,128)(2,1)S(1)} copy-done((bf16[1,4096,384]{2,1,0:T(8,128)(2,1)S(1)}, bf16[1,4096,384]{2,1,0:T(8,128)(2,1)}, u32[]{:S(2)}) %copy-start.1) | copy-done | bytes 3145752
  60.1 2.0 %shard_map.97 = (f32[320,384]{1,0:T(8,128)S(1)}, f32[320,384]{1,0:T(8,128)S(1)}) custom-call(s32[1]{0:T(128)} %bitcast.1.place_ref, bf16[2560,128]{1,0:T(8,128)(2,1)} %bitcast.5.x_ref.x0, bf16[8,4,128,384]{3,2,1,0:T(8,128)(2,1)S(1)} %bitcast.17, bf16[8,4,128,384]{3,2,1,0:T(8,128)(2,1)S(1)} %bitcast.23), custom_call_target="tpu_custom_call" | custom-call | flops 503316480 | bytes 1966080 | tf_op jit(solution)/shard_map/pallas_call | solution.py:370
  62.1 2.0 %shard_map.98 = (f32[320,384]{1,0:T(8,128)S(1)}, f32[320,384]{1,0:T(8,128)S(1)}, f32[8,128]{1,0:T(8,128)S(1)}) custom-call(s32[1]{0:T(128)} %bitcast.1.place_ref, bf16[640,128]{1,0:T(8,128)(2,1)S(1)} %collective-permute-done.1.refs_0_, bf16[640,128]{1,0:T(8,128)(2,1)S(1)} %collective-permute-done.2.refs_1_, bf16[640,128]{1,0:T(8,128)(2,1)} %collective-permute-done.3.refs_2_, ...), custom_call_target="tpu_custom_call" | custom-call | flops 503316480 | bytes 1966080 | tf_op jit(solution)/shard_map/pallas_call | solution.py:370
  64.2 2.2 %shard_map.100 = (f32[320,384]{1,0:T(8,128)S(1)}, f32[320,384]{1,0:T(8,128)S(1)}) custom-call(s32[1]{0:T(128)} %bitcast.1.place_ref, bf16[2560,128]{1,0:T(8,128)(2,1)} %shard_map.99.x2, f32[320,384]{1,0:T(8,128)S(1)} %get-tuple-element.50.g_in, f32[320,384]{1,0:T(8,128)S(1)} %get-tuple-element.51.u_in, bf16[8,4,128,384]{3,2,1,0:T(8,128)(2,1)S(1)} %bitcast.19, ...), custom_call_target="tpu_custom_call" | custom-call | flops 12000000000 | bytes 1966080 | tf_op jit(solution)/shard_map/pallas_call | solution.py:370
  66.5 1.5 shard_map.101
  68.0 0.7 collective-permute-start.6
  68.7 0.5 shard_map.102.keep_ref
  69.3 1.2 collective-permute-done.6.came_ref
  70.5 1.0 shard_map.103
  71.5 0.6 collective-permute-start.8
  72.1 1.4 shard_map.104
  73.5 0.8 copy-done.8
  74.3 13.7 %all-to-all-done.2 = bf16[128,40,128]{2,1,0:T(8,128)(2,1)} async-done(((bf16[128,40,128]{2,1,0:T(8,128)(2,1)}), bf16[128,40,128]{2,1,0:T(8,128)(2,1)}, u32[]{:S(2)}, u32[]{:S(2)}) %all-to-all-start.2) | async-done | bytes 1310752 | tf_op jit(solution)/shard_map/all_to_all | solution.py:457
  88.0 1.3 shard_map.105
  89.3 0.1 collective-permute-start.10
  89.4 0.5 collective-permute-start.11
  89.9 0.1 collective-permute-start.12
  90.0 0.4 collective-permute-start.9
  90.4 1.9 %copy-done.5 = bf16[1,384,4096]{2,1,0:T(8,128)(2,1)S(1)} copy-done((bf16[1,384,4096]{2,1,0:T(8,128)(2,1)S(1)}, bf16[1,384,4096]{2,1,0:T(8,128)(2,1)}, u32[]{:S(2)}) %copy-start.5) | copy-done | bytes 3145752
  92.3 1.5 shard_map.106.refs_4_
  93.8 0.2 collective-permute-start.7
  94.0 1.5 shard_map.107.dact_ref
  95.5 0.2 copy-done.2
  95.8 0.1 copy-done.13
  95.9 2.1 %shard_map.108 = (bf16[320,384]{1,0:T(8,128)(2,1)S(1)}, bf16[320,384]{1,0:T(8,128)(2,1)S(1)}, bf16[320,1024]{1,0:T(8,128)(2,1)S(1)}, bf16[320,512]{1,0:T(8,128)(2,1)}, bf16[320,512]{1,0:T(8,128)(2,1)}) custom-call(s32[1]{0:T(128)} %bitcast.1.place_ref, f32[320,384]{1,0:T(8,128)S(1)} %shard_map.107.dact_ref, f32[320,384]{1,0:T(8,128)S(1)} %copy-done.11, ...), custom_call_target="tpu_custom_call" | custom-call | flops 1006632960 | bytes 1966080 | tf_op jit(solution)/shard_map/pallas_call | solution.py:370
  98.0 0.1 collective-permute-start.13
  98.1 0.4 collective-permute-start.14
  98.6 0.2 copy-done.16
  98.7 1.3 collective-permute-done.13.refs_0_
  100.0 0.5 collective-permute-done.14.refs_1_
  100.5 2.9 %shard_map.110 = (bf16[2560,128]{1,0:T(8,128)(2,1)S(1)}, bf16[320,1024]{1,0:T(8,128)(2,1)}, f32[8,128]{1,0:T(8,128)S(1)}) custom-call(bf16[320,1024]{1,0:T(8,128)(2,1)S(1)} %copy-done.9, bf16[320,1024]{1,0:T(8,128)(2,1)} %collective-permute-done.7.near_ref, bf16[320,1024]{1,0:T(8,128)(2,1)} %collective-permute-done.8.after.far_ref, ...), custom_call_target="tpu_custom_call" | custom-call | flops 1000000 | bytes 3932160 | tf_op jit(solution)/shard_map/pallas_call | solution.py:370
  103.5 0.8 copy-done.7
  104.3 3.4 %collective-permute-start.16 = (bf16[320,1024]{1,0:T(8,128)(2,1)}, bf16[320,1024]{1,0:T(8,128)(2,1)}, u32[]{:S(2)}, u32[]{:S(2)}) collective-permute-start(bf16[320,1024]{1,0:T(8,128)(2,1)} %get-tuple-element.78), channel_id=1, source_target_pairs={{0,2},{1,3},{2,0},{3,1},{4,6},{5,7},{6,4},{7,5},{8,10},{9,11},{10,... | collective-permute-start | bytes 1966088 | tf_op jit(solution)/shard_map/ppermute | solution.py:526
  107.7 5.7 %all-to-all-start.3 = ((bf16[64,40,128]{2,1,0:T(8,128)(2,1)}), bf16[64,40,128]{2,1,0:T(8,128)(2,1)}, u32[]{:S(2)}, u32[]{:S(2)}) async-start(bf16[64,40,128]{2,1,0:T(8,128)(2,1)} %bitcast.37), calls=%async_computation.3 | async-start | bytes 1310720 | tf_op jit(solution)/shard_map/all_to_all | solution.py:418
  113.4 1.9 %copy-done.3 = bf16[1,4096,384]{2,1,0:T(8,128)(2,1)S(1)} copy-done((bf16[1,4096,384]{2,1,0:T(8,128)(2,1)S(1)}, bf16[1,4096,384]{2,1,0:T(8,128)(2,1)}, u32[]{:S(2)}) %copy-start.3) | copy-done | bytes 3145752
  115.3 0.9 copy-done.17
  116.3 1.7 %shard_map.112 = (bf16[320,1024]{1,0:T(8,128)(2,1)}, bf16[320,1024]{1,0:T(8,128)(2,1)S(1)}) custom-call(s32[1]{0:T(128)} %bitcast.1.place_ref, bf16[320,384]{1,0:T(8,128)(2,1)S(1)} %get-tuple-element.73.dgate_ref, bf16[320,384]{1,0:T(8,128)(2,1)S(1)} %copy-done.17, bf16[4,1024,384]{2,1,0:T(8,128)(2,1)S(1)} %bitcast.22, bf16[4,1024,384]{2,1,0:T(8,128)(2,1)S(1)} %bitcast.28, ...), custom_call_target="tpu_custom_call" | custom-call | flops 1006632960 | bytes 1966080 | tf_op jit(solution)/shard_map/pallas_call | solution.py:370
  118.0 11.6 %collective-permute-done.16.after.far_ref = bf16[320,1024]{1,0:T(8,128)(2,1)} collective-permute-done((bf16[320,1024]{1,0:T(8,128)(2,1)}, bf16[320,1024]{1,0:T(8,128)(2,1)}, u32[]{:S(2)}, u32[]{:S(2)}) %collective-permute-start.16) | collective-permute-done | bytes 655392 | tf_op jit(solution)/shard_map/ppermute | solution.py:526
  129.6 3.1 %shard_map.114 = (bf16[2560,128]{1,0:T(8,128)(2,1)}, f32[8,128]{1,0:T(8,128)}) custom-call(bf16[320,1024]{1,0:T(8,128)(2,1)S(1)} %get-tuple-element.76.keep_ref, bf16[320,1024]{1,0:T(8,128)(2,1)} %collective-permute-done.15.near_ref, bf16[320,1024]{1,0:T(8,128)(2,1)} %collective-permute-done.16.after.far_ref, f32[8,128]{1,0:T(8,128)S(1)} %shard_map.113.after), custom_call_target="tpu_custom_call" | custom-call | flops 1000000 | bytes 1966080 | tf_op jit(solution)/shard_map/pallas_call | solution.py:370
  132.7 1.2 all-to-all-done.3
  133.9 5.8 %all-to-all-start.4 = ((bf16[64,40,128]{2,1,0:T(8,128)(2,1)}), bf16[64,40,128]{2,1,0:T(8,128)(2,1)S(1)}, u32[]{:S(2)}, u32[]{:S(2)}) async-start(bf16[64,40,128]{2,1,0:T(8,128)(2,1)} %bitcast.15), calls=%async_computation.4 | async-start | bytes 1310720 | tf_op jit(solution)/shard_map/all_to_all | solution.py:418
  139.8 0.1 copy.11.gates_ref
  139.9 2.7 %shard_map.111 = (bf16[128,1024]{1,0:T(8,128)(2,1)}, f32[128,2]{1,0:T(8,128)S(1)}) custom-call(s32[2,128]{1,0:T(2,128)S(1)} %bitcast.40, f32[128,2]{1,0:T(8,128)S(1)} %copy.11.gates_ref, bf16[128,1024]{1,0:T(8,128)(2,1)S(1)} %copy-done.15, bf16[2560,128]{1,0:T(8,128)(2,1)} %bitcast.14.rows_ref), custom_call_target="tpu_custom_call" | custom-call | flops 100000000 | bytes 1966080 | tf_op jit(solution)/shard_map/pallas_call | solution.py:370
  142.6 1.3 collective-permute-done.17
  143.8 0.9 collective-permute-start.18
  144.7 5.7 %collective-permute-done.18 = f32[128,2]{1,0:T(8,128)S(1)} collective-permute-done((f32[128,2]{1,0:T(8,128)S(1)}, f32[128,2]{1,0:T(8,128)S(1)}, u32[]{:S(2)}, u32[]{:S(2)}) %collective-permute-start.18) | collective-permute-done | bytes 1056 | tf_op jit(solution)/shard_map/ppermute | solution.py:545
  150.4 0.6 copy.12
  151.1 8.7 %all-to-all-done.4 = bf16[64,40,128]{2,1,0:T(8,128)(2,1)S(1)} async-done(((bf16[64,40,128]{2,1,0:T(8,128)(2,1)}), bf16[64,40,128]{2,1,0:T(8,128)(2,1)S(1)}, u32[]{:S(2)}, u32[]{:S(2)}) %all-to-all-start.4) | async-done | bytes 655392 | tf_op jit(solution)/shard_map/all_to_all | solution.py:418
  159.8 1.4 shard_map.115
  (55 shorter events, 0.4 us)
Async XLA Ops:
  0.6 57.5 %copy-start = (bf16[1,4096,384]{2,1,0:T(8,128)(2,1)S(1)}, bf16[1,4096,384]{2,1,0:T(8,128)(2,1)}, u32[]{:S(2)}) copy-start(bf16[1,4096,384]{2,1,0:T(8,128)(2,1)} %param.11) | copy-start | bytes 9437188
  0.6 12.6 %all-to-all-start = ((bf16[8,128,128]{2,1,0:T(8,128)(2,1)}), bf16[8,128,128]{2,1,0:T(8,128)(2,1)S(1)}, u32[]{:S(2)}, u32[]{:S(2)}) async-start(bf16[8,128,128]{2,1,0:T(8,128)(2,1)} %bitcast.43), calls=%async_computation | async-start | bytes 524288 | tf_op jit(solution)/shard_map/all_to_all | solution.py:437
  6.0 0.9 copy-start.14
  7.0 0.7 copy-start.18
  7.6 0.7 copy-start.21
  9.0 1.1 copy-start.6
  13.2 0.7 copy-start.19
  44.7 19.4 %collective-permute-start = (bf16[2560,128]{1,0:T(8,128)(2,1)}, bf16[2560,128]{1,0:T(8,128)(2,1)}, u32[]{:S(2)}, u32[]{:S(2)}) collective-permute-start(bf16[2560,128]{1,0:T(8,128)(2,1)} %bitcast.5.x_ref.x0), channel_id=1, source_target_pairs={{0,2},{1,3},{2,0},{3,1},{4,6},{5,7},{6,4},{7,5},{8,10},{9,11},{10,... | collective-permute-start | bytes 1966088 | tf_op jit(solution)/shard_map/ppermute | solution.py:450
  45.5 42.5 %all-to-all-start.2 = ((bf16[128,40,128]{2,1,0:T(8,128)(2,1)}), bf16[128,40,128]{2,1,0:T(8,128)(2,1)}, u32[]{:S(2)}, u32[]{:S(2)}) async-start(bf16[128,40,128]{2,1,0:T(8,128)(2,1)} %bitcast.36), calls=%async_computation.2 | async-start | bytes 2621440 | tf_op jit(solution)/shard_map/all_to_all | solution.py:457
  57.1 5.0 %collective-permute-start.1 = (bf16[640,128]{1,0:T(8,128)(2,1)}, bf16[640,128]{1,0:T(8,128)(2,1)S(1)}, u32[]{:S(2)}, u32[]{:S(2)}) collective-permute-start(bf16[640,128]{1,0:T(8,128)(2,1)} %get-tuple-element.43), channel_id=1, source_target_pairs={{0,1},{1,0},{2,3},{3,2},{4,5},{5,4},{6,7},{7,6},{8,9},{9,8},{10,11... | collective-permute-start | bytes 491528 | tf_op jit(solution)/shard_map/ppermute | solution.py:468
  57.1 5.0 %collective-permute-start.2 = (bf16[640,128]{1,0:T(8,128)(2,1)}, bf16[640,128]{1,0:T(8,128)(2,1)S(1)}, u32[]{:S(2)}, u32[]{:S(2)}) collective-permute-start(bf16[640,128]{1,0:T(8,128)(2,1)} %get-tuple-element.44), channel_id=1, source_target_pairs={{0,1},{1,0},{2,3},{3,2},{4,5},{5,4},{6,7},{7,6},{8,9},{9,8},{10,11... | collective-permute-start | bytes 491528 | tf_op jit(solution)/shard_map/ppermute | solution.py:468
  57.7 4.5 %collective-permute-start.3 = (bf16[640,128]{1,0:T(8,128)(2,1)}, bf16[640,128]{1,0:T(8,128)(2,1)}, u32[]{:S(2)}, u32[]{:S(2)}) collective-permute-start(bf16[640,128]{1,0:T(8,128)(2,1)} %get-tuple-element.45), channel_id=1, source_target_pairs={{0,1},{1,0},{2,3},{3,2},{4,5},{5,4},{6,7},{7,6},{8,9},{9,8},{10,11... | collective-permute-start | bytes 491528 | tf_op jit(solution)/shard_map/ppermute | solution.py:468
  57.7 4.5 %collective-permute-start.4 = (bf16[640,128]{1,0:T(8,128)(2,1)}, bf16[640,128]{1,0:T(8,128)(2,1)}, u32[]{:S(2)}, u32[]{:S(2)}) collective-permute-start(bf16[640,128]{1,0:T(8,128)(2,1)} %get-tuple-element.46), channel_id=1, source_target_pairs={{0,1},{1,0},{2,3},{3,2},{4,5},{5,4},{6,7},{7,6},{8,9},{9,8},{10,11... | collective-permute-start | bytes 491528 | tf_op jit(solution)/shard_map/ppermute | solution.py:468
  58.2 1.9 %copy-start.1 = (bf16[1,4096,384]{2,1,0:T(8,128)(2,1)S(1)}, bf16[1,4096,384]{2,1,0:T(8,128)(2,1)}, u32[]{:S(2)}) copy-start(bf16[1,4096,384]{2,1,0:T(8,128)(2,1)} %param.12) | copy-start | bytes 9437188
  64.1 2.4 %collective-permute-start.5 = (bf16[2560,128]{1,0:T(8,128)(2,1)}, bf16[2560,128]{1,0:T(8,128)(2,1)S(1)}, u32[]{:S(2)}, u32[]{:S(2)}) collective-permute-start(bf16[2560,128]{1,0:T(8,128)(2,1)} %shard_map.99.x2), channel_id=1, source_target_pairs={{0,1},{1,0},{2,3},{3,2},{4,5},{5,4},{6,7},{7,6},{8,9},{9,8},{10,11... | collective-permute-start | bytes 1966088 | tf_op jit(solution)/shard_map/ppermute | solution.py:474
  64.2 2.3 %copy-start.4 = (bf16[1,384,4096]{2,1,0:T(8,128)(2,1)S(1)}, bf16[1,384,4096]{2,1,0:T(8,128)(2,1)}, u32[]{:S(2)}) copy-start(bf16[1,384,4096]{2,1,0:T(8,128)(2,1)} %param.13) | copy-start | bytes 9437188
  68.0 4.1 %copy-start.10 = (f32[320,384]{1,0:T(8,128)}, f32[320,384]{1,0:T(8,128)S(1)}, u32[]{:S(2)}) copy-start(f32[320,384]{1,0:T(8,128)S(1)} %get-tuple-element.66.silu_ref) | copy-start | bytes 1474564
  68.0 4.1 %copy-start.12 = (f32[320,384]{1,0:T(8,128)}, f32[320,384]{1,0:T(8,128)S(1)}, u32[]{:S(2)}) copy-start(f32[320,384]{1,0:T(8,128)S(1)} %get-tuple-element.67.dsilu_ref) | copy-start | bytes 1474564
  68.0 2.4 %collective-permute-start.6 = (bf16[320,1024]{1,0:T(8,128)(2,1)S(1)}, bf16[320,1024]{1,0:T(8,128)(2,1)S(1)}, u32[]{:S(2)}, u32[]{:S(2)}) collective-permute-start(bf16[320,1024]{1,0:T(8,128)(2,1)S(1)} %get-tuple-element.55), channel_id=1, source_target_pairs={{0,1},{1,0},{2,3},{3,2},{4,5},{5,4},{6,7},{7,6},{8,9},{9,8},{10,11... | collective-permute-start | bytes 1966088 | tf_op jit(solution)/shard_map/ppermute | solution.py:484
  71.5 27.1 %collective-permute-start.8 = (bf16[320,1024]{1,0:T(8,128)(2,1)}, bf16[320,1024]{1,0:T(8,128)(2,1)}, u32[]{:S(2)}, u32[]{:S(2)}) collective-permute-start(bf16[320,1024]{1,0:T(8,128)(2,1)} %get-tuple-element.59), channel_id=1, source_target_pairs={{0,2},{1,3},{2,0},{3,1},{4,6},{5,7},{6,4},{7,5},{8,10},{9,11},{10,... | collective-permute-start | bytes 1966088 | tf_op jit(solution)/shard_map/ppermute | solution.py:493
  73.5 0.8 copy-start.8
  89.3 4.5 %collective-permute-start.10 = (bf16[1280,128]{1,0:T(8,128)(2,1)S(1)}, bf16[1280,128]{1,0:T(8,128)(2,1)S(1)}, u32[]{:S(2)}, u32[]{:S(2)}) collective-permute-start(bf16[1280,128]{1,0:T(8,128)(2,1)S(1)} %get-tuple-element.63.refs_1_), channel_id=1, source_target_pairs={{0,1},{1,0},{2,3},{3,2},{4,5},{5,4},{6,7},{7,6},{8,9},{9,8},{10,11... | collective-permute-start | bytes 983048 | tf_op jit(solution)/shard_map/ppermute | solution.py:503
  89.4 4.6 %collective-permute-start.11 = (bf16[1280,128]{1,0:T(8,128)(2,1)S(1)}, bf16[1280,128]{1,0:T(8,128)(2,1)S(1)}, u32[]{:S(2)}, u32[]{:S(2)}) collective-permute-start(bf16[1280,128]{1,0:T(8,128)(2,1)S(1)} %get-tuple-element.64.refs_2_), channel_id=1, source_target_pairs={{0,1},{1,0},{2,3},{3,2},{4,5},{5,4},{6,7},{7,6},{8,9},{9,8},{10,11... | collective-permute-start | bytes 983048 | tf_op jit(solution)/shard_map/ppermute | solution.py:503
  89.9 4.1 %collective-permute-start.12 = (bf16[1280,128]{1,0:T(8,128)(2,1)S(1)}, bf16[1280,128]{1,0:T(8,128)(2,1)S(1)}, u32[]{:S(2)}, u32[]{:S(2)}) collective-permute-start(bf16[1280,128]{1,0:T(8,128)(2,1)S(1)} %get-tuple-element.65.refs_3_), channel_id=1, source_target_pairs={{0,1},{1,0},{2,3},{3,2},{4,5},{5,4},{6,7},{7,6},{8,9},{9,8},{10,11... | collective-permute-start | bytes 983048 | tf_op jit(solution)/shard_map/ppermute | solution.py:503
  90.0 4.0 %collective-permute-start.9 = (bf16[1280,128]{1,0:T(8,128)(2,1)S(1)}, bf16[1280,128]{1,0:T(8,128)(2,1)S(1)}, u32[]{:S(2)}, u32[]{:S(2)}) collective-permute-start(bf16[1280,128]{1,0:T(8,128)(2,1)S(1)} %get-tuple-element.62.refs_0_), channel_id=1, source_target_pairs={{0,1},{1,0},{2,3},{3,2},{4,5},{5,4},{6,7},{7,6},{8,9},{9,8},{10,11... | collective-permute-start | bytes 983048 | tf_op jit(solution)/shard_map/ppermute | solution.py:503
  90.4 1.9 %copy-start.5 = (bf16[1,384,4096]{2,1,0:T(8,128)(2,1)S(1)}, bf16[1,384,4096]{2,1,0:T(8,128)(2,1)}, u32[]{:S(2)}) copy-start(bf16[1,384,4096]{2,1,0:T(8,128)(2,1)} %param.13) | copy-start | bytes 9437188
  93.8 1.9 %copy-start.2 = (bf16[1,4096,384]{2,1,0:T(8,128)(2,1)S(1)}, bf16[1,4096,384]{2,1,0:T(8,128)(2,1)}, u32[]{:S(2)}) copy-start(bf16[1,4096,384]{2,1,0:T(8,128)(2,1)} %param.12) | copy-start | bytes 9437188
  93.8 2.0 %copy-start.11 = (f32[320,384]{1,0:T(8,128)S(1)}, f32[320,384]{1,0:T(8,128)}, u32[]{:S(2)}) copy-start(f32[320,384]{1,0:T(8,128)} %copy-done.10) | copy-start | bytes 1474564
  93.8 2.1 %copy-start.13 = (f32[320,384]{1,0:T(8,128)S(1)}, f32[320,384]{1,0:T(8,128)}, u32[]{:S(2)}) copy-start(f32[320,384]{1,0:T(8,128)} %copy-done.12) | copy-start | bytes 1474564
  93.8 4.9 %collective-permute-start.7 = (bf16[320,1024]{1,0:T(8,128)(2,1)}, bf16[320,1024]{1,0:T(8,128)(2,1)}, u32[]{:S(2)}, u32[]{:S(2)}) collective-permute-start(bf16[320,1024]{1,0:T(8,128)(2,1)} %get-tuple-element.58), channel_id=1, source_target_pairs={{0,1},{1,0},{2,3},{3,2},{4,5},{5,4},{6,7},{7,6},{8,9},{9,8},{10,11... | collective-permute-start | bytes 1966088 | tf_op jit(solution)/shard_map/ppermute | solution.py:518
  98.0 0.7 copy-start.16
  98.0 2.0 %collective-permute-start.13 = (bf16[320,512]{1,0:T(8,128)(2,1)}, bf16[320,512]{1,0:T(8,128)(2,1)}, u32[]{:S(2)}, u32[]{:S(2)}) collective-permute-start(bf16[320,512]{1,0:T(8,128)(2,1)} %get-tuple-element.69), channel_id=1, source_target_pairs={{0,1},{1,0},{2,3},{3,2},{4,5},{5,4},{6,7},{7,6},{8,9},{9,8},{10,11... | collective-permute-start | bytes 983048 | tf_op jit(solution)/shard_map/ppermute | solution.py:517
  98.1 2.3 %collective-permute-start.14 = (bf16[320,512]{1,0:T(8,128)(2,1)}, bf16[320,512]{1,0:T(8,128)(2,1)}, u32[]{:S(2)}, u32[]{:S(2)}) collective-permute-start(bf16[320,512]{1,0:T(8,128)(2,1)} %get-tuple-element.70), channel_id=1, source_target_pairs={{0,1},{1,0},{2,3},{3,2},{4,5},{5,4},{6,7},{7,6},{8,9},{9,8},{10,11... | collective-permute-start | bytes 983048 | tf_op jit(solution)/shard_map/ppermute | solution.py:517
  98.6 1.9 %copy-start.9 = (bf16[320,1024]{1,0:T(8,128)(2,1)S(1)}, bf16[320,1024]{1,0:T(8,128)(2,1)}, u32[]{:S(2)}) copy-start(bf16[320,1024]{1,0:T(8,128)(2,1)} %copy-done.8) | copy-start | bytes 1966084
  103.4 0.9 copy-start.7
  104.3 25.3 %collective-permute-start.16 = (bf16[320,1024]{1,0:T(8,128)(2,1)}, bf16[320,1024]{1,0:T(8,128)(2,1)}, u32[]{:S(2)}, u32[]{:S(2)}) collective-permute-start(bf16[320,1024]{1,0:T(8,128)(2,1)} %get-tuple-element.78), channel_id=1, source_target_pairs={{0,2},{1,3},{2,0},{3,1},{4,6},{5,7},{6,4},{7,5},{8,10},{9,11},{10,... | collective-permute-start | bytes 1966088 | tf_op jit(solution)/shard_map/ppermute | solution.py:526
  107.7 26.2 %all-to-all-start.3 = ((bf16[64,40,128]{2,1,0:T(8,128)(2,1)}), bf16[64,40,128]{2,1,0:T(8,128)(2,1)}, u32[]{:S(2)}, u32[]{:S(2)}) async-start(bf16[64,40,128]{2,1,0:T(8,128)(2,1)} %bitcast.37), calls=%async_computation.3 | async-start | bytes 1310720 | tf_op jit(solution)/shard_map/all_to_all | solution.py:418
  113.4 1.9 %copy-start.3 = (bf16[1,4096,384]{2,1,0:T(8,128)(2,1)S(1)}, bf16[1,4096,384]{2,1,0:T(8,128)(2,1)}, u32[]{:S(2)}) copy-start(bf16[1,4096,384]{2,1,0:T(8,128)(2,1)} %param.12) | copy-start | bytes 9437188
  115.3 0.9 copy-start.17
  118.0 11.6 %collective-permute-start.15 = (bf16[320,1024]{1,0:T(8,128)(2,1)}, bf16[320,1024]{1,0:T(8,128)(2,1)}, u32[]{:S(2)}, u32[]{:S(2)}) collective-permute-start(bf16[320,1024]{1,0:T(8,128)(2,1)} %get-tuple-element.77), channel_id=1, source_target_pairs={{0,1},{1,0},{2,3},{3,2},{4,5},{5,4},{6,7},{7,6},{8,9},{9,8},{10,11... | collective-permute-start | bytes 1966088 | tf_op jit(solution)/shard_map/ppermute | solution.py:531
  129.6 10.2 %copy-start.22 = (f32[128,2]{0,1:T(2,128)S(1)}, f32[128,2]{0,1:T(2,128)}, u32[]{:S(2)}) copy-start(f32[128,2]{0,1:T(2,128)} %param.10) | copy-start | bytes 3076
  129.6 10.3 %copy-start.15 = (bf16[128,1024]{1,0:T(8,128)(2,1)S(1)}, bf16[128,1024]{1,0:T(8,128)(2,1)}, u32[]{:S(2)}) copy-start(bf16[128,1024]{1,0:T(8,128)(2,1)} %cot_ref.3) | copy-start | bytes 786436
  129.6 10.3 %copy-start.20 = (s32[128,2]{0,1:T(2,128)S(1)}, s32[128,2]{0,1:T(2,128)}, u32[]{:S(2)}) copy-start(s32[128,2]{0,1:T(2,128)} %param.9) | copy-start | bytes 3076
  133.9 25.9 %all-to-all-start.4 = ((bf16[64,40,128]{2,1,0:T(8,128)(2,1)}), bf16[64,40,128]{2,1,0:T(8,128)(2,1)S(1)}, u32[]{:S(2)}, u32[]{:S(2)}) async-start(bf16[64,40,128]{2,1,0:T(8,128)(2,1)} %bitcast.15), calls=%async_computation.4 | async-start | bytes 1310720 | tf_op jit(solution)/shard_map/all_to_all | solution.py:418
  142.6 1.3 collective-permute-start.17
  143.8 6.6 %collective-permute-start.18 = (f32[128,2]{1,0:T(8,128)S(1)}, f32[128,2]{1,0:T(8,128)S(1)}, u32[]{:S(2)}, u32[]{:S(2)}) collective-permute-start(f32[128,2]{1,0:T(8,128)S(1)} %add.6), channel_id=1, source_target_pairs={{0,2},{1,3},{2,0},{3,1},{4,6},{5,7},{6,4},{7,5},{8,10},{9,11},{10,... | collective-permute-start | bytes 3080 | tf_op jit(solution)/shard_map/ppermute | solution.py:545

commit v5 on v4

--- a/solution.py
+++ b/solution.py
@@ -267,7 +267,7 @@
 
 
 def grad_kernel(
-    place_ref, dact_ref, silu_ref, dsilu_ref, gate, up, dgate_ref, dup_ref, keep_ref, *sends
+    place_ref, dact_ref, silu_ref, dsilu_ref, gate, up, dgate_ref, dup_ref, *sends
 ):
     ep = place_ref[0]
     d_act = dact_ref[...]
@@ -277,7 +277,10 @@
     for i, send_ref in enumerate(sends):
         part = send_ref.shape[1]
         send_ref[...] = send[:, i * part : (i + 1) * part]
-    keep_ref[...] = grad_block(dgate_ref, dup_ref, gate, up, ep ^ 2).astype(BF)
+
+
+def grad_keep_kernel(place_ref, dgate_ref, dup_ref, gate, up, keep_ref):
+    keep_ref[...] = grad_block(dgate_ref, dup_ref, gate, up, place_ref[0] ^ 2).astype(BF)
 
 
 def own_out_kernel(place_ref, act_ref, down, after, send_ref, keep_ref, token_ref):
@@ -510,9 +513,13 @@
         dact_last_kernel, [SMEM] + [VMEM] * (RELAY + 2), acc, [wide, lhs],
         2 * dot_flops, moved, place, *cot_there, d_part, down_w,
     )
-    d_gate, d_up, grad_keep, *grad_sends = call(
-        grad_kernel, [SMEM] + [VMEM] * 3 + [VMEM] * 2, [hid, hid, keep_t] + [shape((slots, width // SUMS), BF)] * SUMS, [],
+    d_gate, d_up, *grad_sends = call(
+        grad_kernel, [SMEM] + [VMEM] * 3 + [VMEM] * 2, [hid, hid] + [shape((slots, width // SUMS), BF)] * SUMS, [],
         4 * dot_flops, moved, place, d_act, silu, dsilu, gate_q, up_q,
+    )
+    grad_keep = call(
+        grad_keep_kernel, [SMEM] + [VMEM] * 4, keep_t, [], 2 * dot_flops, moved,
+        place, d_gate, d_up, gate_q, up_q,
     )
     grad_came = [lax.ppermute(send, "ep", near) for send in grad_sends]
     out_near = lax.ppermute(out_send2, "ep", near)

time: 162 us -> 162 us (level)
    pallas_call x21 -> x22, Pallas kernels: 32 us -> 32.4 us  [call(): pl.pallas_call(kernel, out_shape=outs, in_specs=specs, out_specs=place_ou...]
    unnamed x48 -> x52, local copies, waits for them, and re-layouts: 13.7 us -> 13.7 us
where the time goes in v5:
time: 162 us; the launch traced here: 161 us
  waiting for transfers between devices  47.5 us (29%)
  starting transfers between devices  35.9 us (22%)
  Pallas kernels  32.4 us (20%)
  blocking collectives  30.2 us (19%)
  local copies, waits for them, and re-layouts  13.7 us (8%)
    pallas_call x22, Pallas kernels, call(): pl.pallas_call(kernel, out_shape=outs, in_specs=specs, out_specs=place_ou...  32.4 us
    all_to_all x1, blocking collectives, exchange(): lax.all_to_all(rows.reshape(experts, capacity * blocks, LANES), ('cp', 't...  30.2 us
    all_to_all x1, waiting for transfers between devices, local(): lax.all_to_all(cot_rows.reshape(2 * experts, capacity * blocks, LANES), (...  13.7 us
    unnamed x52, local copies, waits for them, and re-layouts  13.7 us
    ppermute x1, waiting for transfers between devices, local(): grad_far = lax.ppermute(grad_sum, 'ep', far)  11.5 us
    all_to_all x2, starting transfers between devices, exchange(): lax.all_to_all(rows.reshape(experts, capacity * blocks, LANES), ('cp', 't...  11.5 us
    all_to_all x2, waiting for transfers between devices, exchange(): lax.all_to_all(rows.reshape(experts, capacity * blocks, LANES), ('cp', 't...  10 us
    all_to_all x1, starting transfers between devices, local(): lax.all_to_all(cot_rows.reshape(2 * experts, capacity * blocks, LANES), (...  9.67 us
  transfers between devices with their start and end apart: 23, of which 11 were waited for; matrix products, arithmetic and copies ran while one was open for 0% of the time, Pallas kernels for 17%

profile of v5, /device:TPU:4, one launch (start us, length us, event | category | flops | bytes accessed | tf_op | source)
XLA Modules:
  0.0 160.8 jit_solution(4125867897775394296)
XLA Ops:
  0.6 5.4 %all-to-all-start = ((bf16[8,128,128]{2,1,0:T(8,128)(2,1)}), bf16[8,128,128]{2,1,0:T(8,128)(2,1)S(1)}, u32[]{:S(2)}, u32[]{:S(2)}) async-start(bf16[8,128,128]{2,1,0:T(8,128)(2,1)} %bitcast.45), calls=%async_computation | async-start | bytes 524288 | tf_op jit(solution)/shard_map/all_to_all | solution.py:440
  6.0 0.9 copy-done.18
  7.0 0.7 copy-done.20
  7.7 0.7 copy-done.23
  8.3 0.6 shard_map.94
  9.0 1.1 copy-done.6
  10.1 3.2 %all-to-all-done.x_ref = bf16[8,128,128]{2,1,0:T(8,128)(2,1)S(1)} async-done(((bf16[8,128,128]{2,1,0:T(8,128)(2,1)}), bf16[8,128,128]{2,1,0:T(8,128)(2,1)S(1)}, u32[]{:S(2)}, u32[]{:S(2)}) %all-to-all-start) | async-done | bytes 262176 | tf_op jit(solution)/shard_map/all_to_all | solution.py:440
  13.2 0.7 copy-done.21
  13.9 0.6 shard_map.95
  14.5 30.2 %all_to_all.25 = bf16[64,40,128]{2,1,0:T(8,128)(2,1)} all-to-all(bf16[64,40,128]{2,1,0:T(8,128)(2,1)S(1)} %bitcast.37), channel_id=1, replica_groups=mesh['cp'=8,'tp'=8,'ep'=4] {'cp','tp'}, dimensions={0} | all-to-all | bytes 1310720 | tf_op jit(solution)/shard_map/all_to_all | solution.py:421
  44.7 0.8 collective-permute-start
  45.5 9.7 %all-to-all-start.2 = ((bf16[128,40,128]{2,1,0:T(8,128)(2,1)}), bf16[128,40,128]{2,1,0:T(8,128)(2,1)}, u32[]{:S(2)}, u32[]{:S(2)}) async-start(bf16[128,40,128]{2,1,0:T(8,128)(2,1)} %bitcast.38), calls=%async_computation.2 | async-start | bytes 2621440 | tf_op jit(solution)/shard_map/all_to_all | solution.py:460
  55.2 1.9 %shard_map.96 = (bf16[640,128]{1,0:T(8,128)(2,1)}, bf16[640,128]{1,0:T(8,128)(2,1)}, bf16[640,128]{1,0:T(8,128)(2,1)}, bf16[640,128]{1,0:T(8,128)(2,1)}) custom-call(bf16[2560,128]{1,0:T(8,128)(2,1)} %bitcast.5.x_ref.x0), custom_call_target="tpu_custom_call" | custom-call | flops 1000000 | bytes 1966080 | tf_op jit(solution)/shard_map/pallas_call | solution.py:373
  57.2 0.5 collective-permute-start.2
  57.7 0.5 collective-permute-start.4
  58.2 1.9 %copy-done.1 = bf16[1,4096,384]{2,1,0:T(8,128)(2,1)S(1)} copy-done((bf16[1,4096,384]{2,1,0:T(8,128)(2,1)S(1)}, bf16[1,4096,384]{2,1,0:T(8,128)(2,1)}, u32[]{:S(2)}) %copy-start.1) | copy-done | bytes 3145752
  60.1 2.0 %shard_map.97 = (f32[320,384]{1,0:T(8,128)S(1)}, f32[320,384]{1,0:T(8,128)S(1)}) custom-call(s32[1]{0:T(128)} %bitcast.1.place_ref, bf16[2560,128]{1,0:T(8,128)(2,1)} %bitcast.5.x_ref.x0, bf16[8,4,128,384]{3,2,1,0:T(8,128)(2,1)S(1)} %bitcast.17, bf16[8,4,128,384]{3,2,1,0:T(8,128)(2,1)S(1)} %bitcast.24), custom_call_target="tpu_custom_call" | custom-call | flops 503316480 | bytes 1966080 | tf_op jit(solution)/shard_map/pallas_call | solution.py:373
  62.2 2.0 %shard_map.98 = (f32[320,384]{1,0:T(8,128)S(1)}, f32[320,384]{1,0:T(8,128)S(1)}, f32[8,128]{1,0:T(8,128)S(1)}) custom-call(s32[1]{0:T(128)} %bitcast.1.place_ref, bf16[640,128]{1,0:T(8,128)(2,1)S(1)} %collective-permute-done.1.refs_0_, bf16[640,128]{1,0:T(8,128)(2,1)S(1)} %collective-permute-done.2.refs_1_, bf16[640,128]{1,0:T(8,128)(2,1)} %collective-permute-done.3.refs_2_, ...), custom_call_target="tpu_custom_call" | custom-call | flops 503316480 | bytes 1966080 | tf_op jit(solution)/shard_map/pallas_call | solution.py:373
  64.1 0.1 collective-permute-start.5
  64.3 2.2 %shard_map.100 = (f32[320,384]{1,0:T(8,128)S(1)}, f32[320,384]{1,0:T(8,128)S(1)}) custom-call(s32[1]{0:T(128)} %bitcast.1.place_ref, bf16[2560,128]{1,0:T(8,128)(2,1)} %shard_map.99.x2, f32[320,384]{1,0:T(8,128)S(1)} %get-tuple-element.49.g_in, f32[320,384]{1,0:T(8,128)S(1)} %get-tuple-element.50.u_in, bf16[8,4,128,384]{3,2,1,0:T(8,128)(2,1)S(1)} %bitcast.19, ...), custom_call_target="tpu_custom_call" | custom-call | flops 12000000000 | bytes 1966080 | tf_op jit(solution)/shard_map/pallas_call | solution.py:373
  66.5 1.5 shard_map.101
  68.1 0.7 collective-permute-start.6
  68.8 0.5 shard_map.102.keep_ref
  69.3 1.2 collective-permute-done.6.came_ref
  70.5 1.0 shard_map.103
  71.5 0.7 collective-permute-start.8
  72.2 1.4 shard_map.104
  73.5 0.8 copy-done.12
  74.4 13.7 %all-to-all-done.2 = bf16[128,40,128]{2,1,0:T(8,128)(2,1)} async-done(((bf16[128,40,128]{2,1,0:T(8,128)(2,1)}), bf16[128,40,128]{2,1,0:T(8,128)(2,1)}, u32[]{:S(2)}, u32[]{:S(2)}) %all-to-all-start.2) | async-done | bytes 1310752 | tf_op jit(solution)/shard_map/all_to_all | solution.py:460
  88.0 1.3 shard_map.105
  89.4 0.5 collective-permute-start.11
  89.9 0.1 collective-permute-start.12
  90.0 0.4 collective-permute-start.9
  90.4 1.9 %copy-done.5 = bf16[1,384,4096]{2,1,0:T(8,128)(2,1)S(1)} copy-done((bf16[1,384,4096]{2,1,0:T(8,128)(2,1)S(1)}, bf16[1,384,4096]{2,1,0:T(8,128)(2,1)}, u32[]{:S(2)}) %copy-start.5) | copy-done | bytes 3145752
  92.3 1.5 shard_map.106.refs_4_
  93.8 0.2 collective-permute-start.7
  94.0 1.5 shard_map.107.dact_ref
  95.5 0.2 copy-done.2
  95.8 0.1 copy-done.17
  95.9 1.6 %shard_map.108 = (bf16[320,384]{1,0:T(8,128)(2,1)S(1)}, bf16[320,384]{1,0:T(8,128)(2,1)S(1)}, bf16[320,512]{1,0:T(8,128)(2,1)}, bf16[320,512]{1,0:T(8,128)(2,1)}) custom-call(s32[1]{0:T(128)} %bitcast.1.place_ref, f32[320,384]{1,0:T(8,128)S(1)} %shard_map.107.dact_ref, f32[320,384]{1,0:T(8,128)S(1)} %copy-done.15, f32[320,384]{1,0:T(8,128)S(1)} %copy-done.17, ...), custom_call_target="tpu_custom_call" | custom-call | flops 1006632960 | bytes 1966080 | tf_op jit(solution)/shard_map/pallas_call | solution.py:373
  97.6 0.1 collective-permute-start.13
  97.7 0.4 collective-permute-start.14
  98.1 0.9 shard_map.109.grad_ref
  99.0 0.5 collective-permute-done.13.refs_0_
  99.5 0.5 collective-permute-done.14.refs_1_
  100.1 2.9 %shard_map.111 = (bf16[2560,128]{1,0:T(8,128)(2,1)S(1)}, bf16[320,1024]{1,0:T(8,128)(2,1)}, f32[8,128]{1,0:T(8,128)S(1)}) custom-call(bf16[320,1024]{1,0:T(8,128)(2,1)S(1)} %copy-done.13, bf16[320,1024]{1,0:T(8,128)(2,1)} %collective-permute-done.7.near_ref, bf16[320,1024]{1,0:T(8,128)(2,1)} %collective-permute-done.8.after.far_ref, ...), custom_call_target="tpu_custom_call" | custom-call | flops 1000000 | bytes 3932160 | tf_op jit(solution)/shard_map/pallas_call | solution.py:373
  103.0 0.9 copy-done.11
  103.9 3.4 %collective-permute-start.16 = (bf16[320,1024]{1,0:T(8,128)(2,1)}, bf16[320,1024]{1,0:T(8,128)(2,1)}, u32[]{:S(2)}, u32[]{:S(2)}) collective-permute-start(bf16[320,1024]{1,0:T(8,128)(2,1)} %get-tuple-element.76), channel_id=1, source_target_pairs={{0,2},{1,3},{2,0},{3,1},{4,6},{5,7},{6,4},{7,5},{8,10},{9,11},{10,... | collective-permute-start | bytes 1966088 | tf_op jit(solution)/shard_map/ppermute | solution.py:533
  107.3 5.7 %all-to-all-start.3 = ((bf16[64,40,128]{2,1,0:T(8,128)(2,1)}), bf16[64,40,128]{2,1,0:T(8,128)(2,1)}, u32[]{:S(2)}, u32[]{:S(2)}) async-start(bf16[64,40,128]{2,1,0:T(8,128)(2,1)} %bitcast.39), calls=%async_computation.3 | async-start | bytes 1310720 | tf_op jit(solution)/shard_map/all_to_all | solution.py:421
  113.1 1.9 %copy-done.3 = bf16[1,4096,384]{2,1,0:T(8,128)(2,1)S(1)} copy-done((bf16[1,4096,384]{2,1,0:T(8,128)(2,1)S(1)}, bf16[1,4096,384]{2,1,0:T(8,128)(2,1)}, u32[]{:S(2)}) %copy-start.3) | copy-done | bytes 3145752
  114.9 0.9 copy-done.10
  115.9 1.7 %shard_map.113 = (bf16[320,1024]{1,0:T(8,128)(2,1)}, bf16[320,1024]{1,0:T(8,128)(2,1)S(1)}) custom-call(s32[1]{0:T(128)} %bitcast.1.place_ref, bf16[320,384]{1,0:T(8,128)(2,1)S(1)} %copy-done.8, bf16[320,384]{1,0:T(8,128)(2,1)S(1)} %copy-done.10, bf16[4,1024,384]{2,1,0:T(8,128)(2,1)S(1)} %bitcast.23, bf16[4,1024,384]{2,1,0:T(8,128)(2,1)S(1)} %bitcast.30, ...), custom_call_target="tpu_custom_call" | custom-call | flops 1006632960 | bytes 1966080 | tf_op jit(solution)/shard_map/pallas_call | solution.py:373
  117.6 11.5 %collective-permute-done.16.after.far_ref = bf16[320,1024]{1,0:T(8,128)(2,1)} collective-permute-done((bf16[320,1024]{1,0:T(8,128)(2,1)}, bf16[320,1024]{1,0:T(8,128)(2,1)}, u32[]{:S(2)}, u32[]{:S(2)}) %collective-permute-start.16) | collective-permute-done | bytes 655392 | tf_op jit(solution)/shard_map/ppermute | solution.py:533
  129.2 3.1 %shard_map.115 = (bf16[2560,128]{1,0:T(8,128)(2,1)}, f32[8,128]{1,0:T(8,128)}) custom-call(bf16[320,1024]{1,0:T(8,128)(2,1)S(1)} %get-tuple-element.74.keep_ref, bf16[320,1024]{1,0:T(8,128)(2,1)} %collective-permute-done.15.near_ref, bf16[320,1024]{1,0:T(8,128)(2,1)} %collective-permute-done.16.after.far_ref, f32[8,128]{1,0:T(8,128)S(1)} %shard_map.114.after), custom_call_target="tpu_custom_call" | custom-call | flops 1000000 | bytes 1966080 | tf_op jit(solution)/shard_map/pallas_call | solution.py:373
  132.3 1.2 all-to-all-done.3
  133.5 5.8 %all-to-all-start.4 = ((bf16[64,40,128]{2,1,0:T(8,128)(2,1)}), bf16[64,40,128]{2,1,0:T(8,128)(2,1)S(1)}, u32[]{:S(2)}, u32[]{:S(2)}) async-start(bf16[64,40,128]{2,1,0:T(8,128)(2,1)} %bitcast.15), calls=%async_computation.4 | async-start | bytes 1310720 | tf_op jit(solution)/shard_map/all_to_all | solution.py:421
  139.3 0.1 copy.11.gates_ref
  139.4 2.7 %shard_map.112 = (bf16[128,1024]{1,0:T(8,128)(2,1)}, f32[128,2]{1,0:T(8,128)S(1)}) custom-call(s32[2,128]{1,0:T(2,128)S(1)} %bitcast.42, f32[128,2]{1,0:T(8,128)S(1)} %copy.11.gates_ref, bf16[128,1024]{1,0:T(8,128)(2,1)S(1)} %copy-done.19, bf16[2560,128]{1,0:T(8,128)(2,1)} %bitcast.14.rows_ref), custom_call_target="tpu_custom_call" | custom-call | flops 100000000 | bytes 1966080 | tf_op jit(solution)/shard_map/pallas_call | solution.py:373
  142.1 1.3 collective-permute-done.17
  143.4 0.8 collective-permute-start.18
  144.3 5.6 %collective-permute-done.18 = f32[128,2]{1,0:T(8,128)S(1)} collective-permute-done((f32[128,2]{1,0:T(8,128)S(1)}, f32[128,2]{1,0:T(8,128)S(1)}, u32[]{:S(2)}, u32[]{:S(2)}) %collective-permute-start.18) | collective-permute-done | bytes 1056 | tf_op jit(solution)/shard_map/ppermute | solution.py:552
  149.9 0.6 copy.12
  150.6 8.8 %all-to-all-done.4 = bf16[64,40,128]{2,1,0:T(8,128)(2,1)S(1)} async-done(((bf16[64,40,128]{2,1,0:T(8,128)(2,1)}), bf16[64,40,128]{2,1,0:T(8,128)(2,1)S(1)}, u32[]{:S(2)}, u32[]{:S(2)}) %all-to-all-start.4) | async-done | bytes 655392 | tf_op jit(solution)/shard_map/all_to_all | solution.py:421
  159.3 1.4 shard_map.116
  (60 shorter events, 0.5 us)
Async XLA Ops:
  0.6 57.6 %copy-start = (bf16[1,4096,384]{2,1,0:T(8,128)(2,1)S(1)}, bf16[1,4096,384]{2,1,0:T(8,128)(2,1)}, u32[]{:S(2)}) copy-start(bf16[1,4096,384]{2,1,0:T(8,128)(2,1)} %param.11) | copy-start | bytes 9437188
  0.6 12.6 %all-to-all-start = ((bf16[8,128,128]{2,1,0:T(8,128)(2,1)}), bf16[8,128,128]{2,1,0:T(8,128)(2,1)S(1)}, u32[]{:S(2)}, u32[]{:S(2)}) async-start(bf16[8,128,128]{2,1,0:T(8,128)(2,1)} %bitcast.45), calls=%async_computation | async-start | bytes 524288 | tf_op jit(solution)/shard_map/all_to_all | solution.py:440
  6.0 0.9 copy-start.18
  7.0 0.7 copy-start.20
  7.6 0.7 copy-start.23
  9.0 1.1 copy-start.6
  13.2 0.7 copy-start.21
  44.7 19.4 %collective-permute-start = (bf16[2560,128]{1,0:T(8,128)(2,1)}, bf16[2560,128]{1,0:T(8,128)(2,1)}, u32[]{:S(2)}, u32[]{:S(2)}) collective-permute-start(bf16[2560,128]{1,0:T(8,128)(2,1)} %bitcast.5.x_ref.x0), channel_id=1, source_target_pairs={{0,2},{1,3},{2,0},{3,1},{4,6},{5,7},{6,4},{7,5},{8,10},{9,11},{10,... | collective-permute-start | bytes 1966088 | tf_op jit(solution)/shard_map/ppermute | solution.py:453
  45.5 42.5 %all-to-all-start.2 = ((bf16[128,40,128]{2,1,0:T(8,128)(2,1)}), bf16[128,40,128]{2,1,0:T(8,128)(2,1)}, u32[]{:S(2)}, u32[]{:S(2)}) async-start(bf16[128,40,128]{2,1,0:T(8,128)(2,1)} %bitcast.38), calls=%async_computation.2 | async-start | bytes 2621440 | tf_op jit(solution)/shard_map/all_to_all | solution.py:460
  57.2 5.0 %collective-permute-start.1 = (bf16[640,128]{1,0:T(8,128)(2,1)}, bf16[640,128]{1,0:T(8,128)(2,1)S(1)}, u32[]{:S(2)}, u32[]{:S(2)}) collective-permute-start(bf16[640,128]{1,0:T(8,128)(2,1)} %get-tuple-element.42), channel_id=1, source_target_pairs={{0,1},{1,0},{2,3},{3,2},{4,5},{5,4},{6,7},{7,6},{8,9},{9,8},{10,11... | collective-permute-start | bytes 491528 | tf_op jit(solution)/shard_map/ppermute | solution.py:471
  57.2 5.0 %collective-permute-start.2 = (bf16[640,128]{1,0:T(8,128)(2,1)}, bf16[640,128]{1,0:T(8,128)(2,1)S(1)}, u32[]{:S(2)}, u32[]{:S(2)}) collective-permute-start(bf16[640,128]{1,0:T(8,128)(2,1)} %get-tuple-element.43), channel_id=1, source_target_pairs={{0,1},{1,0},{2,3},{3,2},{4,5},{5,4},{6,7},{7,6},{8,9},{9,8},{10,11... | collective-permute-start | bytes 491528 | tf_op jit(solution)/shard_map/ppermute | solution.py:471
  57.7 4.5 %collective-permute-start.3 = (bf16[640,128]{1,0:T(8,128)(2,1)}, bf16[640,128]{1,0:T(8,128)(2,1)}, u32[]{:S(2)}, u32[]{:S(2)}) collective-permute-start(bf16[640,128]{1,0:T(8,128)(2,1)} %get-tuple-element.44), channel_id=1, source_target_pairs={{0,1},{1,0},{2,3},{3,2},{4,5},{5,4},{6,7},{7,6},{8,9},{9,8},{10,11... | collective-permute-start | bytes 491528 | tf_op jit(solution)/shard_map/ppermute | solution.py:471
  57.7 4.5 %collective-permute-start.4 = (bf16[640,128]{1,0:T(8,128)(2,1)}, bf16[640,128]{1,0:T(8,128)(2,1)}, u32[]{:S(2)}, u32[]{:S(2)}) collective-permute-start(bf16[640,128]{1,0:T(8,128)(2,1)} %get-tuple-element.45), channel_id=1, source_target_pairs={{0,1},{1,0},{2,3},{3,2},{4,5},{5,4},{6,7},{7,6},{8,9},{9,8},{10,11... | collective-permute-start | bytes 491528 | tf_op jit(solution)/shard_map/ppermute | solution.py:471
  58.2 1.9 %copy-start.1 = (bf16[1,4096,384]{2,1,0:T(8,128)(2,1)S(1)}, bf16[1,4096,384]{2,1,0:T(8,128)(2,1)}, u32[]{:S(2)}) copy-start(bf16[1,4096,384]{2,1,0:T(8,128)(2,1)} %param.12) | copy-start | bytes 9437188
  64.1 2.4 %collective-permute-start.5 = (bf16[2560,128]{1,0:T(8,128)(2,1)}, bf16[2560,128]{1,0:T(8,128)(2,1)S(1)}, u32[]{:S(2)}, u32[]{:S(2)}) collective-permute-start(bf16[2560,128]{1,0:T(8,128)(2,1)} %shard_map.99.x2), channel_id=1, source_target_pairs={{0,1},{1,0},{2,3},{3,2},{4,5},{5,4},{6,7},{7,6},{8,9},{9,8},{10,11... | collective-permute-start | bytes 1966088 | tf_op jit(solution)/shard_map/ppermute | solution.py:477
  64.2 2.3 %copy-start.4 = (bf16[1,384,4096]{2,1,0:T(8,128)(2,1)S(1)}, bf16[1,384,4096]{2,1,0:T(8,128)(2,1)}, u32[]{:S(2)}) copy-start(bf16[1,384,4096]{2,1,0:T(8,128)(2,1)} %param.13) | copy-start | bytes 9437188
  68.0 4.1 %copy-start.14 = (f32[320,384]{1,0:T(8,128)}, f32[320,384]{1,0:T(8,128)S(1)}, u32[]{:S(2)}) copy-start(f32[320,384]{1,0:T(8,128)S(1)} %get-tuple-element.65.silu_ref) | copy-start | bytes 1474564
  68.0 4.1 %copy-start.16 = (f32[320,384]{1,0:T(8,128)}, f32[320,384]{1,0:T(8,128)S(1)}, u32[]{:S(2)}) copy-start(f32[320,384]{1,0:T(8,128)S(1)} %get-tuple-element.66.dsilu_ref) | copy-start | bytes 1474564
  68.1 2.4 %collective-permute-start.6 = (bf16[320,1024]{1,0:T(8,128)(2,1)S(1)}, bf16[320,1024]{1,0:T(8,128)(2,1)S(1)}, u32[]{:S(2)}, u32[]{:S(2)}) collective-permute-start(bf16[320,1024]{1,0:T(8,128)(2,1)S(1)} %get-tuple-element.54), channel_id=1, source_target_pairs={{0,1},{1,0},{2,3},{3,2},{4,5},{5,4},{6,7},{7,6},{8,9},{9,8},{10,11... | collective-permute-start | bytes 1966088 | tf_op jit(solution)/shard_map/ppermute | solution.py:487
  71.5 27.5 %collective-permute-start.8 = (bf16[320,1024]{1,0:T(8,128)(2,1)}, bf16[320,1024]{1,0:T(8,128)(2,1)}, u32[]{:S(2)}, u32[]{:S(2)}) collective-permute-start(bf16[320,1024]{1,0:T(8,128)(2,1)} %get-tuple-element.58), channel_id=1, source_target_pairs={{0,2},{1,3},{2,0},{3,1},{4,6},{5,7},{6,4},{7,5},{8,10},{9,11},{10,... | collective-permute-start | bytes 1966088 | tf_op jit(solution)/shard_map/ppermute | solution.py:496
  73.5 0.8 copy-start.12
  89.3 4.5 %collective-permute-start.10 = (bf16[1280,128]{1,0:T(8,128)(2,1)S(1)}, bf16[1280,128]{1,0:T(8,128)(2,1)S(1)}, u32[]{:S(2)}, u32[]{:S(2)}) collective-permute-start(bf16[1280,128]{1,0:T(8,128)(2,1)S(1)} %get-tuple-element.62.refs_1_), channel_id=1, source_target_pairs={{0,1},{1,0},{2,3},{3,2},{4,5},{5,4},{6,7},{7,6},{8,9},{9,8},{10,11... | collective-permute-start | bytes 983048 | tf_op jit(solution)/shard_map/ppermute | solution.py:506
  89.4 4.6 %collective-permute-start.11 = (bf16[1280,128]{1,0:T(8,128)(2,1)S(1)}, bf16[1280,128]{1,0:T(8,128)(2,1)S(1)}, u32[]{:S(2)}, u32[]{:S(2)}) collective-permute-start(bf16[1280,128]{1,0:T(8,128)(2,1)S(1)} %get-tuple-element.63.refs_2_), channel_id=1, source_target_pairs={{0,1},{1,0},{2,3},{3,2},{4,5},{5,4},{6,7},{7,6},{8,9},{9,8},{10,11... | collective-permute-start | bytes 983048 | tf_op jit(solution)/shard_map/ppermute | solution.py:506
  89.9 4.1 %collective-permute-start.12 = (bf16[1280,128]{1,0:T(8,128)(2,1)S(1)}, bf16[1280,128]{1,0:T(8,128)(2,1)S(1)}, u32[]{:S(2)}, u32[]{:S(2)}) collective-permute-start(bf16[1280,128]{1,0:T(8,128)(2,1)S(1)} %get-tuple-element.64.refs_3_), channel_id=1, source_target_pairs={{0,1},{1,0},{2,3},{3,2},{4,5},{5,4},{6,7},{7,6},{8,9},{9,8},{10,11... | collective-permute-start | bytes 983048 | tf_op jit(solution)/shard_map/ppermute | solution.py:506
  90.0 4.0 %collective-permute-start.9 = (bf16[1280,128]{1,0:T(8,128)(2,1)S(1)}, bf16[1280,128]{1,0:T(8,128)(2,1)S(1)}, u32[]{:S(2)}, u32[]{:S(2)}) collective-permute-start(bf16[1280,128]{1,0:T(8,128)(2,1)S(1)} %get-tuple-element.61.refs_0_), channel_id=1, source_target_pairs={{0,1},{1,0},{2,3},{3,2},{4,5},{5,4},{6,7},{7,6},{8,9},{9,8},{10,11... | collective-permute-start | bytes 983048 | tf_op jit(solution)/shard_map/ppermute | solution.py:506
  90.4 1.9 %copy-start.5 = (bf16[1,384,4096]{2,1,0:T(8,128)(2,1)S(1)}, bf16[1,384,4096]{2,1,0:T(8,128)(2,1)}, u32[]{:S(2)}) copy-start(bf16[1,384,4096]{2,1,0:T(8,128)(2,1)} %param.13) | copy-start | bytes 9437188
  93.8 1.9 %copy-start.2 = (bf16[1,4096,384]{2,1,0:T(8,128)(2,1)S(1)}, bf16[1,4096,384]{2,1,0:T(8,128)(2,1)}, u32[]{:S(2)}) copy-start(bf16[1,4096,384]{2,1,0:T(8,128)(2,1)} %param.12) | copy-start | bytes 9437188
  93.8 2.0 %copy-start.15 = (f32[320,384]{1,0:T(8,128)S(1)}, f32[320,384]{1,0:T(8,128)}, u32[]{:S(2)}) copy-start(f32[320,384]{1,0:T(8,128)} %copy-done.14) | copy-start | bytes 1474564
  93.8 2.1 %copy-start.17 = (f32[320,384]{1,0:T(8,128)S(1)}, f32[320,384]{1,0:T(8,128)}, u32[]{:S(2)}) copy-start(f32[320,384]{1,0:T(8,128)} %copy-done.16) | copy-start | bytes 1474564
  93.8 5.2 %collective-permute-start.7 = (bf16[320,1024]{1,0:T(8,128)(2,1)}, bf16[320,1024]{1,0:T(8,128)(2,1)}, u32[]{:S(2)}, u32[]{:S(2)}) collective-permute-start(bf16[320,1024]{1,0:T(8,128)(2,1)} %get-tuple-element.57), channel_id=1, source_target_pairs={{0,1},{1,0},{2,3},{3,2},{4,5},{5,4},{6,7},{7,6},{8,9},{9,8},{10,11... | collective-permute-start | bytes 1966088 | tf_op jit(solution)/shard_map/ppermute | solution.py:525
  97.6 1.4 copy-start.7
  97.6 1.4 copy-start.9
  97.6 2.0 %collective-permute-start.13 = (bf16[320,512]{1,0:T(8,128)(2,1)}, bf16[320,512]{1,0:T(8,128)(2,1)}, u32[]{:S(2)}, u32[]{:S(2)}) collective-permute-start(bf16[320,512]{1,0:T(8,128)(2,1)} %get-tuple-element.69), channel_id=1, source_target_pairs={{0,1},{1,0},{2,3},{3,2},{4,5},{5,4},{6,7},{7,6},{8,9},{9,8},{10,11... | collective-permute-start | bytes 983048 | tf_op jit(solution)/shard_map/ppermute | solution.py:524
  97.7 2.3 %collective-permute-start.14 = (bf16[320,512]{1,0:T(8,128)(2,1)}, bf16[320,512]{1,0:T(8,128)(2,1)}, u32[]{:S(2)}, u32[]{:S(2)}) collective-permute-start(bf16[320,512]{1,0:T(8,128)(2,1)} %get-tuple-element.70), channel_id=1, source_target_pairs={{0,1},{1,0},{2,3},{3,2},{4,5},{5,4},{6,7},{7,6},{8,9},{9,8},{10,11... | collective-permute-start | bytes 983048 | tf_op jit(solution)/shard_map/ppermute | solution.py:524
  99.0 1.1 copy-start.13
  99.0 14.0 %copy-start.8 = (bf16[320,384]{1,0:T(8,128)(2,1)S(1)}, bf16[320,384]{1,0:T(8,128)(2,1)}, u32[]{:S(2)}) copy-start(bf16[320,384]{1,0:T(8,128)(2,1)} %copy-done.7) | copy-start | bytes 737284
  103.0 0.9 copy-start.11
  103.9 25.2 %collective-permute-start.16 = (bf16[320,1024]{1,0:T(8,128)(2,1)}, bf16[320,1024]{1,0:T(8,128)(2,1)}, u32[]{:S(2)}, u32[]{:S(2)}) collective-permute-start(bf16[320,1024]{1,0:T(8,128)(2,1)} %get-tuple-element.76), channel_id=1, source_target_pairs={{0,2},{1,3},{2,0},{3,1},{4,6},{5,7},{6,4},{7,5},{8,10},{9,11},{10,... | collective-permute-start | bytes 1966088 | tf_op jit(solution)/shard_map/ppermute | solution.py:533
  107.3 26.2 %all-to-all-start.3 = ((bf16[64,40,128]{2,1,0:T(8,128)(2,1)}), bf16[64,40,128]{2,1,0:T(8,128)(2,1)}, u32[]{:S(2)}, u32[]{:S(2)}) async-start(bf16[64,40,128]{2,1,0:T(8,128)(2,1)} %bitcast.39), calls=%async_computation.3 | async-start | bytes 1310720 | tf_op jit(solution)/shard_map/all_to_all | solution.py:421
  113.0 1.9 %copy-start.3 = (bf16[1,4096,384]{2,1,0:T(8,128)(2,1)S(1)}, bf16[1,4096,384]{2,1,0:T(8,128)(2,1)}, u32[]{:S(2)}) copy-start(bf16[1,4096,384]{2,1,0:T(8,128)(2,1)} %param.12) | copy-start | bytes 9437188
  114.9 0.9 copy-start.10
  117.6 11.5 %collective-permute-start.15 = (bf16[320,1024]{1,0:T(8,128)(2,1)}, bf16[320,1024]{1,0:T(8,128)(2,1)}, u32[]{:S(2)}, u32[]{:S(2)}) collective-permute-start(bf16[320,1024]{1,0:T(8,128)(2,1)} %get-tuple-element.75), channel_id=1, source_target_pairs={{0,1},{1,0},{2,3},{3,2},{4,5},{5,4},{6,7},{7,6},{8,9},{9,8},{10,11... | collective-permute-start | bytes 1966088 | tf_op jit(solution)/shard_map/ppermute | solution.py:538
  129.1 10.2 %copy-start.24 = (f32[128,2]{0,1:T(2,128)S(1)}, f32[128,2]{0,1:T(2,128)}, u32[]{:S(2)}) copy-start(f32[128,2]{0,1:T(2,128)} %param.10) | copy-start | bytes 3076
  129.1 10.3 %copy-start.19 = (bf16[128,1024]{1,0:T(8,128)(2,1)S(1)}, bf16[128,1024]{1,0:T(8,128)(2,1)}, u32[]{:S(2)}) copy-start(bf16[128,1024]{1,0:T(8,128)(2,1)} %cot_ref.3) | copy-start | bytes 786436
  129.1 10.3 %copy-start.22 = (s32[128,2]{0,1:T(2,128)S(1)}, s32[128,2]{0,1:T(2,128)}, u32[]{:S(2)}) copy-start(s32[128,2]{0,1:T(2,128)} %param.9) | copy-start | bytes 3076
  133.5 25.9 %all-to-all-start.4 = ((bf16[64,40,128]{2,1,0:T(8,128)(2,1)}), bf16[64,40,128]{2,1,0:T(8,128)(2,1)S(1)}, u32[]{:S(2)}, u32[]{:S(2)}) async-start(bf16[64,40,128]{2,1,0:T(8,128)(2,1)} %bitcast.15), calls=%async_computation.4 | async-start | bytes 1310720 | tf_op jit(solution)/shard_map/all_to_all | solution.py:421
  142.1 1.3 collective-permute-start.17
  143.4 6.5 %collective-permute-start.18 = (f32[128,2]{1,0:T(8,128)S(1)}, f32[128,2]{1,0:T(8,128)S(1)}, u32[]{:S(2)}, u32[]{:S(2)}) collective-permute-start(f32[128,2]{1,0:T(8,128)S(1)} %add.6), channel_id=1, source_target_pairs={{0,2},{1,3},{2,0},{3,1},{4,6},{5,7},{6,4},{7,5},{8,10},{9,11},{10,... | collective-permute-start | bytes 3080 | tf_op jit(solution)/shard_map/ppermute | solution.py:552

commit v6 on v5

--- a/solution.py
+++ b/solution.py
@@ -283,13 +283,16 @@
     keep_ref[...] = grad_block(dgate_ref, dup_ref, gate, up, place_ref[0] ^ 2).astype(BF)
 
 
-def own_out_kernel(place_ref, act_ref, down, after, send_ref, keep_ref, token_ref):
+def own_out_kernel(place_ref, act_ref, down, after, keep_ref, token_ref, *sends):
     token_ref[...] = jnp.zeros_like(token_ref)
     ep = place_ref[0]
-    width = send_ref.shape[1]
-    send_ref[...] = jnp.dot(
+    width = keep_ref.shape[1]
+    send = jnp.dot(
         act_ref[...], column_block(down, ep ^ 1, width), preferred_element_type=F32
     ).astype(BF)
+    for i, send_ref in enumerate(sends):
+        part = send_ref.shape[1]
+        send_ref[...] = send[:, i * part : (i + 1) * part]
     keep_ref[...] = jnp.dot(
         act_ref[...], column_block(down, ep, width), preferred_element_type=F32
     ).astype(BF)
@@ -306,7 +309,8 @@
     out_ref[...] = (keep_ref[...].astype(F32) + came_ref[...].astype(F32)).astype(BF)
 
 
-def finish_out_kernel(keep_ref, near_ref, far_ref, grad_ref, *refs):
+def finish_out_kernel(pieces, keep_ref, far_ref, grad_ref, *refs):
+    near, refs = refs[:pieces], refs[pieces:]
     *came, after, out_ref, sum_ref, token_ref, wide_ref, sum_buf, rows_buf, sems = refs
     token_ref[...] = jnp.zeros_like(token_ref)
     for i, ref in enumerate(came):
@@ -317,7 +321,9 @@
 
     def block(f):
         cols = slice(f * LANES, (f + 1) * LANES)
-        parts = [ref[:, cols].astype(F32) for ref in (keep_ref, near_ref, far_ref)]
+        at = f * LANES % near[0].shape[1]
+        beside = near[f * LANES // near[0].shape[1]][:, at : at + LANES]
+        parts = [part.astype(F32) for part in (keep_ref[:, cols], beside, far_ref[:, cols])]
         return parts[0] + parts[1] + parts[2]
 
     tile_rows(block, keep_ref.shape[1] // LANES, wide_ref, rows_buf)
@@ -494,8 +500,9 @@
         out_keep, out_came, p_token,
     )
     out_far = lax.ppermute(out_sum, "ep", far)
-    out_send2, out_keep2, own_token = call(
-        own_out_kernel, [SMEM, VMEM, VMEM, ANY], [send_t, keep_t, token], [],
+    out_keep2, own_token, *out_sends2 = call(
+        own_out_kernel, [SMEM, VMEM, VMEM, ANY],
+        [keep_t, token] + [shape((slots, width // SUMS), BF)] * SUMS, [],
         2 * dot_flops, moved, place, act, down_w, out_token,
     )
     cot_here = call(
@@ -522,12 +529,13 @@
         place, d_gate, d_up, gate_q, up_q,
     )
     grad_came = [lax.ppermute(send, "ep", near) for send in grad_sends]
-    out_near = lax.ppermute(out_send2, "ep", near)
+    out_near = [lax.ppermute(send, "ep", near) for send in out_sends2]
     out_rows, grad_sum, g_token = call(
-        finish_out_kernel, [VMEM] * (SUMS + 4) + [ANY], [rows_t, send_t, token],
+        functools.partial(finish_out_kernel, SUMS), [VMEM] * (2 * SUMS + 3) + [ANY],
+        [rows_t, send_t, token],
         [wide, pltpu.VMEM((slots, width), BF), pltpu.VMEM((tiled, LANES), BF),
          pltpu.SemaphoreType.DMA((2,))],
-        10**6, 2 * moved, out_keep2, out_near, out_far, grad_keep, *grad_came, far_token,
+        10**6, 2 * moved, out_keep2, out_far, grad_keep, *out_near, *grad_came, far_token,
         place_outs=[ANY, ANY, VMEM],
     )
     grad_far = lax.ppermute(grad_sum, "ep", far)

time: 162 us -> 162 us (level)
  transfers between devices with their start and end apart: 23 -> 24, of which waited for: 11 -> 11; matrix products, arithmetic and copies ran while one was open for 0% -> 0% of each run, Pallas kernels for 17% -> 17%
where the time goes in v6:
time: 162 us; the launch traced here: 161 us
  waiting for transfers between devices  47.9 us (30%)
  starting transfers between devices  36.1 us (22%)
  Pallas kernels  32.3 us (20%)
  blocking collectives  30.2 us (19%)
  local copies, waits for them, and re-layouts  13.2 us (8%)
    pallas_call x22, Pallas kernels, call(): pl.pallas_call(kernel, out_shape=outs, in_specs=specs, out_specs=place_ou...  32.3 us
    all_to_all x1, blocking collectives, exchange(): lax.all_to_all(rows.reshape(experts, capacity * blocks, LANES), ('cp', 't...  30.2 us
    all_to_all x1, waiting for transfers between devices, local(): lax.all_to_all(cot_rows.reshape(2 * experts, capacity * blocks, LANES), (...  13.6 us
    unnamed x52, local copies, waits for them, and re-layouts  13.2 us
    all_to_all x2, starting transfers between devices, exchange(): lax.all_to_all(rows.reshape(experts, capacity * blocks, LANES), ('cp', 't...  11.5 us
    ppermute x1, waiting for transfers between devices, local(): grad_far = lax.ppermute(grad_sum, 'ep', far)  11.4 us
    all_to_all x2, waiting for transfers between devices, exchange(): lax.all_to_all(rows.reshape(experts, capacity * blocks, LANES), ('cp', 't...  10.4 us
    all_to_all x1, starting transfers between devices, local(): lax.all_to_all(cot_rows.reshape(2 * experts, capacity * blocks, LANES), (...  9.67 us
  transfers between devices with their start and end apart: 24, of which 11 were waited for; matrix products, arithmetic and copies ran while one was open for 0% of the time, Pallas kernels for 17%

profile of v6, /device:TPU:4, one launch (start us, length us, event | category | flops | bytes accessed | tf_op | source)
XLA Modules:
  0.0 160.9 jit_solution(1056209069661472364)
XLA Ops:
  0.6 5.4 %all-to-all-start = ((bf16[8,128,128]{2,1,0:T(8,128)(2,1)}), bf16[8,128,128]{2,1,0:T(8,128)(2,1)S(1)}, u32[]{:S(2)}, u32[]{:S(2)}) async-start(bf16[8,128,128]{2,1,0:T(8,128)(2,1)} %bitcast.45), calls=%async_computation | async-start | bytes 524288 | tf_op jit(solution)/shard_map/all_to_all | solution.py:446
  6.0 0.9 copy-done.18
  7.0 0.7 copy-done.20
  7.7 0.7 copy-done.23
  8.3 0.6 shard_map.94
  9.0 1.1 copy-done.6
  10.1 3.2 %all-to-all-done.x_ref = bf16[8,128,128]{2,1,0:T(8,128)(2,1)S(1)} async-done(((bf16[8,128,128]{2,1,0:T(8,128)(2,1)}), bf16[8,128,128]{2,1,0:T(8,128)(2,1)S(1)}, u32[]{:S(2)}, u32[]{:S(2)}) %all-to-all-start) | async-done | bytes 262176 | tf_op jit(solution)/shard_map/all_to_all | solution.py:446
  13.2 0.7 copy-done.21
  13.9 0.6 shard_map.95
  14.5 30.2 %all_to_all.25 = bf16[64,40,128]{2,1,0:T(8,128)(2,1)} all-to-all(bf16[64,40,128]{2,1,0:T(8,128)(2,1)S(1)} %bitcast.37), channel_id=1, replica_groups=mesh['cp'=8,'tp'=8,'ep'=4] {'cp','tp'}, dimensions={0} | all-to-all | bytes 1310720 | tf_op jit(solution)/shard_map/all_to_all | solution.py:427
  44.7 0.8 collective-permute-start
  45.5 9.7 %all-to-all-start.2 = ((bf16[128,40,128]{2,1,0:T(8,128)(2,1)}), bf16[128,40,128]{2,1,0:T(8,128)(2,1)}, u32[]{:S(2)}, u32[]{:S(2)}) async-start(bf16[128,40,128]{2,1,0:T(8,128)(2,1)} %bitcast.38), calls=%async_computation.2 | async-start | bytes 2621440 | tf_op jit(solution)/shard_map/all_to_all | solution.py:466
  55.2 1.9 %shard_map.96 = (bf16[640,128]{1,0:T(8,128)(2,1)}, bf16[640,128]{1,0:T(8,128)(2,1)}, bf16[640,128]{1,0:T(8,128)(2,1)}, bf16[640,128]{1,0:T(8,128)(2,1)}) custom-call(bf16[2560,128]{1,0:T(8,128)(2,1)} %bitcast.5.x_ref.x0), custom_call_target="tpu_custom_call" | custom-call | flops 1000000 | bytes 1966080 | tf_op jit(solution)/shard_map/pallas_call | solution.py:379
  57.2 0.5 collective-permute-start.2
  57.7 0.5 collective-permute-start.4
  58.2 1.9 %copy-done.1 = bf16[1,4096,384]{2,1,0:T(8,128)(2,1)S(1)} copy-done((bf16[1,4096,384]{2,1,0:T(8,128)(2,1)S(1)}, bf16[1,4096,384]{2,1,0:T(8,128)(2,1)}, u32[]{:S(2)}) %copy-start.1) | copy-done | bytes 3145752
  60.1 2.0 %shard_map.97 = (f32[320,384]{1,0:T(8,128)S(1)}, f32[320,384]{1,0:T(8,128)S(1)}) custom-call(s32[1]{0:T(128)} %bitcast.1.place_ref, bf16[2560,128]{1,0:T(8,128)(2,1)} %bitcast.5.x_ref.x0, bf16[8,4,128,384]{3,2,1,0:T(8,128)(2,1)S(1)} %bitcast.17, bf16[8,4,128,384]{3,2,1,0:T(8,128)(2,1)S(1)} %bitcast.24), custom_call_target="tpu_custom_call" | custom-call | flops 503316480 | bytes 1966080 | tf_op jit(solution)/shard_map/pallas_call | solution.py:379
  62.2 2.0 %shard_map.98 = (f32[320,384]{1,0:T(8,128)S(1)}, f32[320,384]{1,0:T(8,128)S(1)}, f32[8,128]{1,0:T(8,128)S(1)}) custom-call(s32[1]{0:T(128)} %bitcast.1.place_ref, bf16[640,128]{1,0:T(8,128)(2,1)S(1)} %collective-permute-done.1.refs_0_, bf16[640,128]{1,0:T(8,128)(2,1)S(1)} %collective-permute-done.2.refs_1_, bf16[640,128]{1,0:T(8,128)(2,1)} %collective-permute-done.3.refs_2_, ...), custom_call_target="tpu_custom_call" | custom-call | flops 503316480 | bytes 1966080 | tf_op jit(solution)/shard_map/pallas_call | solution.py:379
  64.1 0.1 collective-permute-start.5
  64.3 2.2 %shard_map.100 = (f32[320,384]{1,0:T(8,128)S(1)}, f32[320,384]{1,0:T(8,128)S(1)}) custom-call(s32[1]{0:T(128)} %bitcast.1.place_ref, bf16[2560,128]{1,0:T(8,128)(2,1)} %shard_map.99.x2, f32[320,384]{1,0:T(8,128)S(1)} %get-tuple-element.50.g_in, f32[320,384]{1,0:T(8,128)S(1)} %get-tuple-element.51.u_in, bf16[8,4,128,384]{3,2,1,0:T(8,128)(2,1)S(1)} %bitcast.19, ...), custom_call_target="tpu_custom_call" | custom-call | flops 12000000000 | bytes 1966080 | tf_op jit(solution)/shard_map/pallas_call | solution.py:379
  66.5 1.5 shard_map.101
  68.1 0.7 collective-permute-start.6
  68.8 0.5 shard_map.102.keep_ref
  69.3 1.2 collective-permute-done.6.came_ref
  70.5 1.0 shard_map.103
  71.5 0.7 collective-permute-start.7
  72.2 1.4 shard_map.104
  73.6 0.8 copy-done.12
  74.4 13.6 %all-to-all-done.2 = bf16[128,40,128]{2,1,0:T(8,128)(2,1)} async-done(((bf16[128,40,128]{2,1,0:T(8,128)(2,1)}), bf16[128,40,128]{2,1,0:T(8,128)(2,1)}, u32[]{:S(2)}, u32[]{:S(2)}) %all-to-all-start.2) | async-done | bytes 1310752 | tf_op jit(solution)/shard_map/all_to_all | solution.py:466
  88.0 1.3 shard_map.105
  89.3 0.1 collective-permute-start.10
  89.4 0.5 collective-permute-start.11
  89.9 0.1 collective-permute-start.8
  90.0 0.4 collective-permute-start.9
  90.4 1.9 %copy-done.5 = bf16[1,384,4096]{2,1,0:T(8,128)(2,1)S(1)} copy-done((bf16[1,384,4096]{2,1,0:T(8,128)(2,1)S(1)}, bf16[1,384,4096]{2,1,0:T(8,128)(2,1)}, u32[]{:S(2)}) %copy-start.5) | copy-done | bytes 3145752
  92.3 1.5 shard_map.106.refs_4_
  93.8 0.2 collective-permute-start.12
  94.0 0.4 collective-permute-start.13
  94.4 1.5 shard_map.107.dact_ref
  95.9 1.6 %shard_map.108 = (bf16[320,384]{1,0:T(8,128)(2,1)S(1)}, bf16[320,384]{1,0:T(8,128)(2,1)S(1)}, bf16[320,512]{1,0:T(8,128)(2,1)}, bf16[320,512]{1,0:T(8,128)(2,1)}) custom-call(s32[1]{0:T(128)} %bitcast.1.place_ref, f32[320,384]{1,0:T(8,128)S(1)} %shard_map.107.dact_ref, f32[320,384]{1,0:T(8,128)S(1)} %copy-done.15, f32[320,384]{1,0:T(8,128)S(1)} %copy-done.17, ...), custom_call_target="tpu_custom_call" | custom-call | flops 1006632960 | bytes 1966080 | tf_op jit(solution)/shard_map/pallas_call | solution.py:379
  97.6 0.1 collective-permute-start.14
  97.7 0.4 collective-permute-start.15
  98.1 0.9 shard_map.109.grad_ref
  99.0 0.5 collective-permute-done.14.refs_2_
  99.5 0.5 collective-permute-done.15.refs_3_
  100.1 2.9 %shard_map.111 = (bf16[2560,128]{1,0:T(8,128)(2,1)S(1)}, bf16[320,1024]{1,0:T(8,128)(2,1)}, f32[8,128]{1,0:T(8,128)S(1)}) custom-call(bf16[320,1024]{1,0:T(8,128)(2,1)S(1)} %copy-done.13, bf16[320,1024]{1,0:T(8,128)(2,1)} %collective-permute-done.7.after.far_ref, bf16[320,1024]{1,0:T(8,128)(2,1)S(1)} %shard_map.109.grad_ref, ...), custom_call_target="tpu_custom_call" | custom-call | flops 1000000 | bytes 3932160 | tf_op jit(solution)/shard_map/pallas_call | solution.py:379
  102.9 0.8 copy-done.11
  103.8 3.4 %collective-permute-start.17 = (bf16[320,1024]{1,0:T(8,128)(2,1)}, bf16[320,1024]{1,0:T(8,128)(2,1)}, u32[]{:S(2)}, u32[]{:S(2)}) collective-permute-start(bf16[320,1024]{1,0:T(8,128)(2,1)} %get-tuple-element.78), channel_id=1, source_target_pairs={{0,2},{1,3},{2,0},{3,1},{4,6},{5,7},{6,4},{7,5},{8,10},{9,11},{10,... | collective-permute-start | bytes 1966088 | tf_op jit(solution)/shard_map/ppermute | solution.py:541
  107.2 5.7 %all-to-all-start.3 = ((bf16[64,40,128]{2,1,0:T(8,128)(2,1)}), bf16[64,40,128]{2,1,0:T(8,128)(2,1)}, u32[]{:S(2)}, u32[]{:S(2)}) async-start(bf16[64,40,128]{2,1,0:T(8,128)(2,1)} %bitcast.39), calls=%async_computation.3 | async-start | bytes 1310720 | tf_op jit(solution)/shard_map/all_to_all | solution.py:427
  112.9 1.9 %copy-done.3 = bf16[1,4096,384]{2,1,0:T(8,128)(2,1)S(1)} copy-done((bf16[1,4096,384]{2,1,0:T(8,128)(2,1)S(1)}, bf16[1,4096,384]{2,1,0:T(8,128)(2,1)}, u32[]{:S(2)}) %copy-start.3) | copy-done | bytes 3145752
  114.8 0.9 copy-done.10
  115.8 1.7 %shard_map.113 = (bf16[320,1024]{1,0:T(8,128)(2,1)}, bf16[320,1024]{1,0:T(8,128)(2,1)S(1)}) custom-call(s32[1]{0:T(128)} %bitcast.1.place_ref, bf16[320,384]{1,0:T(8,128)(2,1)S(1)} %copy-done.8, bf16[320,384]{1,0:T(8,128)(2,1)S(1)} %copy-done.10, bf16[4,1024,384]{2,1,0:T(8,128)(2,1)S(1)} %bitcast.23, bf16[4,1024,384]{2,1,0:T(8,128)(2,1)S(1)} %bitcast.30, ...), custom_call_target="tpu_custom_call" | custom-call | flops 1006632960 | bytes 1966080 | tf_op jit(solution)/shard_map/pallas_call | solution.py:379
  117.5 11.4 %collective-permute-done.17.after.far_ref = bf16[320,1024]{1,0:T(8,128)(2,1)} collective-permute-done((bf16[320,1024]{1,0:T(8,128)(2,1)}, bf16[320,1024]{1,0:T(8,128)(2,1)}, u32[]{:S(2)}, u32[]{:S(2)}) %collective-permute-start.17) | collective-permute-done | bytes 655392 | tf_op jit(solution)/shard_map/ppermute | solution.py:541
  128.9 3.1 %shard_map.115 = (bf16[2560,128]{1,0:T(8,128)(2,1)}, f32[8,128]{1,0:T(8,128)}) custom-call(bf16[320,1024]{1,0:T(8,128)(2,1)S(1)} %get-tuple-element.76.keep_ref, bf16[320,1024]{1,0:T(8,128)(2,1)} %collective-permute-done.16.near_ref, bf16[320,1024]{1,0:T(8,128)(2,1)} %collective-permute-done.17.after.far_ref, f32[8,128]{1,0:T(8,128)S(1)} %shard_map.114.after), custom_call_target="tpu_custom_call" | custom-call | flops 1000000 | bytes 1966080 | tf_op jit(solution)/shard_map/pallas_call | solution.py:379
  132.1 1.5 all-to-all-done.3
  133.6 5.8 %all-to-all-start.4 = ((bf16[64,40,128]{2,1,0:T(8,128)(2,1)}), bf16[64,40,128]{2,1,0:T(8,128)(2,1)S(1)}, u32[]{:S(2)}, u32[]{:S(2)}) async-start(bf16[64,40,128]{2,1,0:T(8,128)(2,1)} %bitcast.15), calls=%async_computation.4 | async-start | bytes 1310720 | tf_op jit(solution)/shard_map/all_to_all | solution.py:427
  139.4 0.1 copy.11.gates_ref
  139.5 2.7 %shard_map.112 = (bf16[128,1024]{1,0:T(8,128)(2,1)}, f32[128,2]{1,0:T(8,128)S(1)}) custom-call(s32[2,128]{1,0:T(2,128)S(1)} %bitcast.42, f32[128,2]{1,0:T(8,128)S(1)} %copy.11.gates_ref, bf16[128,1024]{1,0:T(8,128)(2,1)S(1)} %copy-done.19, bf16[2560,128]{1,0:T(8,128)(2,1)} %bitcast.14.rows_ref), custom_call_target="tpu_custom_call" | custom-call | flops 100000000 | bytes 1966080 | tf_op jit(solution)/shard_map/pallas_call | solution.py:379
  142.2 1.3 collective-permute-done.18
  143.5 0.7 collective-permute-start.19
  144.2 5.8 %collective-permute-done.19 = f32[128,2]{1,0:T(8,128)S(1)} collective-permute-done((f32[128,2]{1,0:T(8,128)S(1)}, f32[128,2]{1,0:T(8,128)S(1)}, u32[]{:S(2)}, u32[]{:S(2)}) %collective-permute-start.19) | collective-permute-done | bytes 1056 | tf_op jit(solution)/shard_map/ppermute | solution.py:560
  149.9 0.6 copy.12
  150.6 8.9 %all-to-all-done.4 = bf16[64,40,128]{2,1,0:T(8,128)(2,1)S(1)} async-done(((bf16[64,40,128]{2,1,0:T(8,128)(2,1)}), bf16[64,40,128]{2,1,0:T(8,128)(2,1)S(1)}, u32[]{:S(2)}, u32[]{:S(2)}) %all-to-all-start.4) | async-done | bytes 655392 | tf_op jit(solution)/shard_map/all_to_all | solution.py:427
  159.4 1.4 shard_map.116
  (62 shorter events, 0.3 us)
Async XLA Ops:
  0.6 57.6 %copy-start = (bf16[1,4096,384]{2,1,0:T(8,128)(2,1)S(1)}, bf16[1,4096,384]{2,1,0:T(8,128)(2,1)}, u32[]{:S(2)}) copy-start(bf16[1,4096,384]{2,1,0:T(8,128)(2,1)} %param.11) | copy-start | bytes 9437188
  0.6 12.6 %all-to-all-start = ((bf16[8,128,128]{2,1,0:T(8,128)(2,1)}), bf16[8,128,128]{2,1,0:T(8,128)(2,1)S(1)}, u32[]{:S(2)}, u32[]{:S(2)}) async-start(bf16[8,128,128]{2,1,0:T(8,128)(2,1)} %bitcast.45), calls=%async_computation | async-start | bytes 524288 | tf_op jit(solution)/shard_map/all_to_all | solution.py:446
  6.0 0.9 copy-start.18
  7.0 0.7 copy-start.20
  7.6 0.7 copy-start.23
  9.0 1.1 copy-start.6
  13.2 0.7 copy-start.21
  44.7 19.4 %collective-permute-start = (bf16[2560,128]{1,0:T(8,128)(2,1)}, bf16[2560,128]{1,0:T(8,128)(2,1)}, u32[]{:S(2)}, u32[]{:S(2)}) collective-permute-start(bf16[2560,128]{1,0:T(8,128)(2,1)} %bitcast.5.x_ref.x0), channel_id=1, source_target_pairs={{0,2},{1,3},{2,0},{3,1},{4,6},{5,7},{6,4},{7,5},{8,10},{9,11},{10,... | collective-permute-start | bytes 1966088 | tf_op jit(solution)/shard_map/ppermute | solution.py:459
  45.5 42.5 %all-to-all-start.2 = ((bf16[128,40,128]{2,1,0:T(8,128)(2,1)}), bf16[128,40,128]{2,1,0:T(8,128)(2,1)}, u32[]{:S(2)}, u32[]{:S(2)}) async-start(bf16[128,40,128]{2,1,0:T(8,128)(2,1)} %bitcast.38), calls=%async_computation.2 | async-start | bytes 2621440 | tf_op jit(solution)/shard_map/all_to_all | solution.py:466
  57.2 5.0 %collective-permute-start.1 = (bf16[640,128]{1,0:T(8,128)(2,1)}, bf16[640,128]{1,0:T(8,128)(2,1)S(1)}, u32[]{:S(2)}, u32[]{:S(2)}) collective-permute-start(bf16[640,128]{1,0:T(8,128)(2,1)} %get-tuple-element.43), channel_id=1, source_target_pairs={{0,1},{1,0},{2,3},{3,2},{4,5},{5,4},{6,7},{7,6},{8,9},{9,8},{10,11... | collective-permute-start | bytes 491528 | tf_op jit(solution)/shard_map/ppermute | solution.py:477
  57.2 5.0 %collective-permute-start.2 = (bf16[640,128]{1,0:T(8,128)(2,1)}, bf16[640,128]{1,0:T(8,128)(2,1)S(1)}, u32[]{:S(2)}, u32[]{:S(2)}) collective-permute-start(bf16[640,128]{1,0:T(8,128)(2,1)} %get-tuple-element.44), channel_id=1, source_target_pairs={{0,1},{1,0},{2,3},{3,2},{4,5},{5,4},{6,7},{7,6},{8,9},{9,8},{10,11... | collective-permute-start | bytes 491528 | tf_op jit(solution)/shard_map/ppermute | solution.py:477
  57.7 4.5 %collective-permute-start.3 = (bf16[640,128]{1,0:T(8,128)(2,1)}, bf16[640,128]{1,0:T(8,128)(2,1)}, u32[]{:S(2)}, u32[]{:S(2)}) collective-permute-start(bf16[640,128]{1,0:T(8,128)(2,1)} %get-tuple-element.45), channel_id=1, source_target_pairs={{0,1},{1,0},{2,3},{3,2},{4,5},{5,4},{6,7},{7,6},{8,9},{9,8},{10,11... | collective-permute-start | bytes 491528 | tf_op jit(solution)/shard_map/ppermute | solution.py:477
  57.7 4.5 %collective-permute-start.4 = (bf16[640,128]{1,0:T(8,128)(2,1)}, bf16[640,128]{1,0:T(8,128)(2,1)}, u32[]{:S(2)}, u32[]{:S(2)}) collective-permute-start(bf16[640,128]{1,0:T(8,128)(2,1)} %get-tuple-element.46), channel_id=1, source_target_pairs={{0,1},{1,0},{2,3},{3,2},{4,5},{5,4},{6,7},{7,6},{8,9},{9,8},{10,11... | collective-permute-start | bytes 491528 | tf_op jit(solution)/shard_map/ppermute | solution.py:477
  58.2 1.9 %copy-start.1 = (bf16[1,4096,384]{2,1,0:T(8,128)(2,1)S(1)}, bf16[1,4096,384]{2,1,0:T(8,128)(2,1)}, u32[]{:S(2)}) copy-start(bf16[1,4096,384]{2,1,0:T(8,128)(2,1)} %param.12) | copy-start | bytes 9437188
  64.1 2.4 %collective-permute-start.5 = (bf16[2560,128]{1,0:T(8,128)(2,1)}, bf16[2560,128]{1,0:T(8,128)(2,1)S(1)}, u32[]{:S(2)}, u32[]{:S(2)}) collective-permute-start(bf16[2560,128]{1,0:T(8,128)(2,1)} %shard_map.99.x2), channel_id=1, source_target_pairs={{0,1},{1,0},{2,3},{3,2},{4,5},{5,4},{6,7},{7,6},{8,9},{9,8},{10,11... | collective-permute-start | bytes 1966088 | tf_op jit(solution)/shard_map/ppermute | solution.py:483
  64.2 2.3 %copy-start.4 = (bf16[1,384,4096]{2,1,0:T(8,128)(2,1)S(1)}, bf16[1,384,4096]{2,1,0:T(8,128)(2,1)}, u32[]{:S(2)}) copy-start(bf16[1,384,4096]{2,1,0:T(8,128)(2,1)} %param.13) | copy-start | bytes 9437188
  68.0 4.1 %copy-start.14 = (f32[320,384]{1,0:T(8,128)}, f32[320,384]{1,0:T(8,128)S(1)}, u32[]{:S(2)}) copy-start(f32[320,384]{1,0:T(8,128)S(1)} %get-tuple-element.65.silu_ref) | copy-start | bytes 1474564
  68.0 4.1 %copy-start.16 = (f32[320,384]{1,0:T(8,128)}, f32[320,384]{1,0:T(8,128)S(1)}, u32[]{:S(2)}) copy-start(f32[320,384]{1,0:T(8,128)S(1)} %get-tuple-element.66.dsilu_ref) | copy-start | bytes 1474564
  68.1 2.4 %collective-permute-start.6 = (bf16[320,1024]{1,0:T(8,128)(2,1)S(1)}, bf16[320,1024]{1,0:T(8,128)(2,1)S(1)}, u32[]{:S(2)}, u32[]{:S(2)}) collective-permute-start(bf16[320,1024]{1,0:T(8,128)(2,1)S(1)} %get-tuple-element.55), channel_id=1, source_target_pairs={{0,1},{1,0},{2,3},{3,2},{4,5},{5,4},{6,7},{7,6},{8,9},{9,8},{10,11... | collective-permute-start | bytes 1966088 | tf_op jit(solution)/shard_map/ppermute | solution.py:493
  71.5 27.5 %collective-permute-start.7 = (bf16[320,1024]{1,0:T(8,128)(2,1)}, bf16[320,1024]{1,0:T(8,128)(2,1)}, u32[]{:S(2)}, u32[]{:S(2)}) collective-permute-start(bf16[320,1024]{1,0:T(8,128)(2,1)} %get-tuple-element.58), channel_id=1, source_target_pairs={{0,2},{1,3},{2,0},{3,1},{4,6},{5,7},{6,4},{7,5},{8,10},{9,11},{10,... | collective-permute-start | bytes 1966088 | tf_op jit(solution)/shard_map/ppermute | solution.py:502
  73.6 0.8 copy-start.12
  89.3 4.5 %collective-permute-start.10 = (bf16[1280,128]{1,0:T(8,128)(2,1)S(1)}, bf16[1280,128]{1,0:T(8,128)(2,1)S(1)}, u32[]{:S(2)}, u32[]{:S(2)}) collective-permute-start(bf16[1280,128]{1,0:T(8,128)(2,1)S(1)} %get-tuple-element.63.refs_2_), channel_id=1, source_target_pairs={{0,1},{1,0},{2,3},{3,2},{4,5},{5,4},{6,7},{7,6},{8,9},{9,8},{10,11... | collective-permute-start | bytes 983048 | tf_op jit(solution)/shard_map/ppermute | solution.py:513
  89.4 4.6 %collective-permute-start.11 = (bf16[1280,128]{1,0:T(8,128)(2,1)S(1)}, bf16[1280,128]{1,0:T(8,128)(2,1)S(1)}, u32[]{:S(2)}, u32[]{:S(2)}) collective-permute-start(bf16[1280,128]{1,0:T(8,128)(2,1)S(1)} %get-tuple-element.64.refs_3_), channel_id=1, source_target_pairs={{0,1},{1,0},{2,3},{3,2},{4,5},{5,4},{6,7},{7,6},{8,9},{9,8},{10,11... | collective-permute-start | bytes 983048 | tf_op jit(solution)/shard_map/ppermute | solution.py:513
  89.9 4.5 %collective-permute-start.8 = (bf16[1280,128]{1,0:T(8,128)(2,1)S(1)}, bf16[1280,128]{1,0:T(8,128)(2,1)S(1)}, u32[]{:S(2)}, u32[]{:S(2)}) collective-permute-start(bf16[1280,128]{1,0:T(8,128)(2,1)S(1)} %get-tuple-element.61.refs_0_), channel_id=1, source_target_pairs={{0,1},{1,0},{2,3},{3,2},{4,5},{5,4},{6,7},{7,6},{8,9},{9,8},{10,11... | collective-permute-start | bytes 983048 | tf_op jit(solution)/shard_map/ppermute | solution.py:513
  90.0 4.4 %collective-permute-start.9 = (bf16[1280,128]{1,0:T(8,128)(2,1)S(1)}, bf16[1280,128]{1,0:T(8,128)(2,1)S(1)}, u32[]{:S(2)}, u32[]{:S(2)}) collective-permute-start(bf16[1280,128]{1,0:T(8,128)(2,1)S(1)} %get-tuple-element.62.refs_1_), channel_id=1, source_target_pairs={{0,1},{1,0},{2,3},{3,2},{4,5},{5,4},{6,7},{7,6},{8,9},{9,8},{10,11... | collective-permute-start | bytes 983048 | tf_op jit(solution)/shard_map/ppermute | solution.py:513
  90.4 1.9 %copy-start.5 = (bf16[1,384,4096]{2,1,0:T(8,128)(2,1)S(1)}, bf16[1,384,4096]{2,1,0:T(8,128)(2,1)}, u32[]{:S(2)}) copy-start(bf16[1,384,4096]{2,1,0:T(8,128)(2,1)} %param.13) | copy-start | bytes 9437188
  93.8 2.1 %copy-start.2 = (bf16[1,4096,384]{2,1,0:T(8,128)(2,1)S(1)}, bf16[1,4096,384]{2,1,0:T(8,128)(2,1)}, u32[]{:S(2)}) copy-start(bf16[1,4096,384]{2,1,0:T(8,128)(2,1)} %param.12) | copy-start | bytes 9437188
  93.8 2.1 %copy-start.15 = (f32[320,384]{1,0:T(8,128)S(1)}, f32[320,384]{1,0:T(8,128)}, u32[]{:S(2)}) copy-start(f32[320,384]{1,0:T(8,128)} %copy-done.14) | copy-start | bytes 1474564
  93.8 2.1 %copy-start.17 = (f32[320,384]{1,0:T(8,128)S(1)}, f32[320,384]{1,0:T(8,128)}, u32[]{:S(2)}) copy-start(f32[320,384]{1,0:T(8,128)} %copy-done.16) | copy-start | bytes 1474564
  93.8 5.2 %collective-permute-start.12 = (bf16[320,512]{1,0:T(8,128)(2,1)}, bf16[320,512]{1,0:T(8,128)(2,1)}, u32[]{:S(2)}, u32[]{:S(2)}) collective-permute-start(bf16[320,512]{1,0:T(8,128)(2,1)} %get-tuple-element.69), channel_id=1, source_target_pairs={{0,1},{1,0},{2,3},{3,2},{4,5},{5,4},{6,7},{7,6},{8,9},{9,8},{10,11... | collective-permute-start | bytes 983048 | tf_op jit(solution)/shard_map/ppermute | solution.py:532
  94.0 5.0 %collective-permute-start.13 = (bf16[320,512]{1,0:T(8,128)(2,1)}, bf16[320,512]{1,0:T(8,128)(2,1)}, u32[]{:S(2)}, u32[]{:S(2)}) collective-permute-start(bf16[320,512]{1,0:T(8,128)(2,1)} %get-tuple-element.70), channel_id=1, source_target_pairs={{0,1},{1,0},{2,3},{3,2},{4,5},{5,4},{6,7},{7,6},{8,9},{9,8},{10,11... | collective-permute-start | bytes 983048 | tf_op jit(solution)/shard_map/ppermute | solution.py:532
  97.6 1.4 copy-start.7
  97.6 1.4 copy-start.9
  97.6 2.0 %collective-permute-start.14 = (bf16[320,512]{1,0:T(8,128)(2,1)}, bf16[320,512]{1,0:T(8,128)(2,1)}, u32[]{:S(2)}, u32[]{:S(2)}) collective-permute-start(bf16[320,512]{1,0:T(8,128)(2,1)} %get-tuple-element.71), channel_id=1, source_target_pairs={{0,1},{1,0},{2,3},{3,2},{4,5},{5,4},{6,7},{7,6},{8,9},{9,8},{10,11... | collective-permute-start | bytes 983048 | tf_op jit(solution)/shard_map/ppermute | solution.py:531
  97.7 2.3 %collective-permute-start.15 = (bf16[320,512]{1,0:T(8,128)(2,1)}, bf16[320,512]{1,0:T(8,128)(2,1)}, u32[]{:S(2)}, u32[]{:S(2)}) collective-permute-start(bf16[320,512]{1,0:T(8,128)(2,1)} %get-tuple-element.72), channel_id=1, source_target_pairs={{0,1},{1,0},{2,3},{3,2},{4,5},{5,4},{6,7},{7,6},{8,9},{9,8},{10,11... | collective-permute-start | bytes 983048 | tf_op jit(solution)/shard_map/ppermute | solution.py:531
  99.0 1.1 copy-start.13
  99.0 13.9 %copy-start.8 = (bf16[320,384]{1,0:T(8,128)(2,1)S(1)}, bf16[320,384]{1,0:T(8,128)(2,1)}, u32[]{:S(2)}) copy-start(bf16[320,384]{1,0:T(8,128)(2,1)} %copy-done.7) | copy-start | bytes 737284
  102.9 0.9 copy-start.11
  103.8 25.1 %collective-permute-start.17 = (bf16[320,1024]{1,0:T(8,128)(2,1)}, bf16[320,1024]{1,0:T(8,128)(2,1)}, u32[]{:S(2)}, u32[]{:S(2)}) collective-permute-start(bf16[320,1024]{1,0:T(8,128)(2,1)} %get-tuple-element.78), channel_id=1, source_target_pairs={{0,2},{1,3},{2,0},{3,1},{4,6},{5,7},{6,4},{7,5},{8,10},{9,11},{10,... | collective-permute-start | bytes 1966088 | tf_op jit(solution)/shard_map/ppermute | solution.py:541
  107.2 26.4 %all-to-all-start.3 = ((bf16[64,40,128]{2,1,0:T(8,128)(2,1)}), bf16[64,40,128]{2,1,0:T(8,128)(2,1)}, u32[]{:S(2)}, u32[]{:S(2)}) async-start(bf16[64,40,128]{2,1,0:T(8,128)(2,1)} %bitcast.39), calls=%async_computation.3 | async-start | bytes 1310720 | tf_op jit(solution)/shard_map/all_to_all | solution.py:427
  112.9 1.9 %copy-start.3 = (bf16[1,4096,384]{2,1,0:T(8,128)(2,1)S(1)}, bf16[1,4096,384]{2,1,0:T(8,128)(2,1)}, u32[]{:S(2)}) copy-start(bf16[1,4096,384]{2,1,0:T(8,128)(2,1)} %param.12) | copy-start | bytes 9437188
  114.8 0.9 copy-start.10
  117.5 11.5 %collective-permute-start.16 = (bf16[320,1024]{1,0:T(8,128)(2,1)}, bf16[320,1024]{1,0:T(8,128)(2,1)}, u32[]{:S(2)}, u32[]{:S(2)}) collective-permute-start(bf16[320,1024]{1,0:T(8,128)(2,1)} %get-tuple-element.77), channel_id=1, source_target_pairs={{0,1},{1,0},{2,3},{3,2},{4,5},{5,4},{6,7},{7,6},{8,9},{9,8},{10,11... | collective-permute-start | bytes 1966088 | tf_op jit(solution)/shard_map/ppermute | solution.py:546
  128.9 10.5 %copy-start.24 = (f32[128,2]{0,1:T(2,128)S(1)}, f32[128,2]{0,1:T(2,128)}, u32[]{:S(2)}) copy-start(f32[128,2]{0,1:T(2,128)} %param.10) | copy-start | bytes 3076
  128.9 10.6 %copy-start.19 = (bf16[128,1024]{1,0:T(8,128)(2,1)S(1)}, bf16[128,1024]{1,0:T(8,128)(2,1)}, u32[]{:S(2)}) copy-start(bf16[128,1024]{1,0:T(8,128)(2,1)} %cot_ref.3) | copy-start | bytes 786436
  128.9 10.6 %copy-start.22 = (s32[128,2]{0,1:T(2,128)S(1)}, s32[128,2]{0,1:T(2,128)}, u32[]{:S(2)}) copy-start(s32[128,2]{0,1:T(2,128)} %param.9) | copy-start | bytes 3076
  133.6 25.9 %all-to-all-start.4 = ((bf16[64,40,128]{2,1,0:T(8,128)(2,1)}), bf16[64,40,128]{2,1,0:T(8,128)(2,1)S(1)}, u32[]{:S(2)}, u32[]{:S(2)}) async-start(bf16[64,40,128]{2,1,0:T(8,128)(2,1)} %bitcast.15), calls=%async_computation.4 | async-start | bytes 1310720 | tf_op jit(solution)/shard_map/all_to_all | solution.py:427
  142.2 1.3 collective-permute-start.18
  143.5 6.4 %collective-permute-start.19 = (f32[128,2]{1,0:T(8,128)S(1)}, f32[128,2]{1,0:T(8,128)S(1)}, u32[]{:S(2)}, u32[]{:S(2)}) collective-permute-start(f32[128,2]{1,0:T(8,128)S(1)} %add.6), channel_id=1, source_target_pairs={{0,2},{1,3},{2,0},{3,1},{4,6},{5,7},{6,4},{7,5},{8,10},{9,11},{10,... | collective-permute-start | bytes 3080 | tf_op jit(solution)/shard_map/ppermute | solution.py:560
